TPU v7x, 32 devices: a whole 2x2x4 slice. The times are simulated.
32 devices in a mesh: row: 4 (over y, x), col: 8 (over z, core).
Axes of the slice: x: 2, y: 2, z: 4, core: 2. Of those that a mesh axis runs over, the one named last changes fastest.
Arguments:
- trail_adjoint: float32 [32, 512, 16, 1024], P(None, 'row', None, 'col'), may hold values from -6 to 6
- panel: float32 [32, 512, 128], P(None, 'row'), may hold values from -0.046875 to 0.046875
- panel_adjoint: float32 [32, 512, 128], P(None, 'row'), may hold values from -6 to 6
- diag_block: float32 [128, 128], replicated, as said below
Outputs:
- input_adjoint: float32 [32, 512, 128], P(None, 'row')
- block_adjoint: float32 [128, 128], replicated
Inputs may be any that keep to these rules, and one draw needn't show every extreme that they name: diag_block is lower triangular with diagonal entries between 1.5 and 3 and zeros above the diagonal.
All inputs are finite; a program needn't handle non-finite values.
Results may differ from a plain program's by a relative error of at most 0.000082.
Values sent between devices are 32-bit elements; how exact they have to be, the bound alone decides.
No kernel may reach another device: no remote copies, remote signals or barrier semaphores. Data moves between devices by JAX's collectives and lax.ppermute only.
A program may use at most 128 MiB of HBM per device.

v0:
```python
import jax
import jax.numpy as jnp
from jax import lax
from jax.sharding import PartitionSpec as P


def spread(value, axis, root):
    mine = lax.axis_index(axis) == root
    return lax.psum(jnp.where(mine, value, jnp.zeros_like(value)), axis)


def solve_rows(total, diag_block):
    return lax.linalg.triangular_solve(diag_block, total, left_side=False, lower=True)


def per_device(trail_adjoint, panel, panel_adjoint, diag_block):
    width = diag_block.shape[0]
    n_row = lax.axis_size("row")
    n_col = lax.axis_size("col")
    ratio = n_col // n_row
    row_blocks = panel.shape[0]
    col_blocks = trail_adjoint.shape[2]
    col_index = lax.axis_index("col")
    row_index = lax.axis_index("row")
    grouped = panel.reshape(col_blocks, ratio, width, width)
    chosen = lax.dynamic_index_in_dim(grouped, col_index // n_row, 1, keepdims=False)
    col_panel = spread(chosen, "row", col_index % n_row)
    flip_part = jnp.einsum(
        "aibj,aik->bjk",
        trail_adjoint,
        panel,
        precision=lax.Precision.HIGHEST,
        preferred_element_type=jnp.float32,
    )
    flip_total = lax.psum(flip_part, "row")
    flat_panel = panel.reshape(row_blocks * width, width)
    flat_given = panel_adjoint.reshape(row_blocks * width, width)
    owner = col_index % n_row == row_index
    selector = jnp.logical_and(jnp.arange(ratio) == col_index // n_row, owner).astype(jnp.float32)
    placed = (flip_total[:, None, :, :] * selector[None, :, None, None]).reshape(
        row_blocks * width, width
    )
    direct_part = jnp.einsum(
        "aibj,bjk->aik",
        trail_adjoint,
        col_panel,
        precision=lax.Precision.HIGHEST,
        preferred_element_type=jnp.float32,
    )
    direct_part = direct_part + placed.reshape(row_blocks, width, width)
    direct = lax.psum(direct_part, "col").reshape(row_blocks * width, width)
    total = flat_given - direct
    solved = solve_rows(total, diag_block)
    gram_part = -jnp.dot(
        solved.T, flat_panel, precision=lax.Precision.HIGHEST, preferred_element_type=jnp.float32
    )
    gram = lax.psum(gram_part, "row")
    return (solved.reshape(row_blocks, width, width), jnp.tril(gram))


def solution(mesh):
    in_specs = (P(None, "row", None, "col"), P(None, "row", None), P(None, "row", None), P())
    out_specs = (P(None, "row", None), P())
    return jax.shard_map(
        per_device, mesh=mesh, in_specs=in_specs, out_specs=out_specs, check_vma=False
    )
```

profile of v0, /device:TPU:0, one launch (start us, length us, event | category | flops | bytes accessed | tf_op | source)
XLA Modules:
  0.0 329.0 jit_solution(17504232344798805224)
XLA Ops:
  7.2 0.0 copy-start
  7.2 0.0 all-reduce.9.cloned.1.call-start
  7.2 1.5 copy-done
  8.8 1.1 constant_dynamic-slice_fusion
  9.8 1.6 copy.18
  11.4 61.2 %fusion.7 = f32[16,128,128]{2,1,0:T(8,128)} fusion(f32[32,128,128]{2,1,0:T(8,128)S(1)} %copy-done, f32[32,128,16,128]{3,2,1,0:T(8,128)} %param.4), kind=kOutput, calls=%fused_computation.7 | convolution fusion | flops 12884901888 | bytes 36700160 | tf_op jit(solution)/shard_map/aibj,aik->bjk/dot_general | solution.py:28
  72.6 1.1 select_bitcast_fusion
  73.6 0.0 all-reduce.9.cloned.1.call-update
  73.7 0.0 all-reduce.5.cloned.1.call-start
  73.7 0.1 mul.23
  73.8 72.5 %all-reduce.9.cloned.1.call-done = (f32[16,128,128]{1,2,0:T(8,128)}, f32[16,128,128]{2,1,0:T(8,128)}) async-done(((f32[16,128,128]{1,2,0:T(8,128)}, f32[16,128,128]{2,1,0:T(8,128)}), (f32[16,128,128]{1,2,0:T(8,128)}, f32[16,128,128]{2,1,0:T(8,128)})) %all-reduce.9.cloned.1.call-update) | async-done | bytes 2097168 | tf_op jit(solution)/shard_map/psum | solution.py:9
  146.4 1.6 copy.13
  147.9 50.7 %bitcast_add_fusion = f32[32,128,128]{1,2,0:T(8,128)} fusion(f32[32,128,16,128]{3,2,1,0:T(8,128)} %param.4, f32[16,128,128]{1,2,0:T(8,128)} %get-tuple-element.2, f32[32]{0:T(128)S(1)} %mul.23, f32[16,128,128]{1,2,0:T(8,128)S(1)} %copy.13), kind=kOutput, calls=%fused_computation.4 | convolution fusion | flops 12885950464 | bytes 37748864 | tf_op jit(solution)/shard_map/aibj,bjk->aik/dot_general | solution.py:43
  198.6 0.0 all-reduce.5.cloned.1.call-update
  198.6 0.0 copy-start.2
  198.6 0.0 all-reduce.7.cloned.1.call-start
  198.7 3.1 copy.14
  201.8 0.0 copy-done.2
  201.8 9.8 %custom-call.3 = f32[1,128,128]{1,2,0:T(8,128)S(1)} custom-call(f32[1,128,128]{2,1,0:T(8,128)S(1)} %select_bitcast_fusion.1), custom_call_target="InvertDiagBlocksLowerTriangular" | custom-call | tf_op jit(solution)/shard_map/triangular_solve | solution.py:13
  211.6 52.2 %all-reduce.5.cloned.1.call-done = f32[32,128,128]{1,2,0:T(8,128)} async-done(((f32[32,128,128]{1,2,0:T(8,128)}), f32[32,128,128]{1,2,0:T(8,128)}) %all-reduce.5.cloned.1.call-update) | async-done | bytes 2097168 | tf_op jit(solution)/shard_map/psum | solution.py:51
  263.8 3.9 %sub.12 = f32[32,128,128]{1,2,0:T(8,128)} subtract(f32[32,128,128]{1,2,0:T(8,128)} %copy.14, f32[32,128,128]{1,2,0:T(8,128)} %all-reduce.5.cloned.1.call-done) | non-fusion elementwise | flops 524288 | bytes 6291456 | tf_op jit(solution)/shard_map/sub | solution.py:52
  267.7 2.9 copy.15
  270.6 3.5 %fusion.13 = f32[4096,128]{1,0:T(8,128)S(1)} fusion(f32[4096,128]{1,0:T(8,128)} %bitcast.37, f32[1,128,128]{1,2,0:T(8,128)S(1)} %custom-call.3), kind=kOutput, calls=%fused_computation.11 | convolution fusion | flops 805306368 | bytes 4259840 | tf_op jit(solution)/shard_map/triangular_solve | solution.py:13
  274.1 0.0 copy-start.1
  274.1 1.3 copy-done.1
  275.4 4.2 %convolution_negate_fusion = f32[128,128]{1,0:T(8,128)} fusion(f32[4096,128]{1,0:T(8,128)S(1)} %fusion.13, f32[4096,128]{1,0:T(8,128)S(1)} %bitcast.35), kind=kOutput, calls=%fused_computation.8 | convolution fusion | flops 805322752 | bytes 4259840 | tf_op jit(solution)/shard_map/dot_general | solution.py:54
  279.7 0.0 all-reduce.7.cloned.1.call-update
  279.7 41.3 %all-reduce.7.cloned.1.call-done = f32[128,128]{1,0:T(8,128)} async-done(((f32[128,128]{1,0:T(8,128)}), f32[128,128]{1,0:T(8,128)}) %all-reduce.7.cloned.1.call-update) | async-done | bytes 65552 | tf_op jit(solution)/shard_map/psum | solution.py:57
  321.0 1.5 fusion.15
  (3 shorter events, 0.0 us)
Async XLA Ops:
  7.2 1.6 copy-start
  7.2 139.2 %all-reduce.9.cloned.1.call-start = ((), (), s32[]{:S(2)}) async-start(), calls=%async_computation.2 | async-start | bytes 4194304 | tf_op jit(solution)/shard_map/psum | solution.py:9
  73.7 190.2 %all-reduce.5.cloned.1.call-start = ((), (), s32[]{:S(2)}) async-start(), calls=%async_computation | async-start | bytes 4194304 | tf_op jit(solution)/shard_map/psum | solution.py:51
  198.6 3.2 copy-start.2
  198.6 122.4 %all-reduce.7.cloned.1.call-start = ((), (), s32[]{:S(2)}) async-start(), calls=%async_computation.1 | async-start | bytes 131072 | tf_op jit(solution)/shard_map/psum | solution.py:57
  274.1 1.3 copy-start.1
Sparse Core Ops, SparseCore 0:
  73.8 72.5 all-reduce.8
  198.7 65.0 all-reduce.4
  279.8 41.1 all-reduce.6
where the time goes:
time: 329 us
  waiting for transfers between devices  166 us (50%)
  matrix products  120 us (36%)
  other arithmetic  16.2 us (5%)
  between operations  13.9 us (4%)
  local copies, waits for them, and re-layouts  13.1 us (4%)
    psum x1, waiting for transfers between devices, spread(): return lax.psum(jnp.where(mine, value, jnp.zeros_like(value)), axis)  72.5 us
    dot_general x1, matrix products, per_device(): jnp.einsum('aibj,aik->bjk', trail_adjoint, panel, precision=lax.Precision...  61.2 us
    psum x1, waiting for transfers between devices, per_device(): direct = lax.psum(direct_part, 'col').reshape(row_blocks * width, width)  52.2 us
    dot_general x1, matrix products, per_device(): jnp.einsum('aibj,bjk->aik', trail_adjoint, col_panel, precision=lax.Preci...  50.7 us
    psum x1, waiting for transfers between devices, per_device(): gram = lax.psum(gram_part, 'row')  41.3 us
    another operation x2, other arithmetic, solve_rows(): lax.linalg.triangular_solve(diag_block, total, left_side=False, lower=True)  9.82 us
    unnamed x8, local copies, waits for them, and re-layouts  7.5 us
  transfers between devices with their start and end apart: 3, of which 3 were waited for; matrix products, arithmetic and copies ran while one was open for 4% of the time, Pallas kernels for 0%

commit v1 on v0

v1 whole, which is shorter than its diff:
```python
import functools
import math

import jax
import jax.numpy as jnp
from jax import lax
from jax.experimental import pallas as pl
from jax.experimental.pallas import tpu as pltpu
from jax.sharding import PartitionSpec as P

F32 = jnp.float32
BF16 = jnp.bfloat16
HIGHEST = lax.Precision.HIGHEST
AXES = ("row", "col")
KEEP_BYTES = 24 * 2**20
FLIP_VMEM = 20 * 2**20
DIRECT_VMEM = 12 * 2**20
CHUNK_VMEM = 24 * 2**20
SMALL_VMEM = 8 * 2**20


def split(x):
    high = x.astype(BF16)
    return high, (x - high.astype(F32)).astype(BF16)


def dot(a, b):
    return jnp.dot(a, b, preferred_element_type=F32)


def full_dot(a, b):
    return jnp.dot(a, b, preferred_element_type=F32, precision=HIGHEST)


def send(x, target, n_row, n_col):
    pairs = []
    for r in range(n_row):
        for c in range(n_col):
            to_r, to_c = target(r, c)
            pairs.append((r * n_col + c, to_r * n_col + to_c))
    return lax.ppermute(x, AXES, pairs)


def choose(grouped, which):
    blocks, _, width, _ = grouped.shape

    def body(which_ref, source, target):
        target[...] = source[...]

    return pl.pallas_call(
        body,
        grid_spec=pltpu.PrefetchScalarGridSpec(
            num_scalar_prefetch=1,
            grid=(1,),
            in_specs=[pl.BlockSpec((blocks, None, width, width), lambda i, which: (0, which[0], 0, 0))],
            out_specs=pl.BlockSpec((blocks, width, width), lambda i, which: (0, 0, 0)),
        ),
        out_shape=jax.ShapeDtypeStruct((blocks, width, width), F32),
        compiler_params=pltpu.CompilerParams(vmem_limit_bytes=SMALL_VMEM),
        name="choose",
    )(which, grouped)


def flip_body(plan, n_parts, me_ref, ids_ref, s_ref, l_ref, d_ref, *refs):
    outs, (inv_ref, high_ref, low_ref, acc, turned, buf, sems) = refs[:n_parts], refs[n_parts:]
    step, n_steps, slot = pl.program_id(0), plan.n_chunks, pl.program_id(0) % 2
    n_blocks, rows, width = plan.n_blocks, plan.chunk_rows, plan.width

    def fetch(i, slot):
        qb, h, qs = plan.chunk_at(ids_ref[plan.flip_place(i)])
        target = buf.at[slot]
        if plan.pitch > n_blocks:
            target = target.at[:, :, pl.ds(0, n_blocks), :]
        return pltpu.make_async_copy(s_ref.at[qb, :, h, qs], target, sems.at[slot])

    @pl.when(step == 0)
    def _():
        fetch(0, 0).start()
        acc[...] = jnp.zeros_like(acc)
        inv_ref[...] = inverse_start(d_ref[...])

    @pl.when(step + 1 < n_steps)
    def _():
        fetch(step + 1, 1 - slot).start()

    inv = inv_ref[...]
    for level in range(plan.levels_per_step):
        inv = inverse_level(d_ref[...], inv, step * plan.levels_per_step + level)
    inv_ref[...] = inv

    l_high, l_low = split(l_ref[...].reshape(rows, width))
    left = jnp.concatenate([l_high, l_low], 1).T
    fetch(step, slot).wait()
    flat = buf.at[slot].reshape(rows * plan.pitch, width)
    kept = pl.ds(pl.multiple_of(jnp.maximum(step - plan.skip, 0) * rows, rows), rows)
    for first in range(0, n_blocks, plan.group):
        x = jnp.concatenate(
            [flat[pl.ds(b, rows, stride=plan.pitch), :] for b in range(first, first + plan.group)], 1
        )
        high, low = split(x)
        here = pl.ds(first * width, plan.group * width)
        high_ref[kept, here] = high
        low_ref[kept, here] = low
        both = dot(left, high)
        acc[:, here] += both[:width] + both[width:] + dot(left[:width], low)

    @pl.when(step == n_steps - 1)
    def _():
        for b in range(n_blocks):
            here = pl.ds(b * width, width)
            turned[here, :] = acc[:, here].T
        size = outs[0].shape[0]
        for k, out in enumerate(outs):
            start = pl.multiple_of((me_ref[0] ^ k) * size, size)
            out[...] = turned[pl.ds(start, size), :]


def flip_parts(plan, trail, panel, diag_block, ids, me, n_row):
    width, n_blocks = plan.width, plan.n_blocks
    size = n_blocks * width // n_row
    kept = plan.keep * plan.chunk_rows
    qb, n_sub, ratio, qs, rows = plan.view
    if plan.pitch > n_blocks:
        source = trail.reshape(*plan.view, n_blocks, width)
        buffer = pltpu.VMEM((2, n_sub, rows, plan.pitch, width), F32)
    else:
        source = trail.reshape(*plan.view[:4], rows * n_blocks, width)
        buffer = pltpu.VMEM((2, n_sub, rows * n_blocks, width), F32)

    def l_index(i, me, ids):
        b, h, s = plan.chunk_at(ids[plan.flip_place(i)])
        return (b, 0, h, s, 0, 0)

    square = pl.BlockSpec((width, width), lambda i, me, ids: (0, 0))
    whole = pl.BlockSpec(memory_space=pltpu.VMEM)
    resident = pltpu.VMEM((kept, n_blocks * width), BF16)
    n = plan.n_chunks * plan.chunk_rows
    out = pl.pallas_call(
        functools.partial(flip_body, plan, n_row),
        grid_spec=pltpu.PrefetchScalarGridSpec(
            num_scalar_prefetch=2,
            grid=(plan.n_chunks,),
            in_specs=[
                pl.BlockSpec(memory_space=pl.ANY),
                pl.BlockSpec((None, n_sub, None, None, rows, width), l_index),
                square,
            ],
            out_specs=[pl.BlockSpec((size, width), lambda i, me, ids: (0, 0))] * n_row + [square, whole, whole],
            scratch_shapes=[
                pltpu.VMEM((width, n_blocks * width), F32),
                pltpu.VMEM((n_blocks * width, width), F32),
                buffer,
                pltpu.SemaphoreType.DMA((2,)),
            ],
        ),
        out_shape=[jax.ShapeDtypeStruct((size, width), F32)] * n_row
        + [jax.ShapeDtypeStruct((width, width), F32), resident, resident],
        compiler_params=pltpu.CompilerParams(vmem_limit_bytes=FLIP_VMEM),
        cost_estimate=pl.CostEstimate(
            flops=6 * n * n_blocks * width * width, bytes_accessed=4 * n * n_blocks * width, transcendentals=0
        ),
        name="flip",
    )(me, ids, source, panel.reshape(*plan.view, width), diag_block)
    return out[:n_row], out[n_row], out[n_row + 1], out[n_row + 2]


def inverse_start(d):
    i = lax.broadcasted_iota(jnp.int32, d.shape, 0)
    j = lax.broadcasted_iota(jnp.int32, d.shape, 1)
    return jnp.where(i == j, 1.0 / d, 0.0)


def inverse_level(d, inv, level):
    i = lax.broadcasted_iota(jnp.int32, d.shape, 0)
    j = lax.broadcasted_iota(jnp.int32, d.shape, 1)
    same = (i >> (level + 1)) == (j >> (level + 1))
    below = (i >> level) > (j >> level)
    part = jnp.where(jnp.logical_and(same, below), d, 0.0)
    return inv - full_dot(inv, full_dot(part, inv))


def direct_body(n_blocks, group, half, ids_ref, s_ref, p_ref, away_ref, keep_ref, right):
    step = pl.program_id(0)
    width = p_ref.shape[1]

    @pl.when(step == 0)
    def _():
        for g in range(n_blocks // group):
            high, low = split(p_ref[pl.ds(g * group * width, group * width), :])
            right[g, :, :width] = high
            right[g, :, width:] = low

    n_sub, sub_rows, _ = s_ref.shape
    rows = sub_rows // n_blocks

    def column(b):
        return jnp.concatenate([s_ref[i, pl.ds(b, rows, stride=n_blocks), :] for i in range(n_sub)], 0)

    both, rest = None, None
    for g in range(n_blocks // group):
        x = jnp.concatenate([column(g * group + b) for b in range(group)], 1)
        high, low = split(x)
        new_both = dot(high, right[g])
        new_rest = dot(low, right[g, :, :width])
        both = new_both if both is None else both + new_both
        rest = new_rest if rest is None else rest + new_rest
    result = both[:, :width] + both[:, width:] + rest

    @pl.when(step < half)
    def _():
        away_ref[...] = result

    @pl.when(step >= half)
    def _():
        keep_ref[...] = result


def direct_chunks(chunked, col_panel, ids, first, half, chunk_at):
    _, n_sub, _, _, sub_rows, width = chunked.shape
    n_blocks = col_panel.shape[0] // width
    group = math.gcd(n_blocks, 2)
    chunk_rows = n_sub * sub_rows // n_blocks

    def s_index(i, ids):
        qb, h, qs = chunk_at(ids[first + i])
        return (qb, 0, h, qs, 0, 0)

    out = jax.ShapeDtypeStruct((half * chunk_rows, width), F32)
    return pl.pallas_call(
        functools.partial(direct_body, n_blocks, group, half),
        grid_spec=pltpu.PrefetchScalarGridSpec(
            num_scalar_prefetch=1,
            grid=(2 * half,),
            in_specs=[
                pl.BlockSpec((None, n_sub, None, None, sub_rows, width), s_index),
                pl.BlockSpec((n_blocks * width, width), lambda i, ids: (0, 0)),
            ],
            out_specs=[
                pl.BlockSpec((chunk_rows, width), lambda i, ids: (jnp.minimum(i, half - 1), 0)),
                pl.BlockSpec((chunk_rows, width), lambda i, ids: (jnp.maximum(i - half, 0), 0)),
            ],
            scratch_shapes=[pltpu.VMEM((n_blocks // group, group * width, 2 * width), BF16)],
        ),
        out_shape=[out, out],
        compiler_params=pltpu.CompilerParams(vmem_limit_bytes=CHUNK_VMEM),
        cost_estimate=pl.CostEstimate(
            flops=12 * half * chunk_rows * n_blocks * width * width,
            bytes_accessed=8 * half * chunk_rows * n_blocks * width,
            transcendentals=0,
        ),
        name="direct",
    )(ids, chunked, col_panel)


def kept_body(first, half, high_ref, low_ref, p_ref, away_ref, keep_ref, right):
    step = pl.program_id(0)
    width = p_ref.shape[1]
    rows = away_ref.shape[0]

    @pl.when(step == 0)
    def _():
        high, low = split(p_ref[...])
        right[:, :width] = high
        right[:, width:] = low

    here = pl.ds(pl.multiple_of((first + step) * rows, rows), rows)
    both = dot(high_ref[here, :], right[...])
    result = both[:, :width] + both[:, width:] + dot(low_ref[here, :], right[:, :width])

    @pl.when(step < half)
    def _():
        away_ref[...] = result

    @pl.when(step >= half)
    def _():
        keep_ref[...] = result


def direct_kept(plan, high, low, col_panel, first, half):
    rows, width, depth = plan.chunk_rows, plan.width, col_panel.shape[0]
    out = jax.ShapeDtypeStruct((half * rows, width), F32)
    held = pl.BlockSpec(memory_space=pltpu.VMEM)
    return pl.pallas_call(
        functools.partial(kept_body, first, half),
        grid=(2 * half,),
        in_specs=[held, held, pl.BlockSpec((depth, width), lambda i: (0, 0))],
        out_specs=[
            pl.BlockSpec((rows, width), lambda i: (jnp.minimum(i, half - 1), 0)),
            pl.BlockSpec((rows, width), lambda i: (jnp.maximum(i - half, 0), 0)),
        ],
        out_shape=[out, out],
        scratch_shapes=[pltpu.VMEM((depth, 2 * width), BF16)],
        compiler_params=pltpu.CompilerParams(vmem_limit_bytes=DIRECT_VMEM),
        cost_estimate=pl.CostEstimate(
            flops=12 * half * rows * depth * width, bytes_accessed=8 * half * rows * width, transcendentals=0
        ),
        name="direct_kept",
    )(high, low, col_panel)


def solve_body(n_terms, ids_ref, *refs):
    terms, (inv_ref, b_ref, x_ref) = refs[:n_terms], refs[n_terms:]
    image = terms[0][...]
    for term in terms[1:]:
        image = image + term[...]
    total = b_ref[...].reshape(image.shape) - image
    x_ref[...] = full_dot(total, inv_ref[...])


def gram_body(ids_ref, x_ref, l_ref, g_ref):
    x = x_ref[...]
    g_ref[...] = -lax.dot_general(
        x, l_ref[...].reshape(x.shape), (((0,), (0,)), ((), ())), precision=HIGHEST, preferred_element_type=F32
    )


def on_my_chunk(plan, body, ids, inputs, laid_out, out_shape, name):
    _, n_sub, _, _, rows = plan.view

    def at(i, ids):
        b, h, s = plan.chunk_at(ids[plan.n_chunks - 1])
        return (b, 0, h, s, 0, 0)

    def whole(shape):
        return pl.BlockSpec(shape, lambda i, ids: (0, 0))

    return pl.pallas_call(
        body,
        grid_spec=pltpu.PrefetchScalarGridSpec(
            num_scalar_prefetch=1,
            grid=(1,),
            in_specs=[whole(x.shape) for x in inputs]
            + [pl.BlockSpec((None, n_sub, None, None, rows, plan.width), at)],
            out_specs=whole(out_shape),
        ),
        out_shape=jax.ShapeDtypeStruct(out_shape, F32),
        compiler_params=pltpu.CompilerParams(vmem_limit_bytes=SMALL_VMEM),
        name=name,
    )(ids, *inputs, laid_out.reshape(*plan.view, plan.width))


def place_body(plan, slots, has_base, ids_ref, *refs):
    out_ref, sems = refs[-2:]
    pieces = refs[1:-2] if has_base else refs[:-2]
    _, n_sub, _, _, rows = plan.view
    copies = []
    for k, (piece, slot) in enumerate(zip(pieces, slots)):
        b, h, s = plan.chunk_at(ids_ref[slot[0]])
        for i in range(n_sub):
            source = piece.at[pl.ds(i * rows, rows), :]
            copies.append(pltpu.make_async_copy(source, out_ref.at[b, i, h, s], sems.at[k, i]))
    for copy in copies:
        copy.start()
    for copy in copies:
        copy.wait()


def place(plan, base, pieces, slots, ids):
    _, n_sub, _, _, _ = plan.view
    anywhere = pl.BlockSpec(memory_space=pl.ANY)
    held = pl.BlockSpec(memory_space=pltpu.VMEM)
    bases = [] if base is None else [base]
    return pl.pallas_call(
        functools.partial(place_body, plan, [(slot,) for slot in slots], base is not None),
        grid_spec=pltpu.PrefetchScalarGridSpec(
            num_scalar_prefetch=1,
            grid=(1,),
            in_specs=[anywhere] * len(bases) + [held] * len(pieces),
            out_specs=anywhere,
            scratch_shapes=[pltpu.SemaphoreType.DMA((len(pieces), n_sub))],
        ),
        out_shape=jax.ShapeDtypeStruct((*plan.view, plan.width), F32),
        input_output_aliases={1: 0} if bases else {},
        compiler_params=pltpu.CompilerParams(vmem_limit_bytes=SMALL_VMEM),
        name="place",
    )(ids, *bases, *pieces)


class Plan:
    def __init__(self, n_row, n_col, col_blocks, width):
        self.n_row, self.n_chunks = n_row, n_col
        self.n_blocks, self.width = col_blocks, width
        self.group = math.gcd(col_blocks, 2)
        qb = min(n_row, col_blocks)
        self.qs = n_row // qb
        self.view = (qb, col_blocks // qb, n_col // n_row, self.qs, width // self.qs)
        self.chunk_rows = self.view[1] * self.view[4]
        self.pitch = col_blocks
        if col_blocks % 16 == 0:
            self.pitch = col_blocks + 8
        n_z = n_col // 2
        self.far = n_z // 2
        self.steps, self.offsets, self.twins = [], [], []
        for distance in range(self.far, -1, -1):
            here = sorted({distance % n_z, -distance % n_z})
            self.steps.append((len(self.offsets), here))
            self.offsets += here + here
            self.twins += [1] * len(here) + [0] * len(here)
        fits = KEEP_BYTES // (4 * self.chunk_rows * col_blocks * width)
        ends = [begin + 2 * len(here) for begin, here in self.steps]
        self.keep = max([end for end in ends if end <= fits], default=ends[0])
        self.skip = self.n_chunks - self.keep
        self.levels_per_step = -(-(width - 1).bit_length() // self.n_chunks)

    def chunk_at(self, chunk):
        h, q = chunk // self.n_row, chunk % self.n_row
        return q // self.qs, h, q % self.qs

    def flip_place(self, i):
        return (i + self.keep) % self.n_chunks


def per_device(trail_adjoint, panel, panel_adjoint, diag_block):
    width = diag_block.shape[0]
    n_row = lax.axis_size("row")
    n_col = lax.axis_size("col")
    ratio = n_col // n_row
    n_z = n_col // 2
    row_blocks = panel.shape[0]
    col_blocks = trail_adjoint.shape[2]
    plan = Plan(n_row, n_col, col_blocks, width)
    row_index = lax.axis_index("row")
    col_index = lax.axis_index("col")
    z, core = col_index // 2, col_index % 2
    move = functools.partial(send, n_row=n_row, n_col=n_col)
    up = lambda r, c: (r, (c + 2) % n_col)
    down = lambda r, c: (r, (c - 2) % n_col)
    twin = lambda r, c: (r, c ^ 1)
    ids = (z + jnp.array(plan.offsets, jnp.int32)) % n_z * 2 + (core ^ jnp.array(plan.twins, jnp.int32))

    def to_panel_user(r, c):
        h, s = divmod(c, n_row)
        return r ^ (((r ^ s) + 1) % n_row), h * n_row + r

    chosen = choose(panel.reshape(col_blocks, ratio, width, width), (col_index // n_row).reshape(1))
    col_panel = move(chosen.reshape(col_blocks * width, width), to_panel_user)

    parts, inv, high, low = flip_parts(plan, trail_adjoint, panel, diag_block, ids, row_index.reshape(1), n_row)
    flipped = parts[0]
    for k in range(1, n_row):
        flipped = flipped + move(parts[k], lambda r, c: (r ^ k, c))
    flipped = move(flipped, lambda r, c: (c % n_row, c // n_row * n_row + r))

    rows = plan.chunk_rows
    cut = rows // 2
    below, above, mine, after = None, None, None, None
    for begin, here in plan.steps:
        right, _ = lax.optimization_barrier((col_panel, after))
        if begin + 2 * len(here) <= plan.keep:
            away, keep = direct_kept(plan, high, low, right, begin, len(here))
        else:
            chunked = trail_adjoint.reshape(*plan.view[:4], plan.view[4] * col_blocks, width)
            away, keep = direct_chunks(chunked, right, ids, begin, len(here), plan.chunk_at)
        after = total = keep + move(away, twin)
        if here[0] == 0:
            mine = [total, below, above, flipped]
        elif len(here) == 1:
            below, above = move(total[:cut], up), move(total[cut:], down)
        else:
            first, second = total[:rows], total[rows:]
            if below.shape[0] == cut:
                first = jnp.concatenate([first[:cut] + below, first[cut:]], 0)
                second = jnp.concatenate([second[:cut], second[cut:] + above], 0)
            else:
                first, second = first + below, second + above
            below, above = move(first, up), move(second, down)

    x = on_my_chunk(
        plan, functools.partial(solve_body, len(mine)), ids, mine + [inv], panel_adjoint, (rows, width), "solve"
    )

    held = {0: x}
    below, above = x, x
    for distance in range(1, plan.far):
        below, above = move(below, up), move(above, down)
        held[-distance % n_z], held[distance] = below, above
    gram = on_my_chunk(plan, gram_body, ids, [x], panel, (width, width), "gram")
    gram = gram + sum(move(gram, lambda r, c: (r ^ k, c)) for k in range(1, n_row))
    other = {d: move(piece, twin) for d, piece in held.items()}
    halves = [move(below[:cut], up), move(above[cut:], down)]
    moving, total = gram, gram
    for _ in range(1, n_z):
        moving = move(moving, up)
        total = total + moving
    order = (z + jnp.arange(n_z, dtype=jnp.int32)) % n_z * 2
    place_ids = jnp.concatenate([order + core, order + (1 - core)])
    near = sorted(held)
    solved = place(
        plan, None, [held[d] for d in near] + [other[d] for d in near], near + [n_z + d for d in near], place_ids
    )
    last = jnp.concatenate(halves, 0)
    solved = place(plan, solved, [last, move(last, twin)], [plan.far, n_z + plan.far], place_ids)
    gram = total + move(total, twin)
    return (solved.reshape(row_blocks, width, width), jnp.tril(gram))


def solution(mesh):
    in_specs = (P(None, "row", None, "col"), P(None, "row", None), P(None, "row", None), P())
    out_specs = (P(None, "row", None), P())
    return jax.shard_map(
        per_device, mesh=mesh, in_specs=in_specs, out_specs=out_specs, check_vma=False
    )
```

time: 329 us -> 121 us (0.37)
  waiting for transfers between devices: 166 us -> 43.4 us
  matrix products: 120 us -> 0 us
  Pallas kernels: 0 us -> 41.5 us
  starting transfers between devices: 0.12 us -> 32.6 us
  other arithmetic: 16.2 us -> 1.06 us
  between operations: 13.9 us -> 0.91 us
  local copies, waits for them, and re-layouts: 13.1 us -> 1.67 us
    psum x3 -> x0, waiting for transfers between devices: 166 us -> none  [the longest x1 72.5 us: spread(): return lax.psum(jnp.where(mine, value, jnp.zeros_like(value)), axis)]
    dot_general x3 -> x0, matrix products: 116 us -> none  [the longest x1 61.2 us: per_device(): jnp.einsum('aibj,aik->bjk', trail_adjoint, panel, precision=lax.Precision...]
    ppermute x0 -> x27, waiting for transfers between devices: none -> 43.4 us  [send(): return lax.ppermute(x, AXES, pairs)]
    pallas_call x0 -> x9, Pallas kernels: none -> 41.5 us  [the longest x1 20.7 us: flip_parts(): pl.pallas_call(functools.partial(flip_body, plan, n_row), grid_spec=pltpu...]
    ppermute x0 -> x27, starting transfers between devices: none -> 32.6 us  [send(): return lax.ppermute(x, AXES, pairs)]
    another operation x2 -> x0, other arithmetic: 9.82 us -> none  [solve_rows(): lax.linalg.triangular_solve(diag_block, total, left_side=False, lower=True)]
    unnamed x8 -> x13, local copies, waits for them, and re-layouts: 7.5 us -> 1.62 us
    sub x1 -> x0, other arithmetic: 3.88 us -> none  [per_device(): total = flat_given - direct]
  transfers between devices with their start and end apart: 3 -> 27, of which waited for: 3 -> 14; matrix products, arithmetic and copies ran while one was open for 4% -> 1% of each run, Pallas kernels for 0% -> 24%
where the time goes in v1:
time: 121 us
  waiting for transfers between devices  43.4 us (36%)
  Pallas kernels  41.5 us (34%)
  starting transfers between devices  32.6 us (27%)
  local copies, waits for them, and re-layouts  1.67 us (1%)
    ppermute x27, waiting for transfers between devices, send(): return lax.ppermute(x, AXES, pairs)  43.4 us
    ppermute x27, starting transfers between devices, send(): return lax.ppermute(x, AXES, pairs)  32.6 us
    pallas_call x1, Pallas kernels, flip_parts(): pl.pallas_call(functools.partial(flip_body, plan, n_row), grid_spec=pltpu...  20.7 us
    pallas_call x2, Pallas kernels, direct_kept(): pl.pallas_call(functools.partial(kept_body, first, half), grid=(2 * half,...  8.26 us
    pallas_call x1, Pallas kernels, direct_chunks(): pl.pallas_call(functools.partial(direct_body, n_blocks, group, half), gri...  6.3 us
    pallas_call x2, Pallas kernels, place(): pl.pallas_call(functools.partial(place_body, plan, [(slot,) for slot in s...  3.28 us
  transfers between devices with their start and end apart: 27, of which 14 were waited for; matrix products, arithmetic and copies ran while one was open for 1% of the time, Pallas kernels for 24%

profile of v1, /device:TPU:0, one launch (start us, length us, event | category | flops | bytes accessed | tf_op | source)
XLA Modules:
  0.0 121.1 jit_solution(12165035413208696657)
XLA Ops:
  0.7 1.6 %copy-done = f32[32,128,128]{2,1,0:T(8,128)S(1)} copy-done((f32[32,128,128]{2,1,0:T(8,128)S(1)}, f32[32,128,128]{2,1,0:T(8,128)}, u32[]{:S(2)}) %copy-start) | copy-done | bytes 2097176
  2.3 1.0 choose.1
  3.3 2.9 %collective-permute-start = (f32[2048,128]{1,0:T(8,128)}, f32[2048,128]{1,0:T(8,128)S(1)}, u32[]{:S(2)}, u32[]{:S(2)}) collective-permute-start(f32[2048,128]{1,0:T(8,128)} %bitcast.3), channel_id=1, source_target_pairs={{0,8},{1,16},{2,24},{3,0},{4,12},{5,20},{6,28},{7,4},{8,25},{9,1},... | collective-permute-start | bytes 3145736 | tf_op jit(solution)/shard_map/ppermute | solution.py:41
  6.3 20.7 %flip.1 = (f32[512,128]{1,0:T(8,128)S(1)}, f32[512,128]{1,0:T(8,128)S(1)}, f32[512,128]{1,0:T(8,128)S(1)}, f32[512,128]{1,0:T(8,128)S(1)}, f32[128,128]{1,0:T(8,...) custom-call(s32[1]{0:T(128)} %bitcast.4.me_ref, s32[8]{0:T(128)S(1)} %fusion.2.ids_ref, ...), custom_call_target="tpu_custom_call" | custom-call | flops 6442450944 | bytes 33554432 | tf_op jit(solution)/shard_map/flip/pallas_call | solution.py:138
  27.0 3.1 %collective-permute-done.p_ref = f32[2048,128]{1,0:T(8,128)S(1)} collective-permute-done((f32[2048,128]{1,0:T(8,128)}, f32[2048,128]{1,0:T(8,128)S(1)}, u32[]{:S(2)}, u32[]{:S(2)}) %collective-permute-start) | collective-permute-done | bytes 1048608 | tf_op jit(solution)/shard_map/ppermute | solution.py:41
  30.1 2.8 %direct_kept.2 = (f32[512,128]{1,0:T(8,128)S(1)}, f32[512,128]{1,0:T(8,128)S(1)}) custom-call(bf16[3072,2048]{1,0:T(8,128)(2,1)S(1)} %get-tuple-element.17.high_ref, bf16[3072,2048]{1,0:T(8,128)(2,1)S(1)} %get-tuple-element.18.low_ref, f32[2048,128]{1,0:T(8,128)S(1)} %collective-permute-done.p_ref), custom_call_target="tpu_custom_call" | custom-call | flops 1610612736 | bytes 524288 | tf_op jit(solution)/shard_map/direct_kept/pallas_call | solution.py:283
  32.9 0.1 collective-permute-start.1
  33.0 1.5 %collective-permute-done.1 = f32[512,128]{1,0:T(8,128)S(1)} collective-permute-done((f32[512,128]{1,0:T(8,128)S(1)}, f32[512,128]{1,0:T(8,128)S(1)}, u32[]{:S(2)}, u32[]{:S(2)}) %collective-permute-start.1) | collective-permute-done | bytes 262176 | tf_op jit(solution)/shard_map/ppermute | solution.py:41
  34.6 5.4 %direct_kept.3 = (f32[1024,128]{1,0:T(8,128)S(1)}, f32[1024,128]{1,0:T(8,128)S(1)}) custom-call(bf16[3072,2048]{1,0:T(8,128)(2,1)S(1)} %get-tuple-element.17.high_ref, bf16[3072,2048]{1,0:T(8,128)(2,1)S(1)} %get-tuple-element.18.low_ref, f32[2048,128]{1,0:T(8,128)S(1)} %collective-permute-done.p_ref), custom_call_target="tpu_custom_call" | custom-call | flops 3221225472 | bytes 1048576 | tf_op jit(solution)/shard_map/direct_kept/pallas_call | solution.py:283
  40.0 0.2 collective-permute-start.2
  40.2 2.4 %collective-permute-start.8 = (f32[512,128]{1,0:T(8,128)S(1)}, f32[512,128]{1,0:T(8,128)S(1)}, u32[]{:S(2)}, u32[]{:S(2)}) collective-permute-start(f32[512,128]{1,0:T(8,128)S(1)} %get-tuple-element.28), channel_id=1, source_target_pairs={{0,8},{1,9},{2,10},{3,11},{4,12},{5,13},{6,14},{7,15},{8,0},{9,1},... | collective-permute-start | bytes 786440 | tf_op jit(solution)/shard_map/ppermute | solution.py:41
  42.6 0.6 collective-permute-start.9
  43.2 1.0 collective-permute-start.10
  44.2 4.0 %collective-permute-start.6 = (f32[256,128]{1,0:T(8,128)S(1)}, f32[256,128]{1,0:T(8,128)S(1)}, u32[]{:S(2)}, u32[]{:S(2)}) collective-permute-start(f32[256,128]{1,0:T(8,128)S(1)} %get-tuple-element.36), channel_id=1, source_target_pairs={{0,6},{1,7},{2,0},{3,1},{4,2},{5,3},{6,4},{7,5},{8,14},{9,15},{10,... | collective-permute-start | bytes 393224 | tf_op jit(solution)/shard_map/ppermute | solution.py:41
  48.2 1.5 %collective-permute-done.8 = f32[512,128]{1,0:T(8,128)S(1)} collective-permute-done((f32[512,128]{1,0:T(8,128)S(1)}, f32[512,128]{1,0:T(8,128)S(1)}, u32[]{:S(2)}, u32[]{:S(2)}) %collective-permute-start.8) | collective-permute-done | bytes 262176 | tf_op jit(solution)/shard_map/ppermute | solution.py:41
  49.8 2.0 %collective-permute-start.4 = (f32[256,128]{1,0:T(8,128)S(1)}, f32[256,128]{1,0:T(8,128)S(1)}, u32[]{:S(2)}, u32[]{:S(2)}) collective-permute-start(f32[256,128]{1,0:T(8,128)S(1)} %get-tuple-element.37), channel_id=1, source_target_pairs={{0,2},{1,3},{2,4},{3,5},{4,6},{5,7},{6,0},{7,1},{8,10},{9,11},{10,... | collective-permute-start | bytes 393224 | tf_op jit(solution)/shard_map/ppermute | solution.py:41
  51.8 4.7 %collective-permute-done.9 = f32[512,128]{1,0:T(8,128)S(1)} collective-permute-done((f32[512,128]{1,0:T(8,128)S(1)}, f32[512,128]{1,0:T(8,128)S(1)}, u32[]{:S(2)}, u32[]{:S(2)}) %collective-permute-start.9) | collective-permute-done | bytes 262176 | tf_op jit(solution)/shard_map/ppermute | solution.py:41
  56.6 0.7 collective-permute-start.11
  57.5 3.3 %collective-permute-start.5 = (f32[512,128]{1,0:T(8,128)S(1)}, f32[512,128]{1,0:T(8,128)S(1)}, u32[]{:S(2)}, u32[]{:S(2)}) collective-permute-start(f32[512,128]{1,0:T(8,128)S(1)} %pad_maximum_fusion), channel_id=1, source_target_pairs={{0,2},{1,3},{2,4},{3,5},{4,6},{5,7},{6,0},{7,1},{8,10},{9,11},{10,... | collective-permute-start | bytes 786440 | tf_op jit(solution)/shard_map/ppermute | solution.py:41
  60.8 6.3 %direct.1 = (f32[512,128]{1,0:T(8,128)S(1)}, f32[512,128]{1,0:T(8,128)S(1)}) custom-call(s32[8]{0:T(128)S(1)} %fusion.2.ids_ref, f32[4,4,2,1,2048,128]{5,4,3,2,1,0:T(8,128)} %bitcast.14, f32[2048,128]{1,0:T(8,128)S(1)} %collective-permute-done.p_ref), custom_call_target="tpu_custom_call" | custom-call | flops 1610612736 | bytes 8388608 | tf_op jit(solution)/shard_map/direct/pallas_call | solution.py:229
  67.1 0.7 collective-permute-start.3
  67.8 2.4 %collective-permute-start.7 = (f32[512,128]{1,0:T(8,128)S(1)}, f32[512,128]{1,0:T(8,128)S(1)}, u32[]{:S(2)}, u32[]{:S(2)}) collective-permute-start(f32[512,128]{1,0:T(8,128)S(1)} %pad_maximum_fusion.1), channel_id=1, source_target_pairs={{0,6},{1,7},{2,0},{3,1},{4,2},{5,3},{6,4},{7,5},{8,14},{9,15},{10,... | collective-permute-start | bytes 786440 | tf_op jit(solution)/shard_map/ppermute | solution.py:41
  70.2 5.5 %collective-permute-done.5.refs_1_ = f32[512,128]{1,0:T(8,128)S(1)} collective-permute-done((f32[512,128]{1,0:T(8,128)S(1)}, f32[512,128]{1,0:T(8,128)S(1)}, u32[]{:S(2)}, u32[]{:S(2)}) %collective-permute-start.5) | collective-permute-done | bytes 262176 | tf_op jit(solution)/shard_map/ppermute | solution.py:41
  75.7 5.4 %collective-permute-done.7.refs_2_ = f32[512,128]{1,0:T(8,128)S(1)} collective-permute-done((f32[512,128]{1,0:T(8,128)S(1)}, f32[512,128]{1,0:T(8,128)S(1)}, u32[]{:S(2)}, u32[]{:S(2)}) %collective-permute-start.7) | collective-permute-done | bytes 262176 | tf_op jit(solution)/shard_map/ppermute | solution.py:41
  81.1 0.9 solve.1.refs_0_.x_ref
  82.1 1.0 gram.1
  83.0 0.1 collective-permute-start.22
  83.1 1.0 collective-permute-start.21
  84.1 2.4 %collective-permute-start.20 = (f32[128,128]{1,0:T(8,128)S(1)}, f32[128,128]{1,0:T(8,128)S(1)}, u32[]{:S(2)}, u32[]{:S(2)}) collective-permute-start(f32[128,128]{1,0:T(8,128)S(1)} %gram.1), channel_id=1, source_target_pairs={{0,8},{1,9},{2,10},{3,11},{4,12},{5,13},{6,14},{7,15},{8,0},{9,1},... | collective-permute-start | bytes 196616 | tf_op jit(solution)/shard_map/ppermute | solution.py:41
  86.6 2.1 %collective-permute-done.22 = f32[128,128]{1,0:T(8,128)S(1)} collective-permute-done((f32[128,128]{1,0:T(8,128)S(1)}, f32[128,128]{1,0:T(8,128)S(1)}, u32[]{:S(2)}, u32[]{:S(2)}) %collective-permute-start.22) | collective-permute-done | bytes 65568 | tf_op jit(solution)/shard_map/ppermute | solution.py:41
  88.7 0.1 collective-permute-done.20
  88.8 0.6 collective-permute-start.23
  89.5 0.6 collective-permute-start.13
  90.1 3.2 %collective-permute-start.12 = (f32[512,128]{1,0:T(8,128)S(1)}, f32[512,128]{1,0:T(8,128)S(1)}, u32[]{:S(2)}, u32[]{:S(2)}) collective-permute-start(f32[512,128]{1,0:T(8,128)S(1)} %solve.1.refs_0_.x_ref), channel_id=1, source_target_pairs={{0,6},{1,7},{2,0},{3,1},{4,2},{5,3},{6,4},{7,5},{8,14},{9,15},{10,... | collective-permute-start | bytes 786440 | tf_op jit(solution)/shard_map/ppermute | solution.py:41
  93.3 2.6 %collective-permute-done.23 = f32[128,128]{1,0:T(8,128)S(1)} collective-permute-done((f32[128,128]{1,0:T(8,128)S(1)}, f32[128,128]{1,0:T(8,128)S(1)}, u32[]{:S(2)}, u32[]{:S(2)}) %collective-permute-start.23) | collective-permute-done | bytes 65568 | tf_op jit(solution)/shard_map/ppermute | solution.py:41
  95.9 10.4 %collective-permute-done.24 = f32[128,128]{1,0:T(8,128)S(1)} collective-permute-done((f32[128,128]{1,0:T(8,128)S(1)}, f32[128,128]{1,0:T(8,128)S(1)}, u32[]{:S(2)}, u32[]{:S(2)}) %collective-permute-start.24) | collective-permute-done | bytes 65568 | tf_op jit(solution)/shard_map/ppermute | solution.py:41
  106.4 0.4 collective-permute-start.17
  106.8 3.6 %collective-permute-start.18 = (f32[256,128]{1,0:T(8,128)S(1)}, f32[256,128]{1,0:T(8,128)S(1)}, u32[]{:S(2)}, u32[]{:S(2)}) collective-permute-start(f32[256,128]{1,0:T(8,128)S(1)} %slice.45), channel_id=1, source_target_pairs={{0,6},{1,7},{2,0},{3,1},{4,2},{5,3},{6,4},{7,5},{8,14},{9,15},{10,... | collective-permute-start | bytes 393224 | tf_op jit(solution)/shard_map/ppermute | solution.py:41
  110.4 0.2 collective-permute-start.16
  110.6 2.6 %collective-permute-done.25 = f32[128,128]{1,0:T(8,128)S(1)} collective-permute-done((f32[128,128]{1,0:T(8,128)S(1)}, f32[128,128]{1,0:T(8,128)S(1)}, u32[]{:S(2)}, u32[]{:S(2)}) %collective-permute-start.25) | collective-permute-done | bytes 65568 | tf_op jit(solution)/shard_map/ppermute | solution.py:41
  113.2 2.7 %collective-permute-done.17 = f32[256,128]{1,0:T(8,128)S(1)} collective-permute-done((f32[256,128]{1,0:T(8,128)S(1)}, f32[256,128]{1,0:T(8,128)S(1)}, u32[]{:S(2)}, u32[]{:S(2)}) %collective-permute-start.17) | collective-permute-done | bytes 131104 | tf_op jit(solution)/shard_map/ppermute | solution.py:41
  115.9 0.8 collective-permute-done.18
  116.7 0.1 collective-permute-start.19
  116.8 0.1 pad_add_fusion.ids_ref
  116.9 0.3 collective-permute-done.26
  117.1 0.6 add_select_fusion
  117.8 1.9 %place.2.refs_0_ = f32[4,4,2,1,128,128]{5,4,3,2,1,0:T(8,128)} custom-call(s32[8]{0:T(128)S(1)} %pad_add_fusion.ids_ref, f32[512,128]{1,0:T(8,128)S(1)} %solve.1.refs_0_.x_ref, f32[512,128]{1,0:T(8,128)S(1)} %collective-permute-done.12.refs_1_, f32[512,128]{1,0:T(8,128)S(1)} %collective-permute-done.13.refs_2_, ...), custom_call_target="tpu_custom_call" | custom-call | tf_op jit(solution)/shard_map/place/pallas_call | solution.py:363
  119.7 1.4 %place.3 = f32[4,4,2,1,128,128]{5,4,3,2,1,0:T(8,128)} custom-call(s32[8]{0:T(128)S(1)} %pad_add_fusion.ids_ref, f32[4,4,2,1,128,128]{5,4,3,2,1,0:T(8,128)} %place.2.refs_0_, f32[512,128]{1,0:T(8,128)S(1)} %constant_dynamic-update-slice_fusion.refs_1_, f32[512,128]{1,0:T(8,128)S(1)} %collective-permute-done.19.refs_2_), custom_call_target="tpu_custom_call", output_to_operand_aliasing={{}: (1, {})} | custom-call | tf_op jit(solution)/shard_map/place/pallas_call | solution.py:363
  (46 shorter events, 0.5 us)
Async XLA Ops:
  0.6 5.6 %copy-start.4 = (s32[8]{0:T(128)S(1)}, s32[8]{0:T(128)}, u32[]{:S(2)}) copy-start(s32[8]{0:T(128)} %constant.73.clone) | copy-start | bytes 100
  0.6 5.6 %copy-start.5 = (s32[8]{0:T(128)S(1)}, s32[8]{0:T(128)}, u32[]{:S(2)}) copy-start(s32[8]{0:T(128)} %constant.72.clone) | copy-start | bytes 100
  0.7 1.6 %copy-start = (f32[32,128,128]{2,1,0:T(8,128)S(1)}, f32[32,128,128]{2,1,0:T(8,128)}, u32[]{:S(2)}) copy-start(f32[32,128,128]{2,1,0:T(8,128)} %param.7) | copy-start | bytes 6291460
  2.3 4.0 %copy-start.1 = (f32[32,128,128]{2,1,0:T(8,128)S(1)}, f32[32,128,128]{2,1,0:T(8,128)}, u32[]{:S(2)}) copy-start(f32[32,128,128]{2,1,0:T(8,128)} %param.7) | copy-start | bytes 6291460
  2.3 4.0 %copy-start.3 = (f32[128,128]{1,0:T(8,128)S(1)}, f32[128,128]{1,0:T(8,128)}, u32[]{:S(2)}) copy-start(f32[128,128]{1,0:T(8,128)} %d_ref.1) | copy-start | bytes 196612
  3.3 26.8 %collective-permute-start = (f32[2048,128]{1,0:T(8,128)}, f32[2048,128]{1,0:T(8,128)S(1)}, u32[]{:S(2)}, u32[]{:S(2)}) collective-permute-start(f32[2048,128]{1,0:T(8,128)} %bitcast.3), channel_id=1, source_target_pairs={{0,8},{1,16},{2,24},{3,0},{4,12},{5,20},{6,28},{7,4},{8,25},{9,1},... | collective-permute-start | bytes 3145736 | tf_op jit(solution)/shard_map/ppermute | solution.py:41
  32.9 1.6 %collective-permute-start.1 = (f32[512,128]{1,0:T(8,128)S(1)}, f32[512,128]{1,0:T(8,128)S(1)}, u32[]{:S(2)}, u32[]{:S(2)}) collective-permute-start(f32[512,128]{1,0:T(8,128)S(1)} %get-tuple-element.20), channel_id=1, source_target_pairs={{0,1},{1,0},{2,3},{3,2},{4,5},{5,4},{6,7},{7,6},{8,9},{9,8},{10,11... | collective-permute-start | bytes 786440 | tf_op jit(solution)/shard_map/ppermute | solution.py:41
  40.0 17.2 %collective-permute-start.2 = (f32[1024,128]{1,0:T(8,128)S(1)}, f32[1024,128]{1,0:T(8,128)S(1)}, u32[]{:S(2)}, u32[]{:S(2)}) collective-permute-start(f32[1024,128]{1,0:T(8,128)S(1)} %get-tuple-element.23), channel_id=1, source_target_pairs={{0,1},{1,0},{2,3},{3,2},{4,5},{5,4},{6,7},{7,6},{8,9},{9,8},{10,11... | collective-permute-start | bytes 1572872 | tf_op jit(solution)/shard_map/ppermute | solution.py:41
  40.2 9.5 %collective-permute-start.8 = (f32[512,128]{1,0:T(8,128)S(1)}, f32[512,128]{1,0:T(8,128)S(1)}, u32[]{:S(2)}, u32[]{:S(2)}) collective-permute-start(f32[512,128]{1,0:T(8,128)S(1)} %get-tuple-element.28), channel_id=1, source_target_pairs={{0,8},{1,9},{2,10},{3,11},{4,12},{5,13},{6,14},{7,15},{8,0},{9,1},... | collective-permute-start | bytes 786440 | tf_op jit(solution)/shard_map/ppermute | solution.py:41
  42.6 13.9 %collective-permute-start.9 = (f32[512,128]{1,0:T(8,128)S(1)}, f32[512,128]{1,0:T(8,128)S(1)}, u32[]{:S(2)}, u32[]{:S(2)}) collective-permute-start(f32[512,128]{1,0:T(8,128)S(1)} %get-tuple-element.29), channel_id=1, source_target_pairs={{0,16},{1,17},{2,18},{3,19},{4,20},{5,21},{6,22},{7,23},{8,24},{9,... | collective-permute-start | bytes 786440 | tf_op jit(solution)/shard_map/ppermute | solution.py:41
  43.2 13.3 %collective-permute-start.10 = (f32[512,128]{1,0:T(8,128)S(1)}, f32[512,128]{1,0:T(8,128)S(1)}, u32[]{:S(2)}, u32[]{:S(2)}) collective-permute-start(f32[512,128]{1,0:T(8,128)S(1)} %get-tuple-element.30), channel_id=1, source_target_pairs={{0,24},{1,25},{2,26},{3,27},{4,28},{5,29},{6,30},{7,31},{8,16},{9,... | collective-permute-start | bytes 786440 | tf_op jit(solution)/shard_map/ppermute | solution.py:41
  44.2 13.1 %collective-permute-start.6 = (f32[256,128]{1,0:T(8,128)S(1)}, f32[256,128]{1,0:T(8,128)S(1)}, u32[]{:S(2)}, u32[]{:S(2)}) collective-permute-start(f32[256,128]{1,0:T(8,128)S(1)} %get-tuple-element.36), channel_id=1, source_target_pairs={{0,6},{1,7},{2,0},{3,1},{4,2},{5,3},{6,4},{7,5},{8,14},{9,15},{10,... | collective-permute-start | bytes 393224 | tf_op jit(solution)/shard_map/ppermute | solution.py:41
  49.8 7.6 %collective-permute-start.4 = (f32[256,128]{1,0:T(8,128)S(1)}, f32[256,128]{1,0:T(8,128)S(1)}, u32[]{:S(2)}, u32[]{:S(2)}) collective-permute-start(f32[256,128]{1,0:T(8,128)S(1)} %get-tuple-element.37), channel_id=1, source_target_pairs={{0,2},{1,3},{2,4},{3,5},{4,6},{5,7},{6,0},{7,1},{8,10},{9,11},{10,... | collective-permute-start | bytes 393224 | tf_op jit(solution)/shard_map/ppermute | solution.py:41
  56.6 13.6 %collective-permute-start.11 = (f32[512,128]{1,0:T(8,128)S(1)}, f32[512,128]{1,0:T(8,128)S(1)}, u32[]{:S(2)}, u32[]{:S(2)}) collective-permute-start(f32[512,128]{1,0:T(8,128)S(1)} %add_add_fusion), channel_id=1, source_target_pairs={{0,0},{1,8},{2,16},{3,24},{4,4},{5,12},{6,20},{7,28},{8,1},{9,9},{... | collective-permute-start | bytes 786440 | tf_op jit(solution)/shard_map/ppermute | solution.py:41
  57.5 18.3 %collective-permute-start.5 = (f32[512,128]{1,0:T(8,128)S(1)}, f32[512,128]{1,0:T(8,128)S(1)}, u32[]{:S(2)}, u32[]{:S(2)}) collective-permute-start(f32[512,128]{1,0:T(8,128)S(1)} %pad_maximum_fusion), channel_id=1, source_target_pairs={{0,2},{1,3},{2,4},{3,5},{4,6},{5,7},{6,0},{7,1},{8,10},{9,11},{10,... | collective-permute-start | bytes 786440 | tf_op jit(solution)/shard_map/ppermute | solution.py:41
  60.8 20.4 %copy-start.2 = (f32[32,128,128]{2,1,0:T(8,128)S(1)}, f32[32,128,128]{2,1,0:T(8,128)}, u32[]{:S(2)}) copy-start(f32[32,128,128]{2,1,0:T(8,128)} %param.8) | copy-start | bytes 6291460
  67.1 3.1 %collective-permute-start.3 = (f32[512,128]{1,0:T(8,128)S(1)}, f32[512,128]{1,0:T(8,128)S(1)}, u32[]{:S(2)}, u32[]{:S(2)}) collective-permute-start(f32[512,128]{1,0:T(8,128)S(1)} %get-tuple-element.26), channel_id=1, source_target_pairs={{0,1},{1,0},{2,3},{3,2},{4,5},{5,4},{6,7},{7,6},{8,9},{9,8},{10,11... | collective-permute-start | bytes 786440 | tf_op jit(solution)/shard_map/ppermute | solution.py:41
  67.8 13.4 %collective-permute-start.7 = (f32[512,128]{1,0:T(8,128)S(1)}, f32[512,128]{1,0:T(8,128)S(1)}, u32[]{:S(2)}, u32[]{:S(2)}) collective-permute-start(f32[512,128]{1,0:T(8,128)S(1)} %pad_maximum_fusion.1), channel_id=1, source_target_pairs={{0,6},{1,7},{2,0},{3,1},{4,2},{5,3},{6,4},{7,5},{8,14},{9,15},{10,... | collective-permute-start | bytes 786440 | tf_op jit(solution)/shard_map/ppermute | solution.py:41
  83.0 5.7 %collective-permute-start.22 = (f32[128,128]{1,0:T(8,128)S(1)}, f32[128,128]{1,0:T(8,128)S(1)}, u32[]{:S(2)}, u32[]{:S(2)}) collective-permute-start(f32[128,128]{1,0:T(8,128)S(1)} %gram.1), channel_id=1, source_target_pairs={{0,24},{1,25},{2,26},{3,27},{4,28},{5,29},{6,30},{7,31},{8,16},{9,... | collective-permute-start | bytes 196616 | tf_op jit(solution)/shard_map/ppermute | solution.py:41
  83.1 5.6 %collective-permute-start.21 = (f32[128,128]{1,0:T(8,128)S(1)}, f32[128,128]{1,0:T(8,128)S(1)}, u32[]{:S(2)}, u32[]{:S(2)}) collective-permute-start(f32[128,128]{1,0:T(8,128)S(1)} %gram.1), channel_id=1, source_target_pairs={{0,16},{1,17},{2,18},{3,19},{4,20},{5,21},{6,22},{7,23},{8,24},{9,... | collective-permute-start | bytes 196616 | tf_op jit(solution)/shard_map/ppermute | solution.py:41
  84.1 4.7 %collective-permute-start.20 = (f32[128,128]{1,0:T(8,128)S(1)}, f32[128,128]{1,0:T(8,128)S(1)}, u32[]{:S(2)}, u32[]{:S(2)}) collective-permute-start(f32[128,128]{1,0:T(8,128)S(1)} %gram.1), channel_id=1, source_target_pairs={{0,8},{1,9},{2,10},{3,11},{4,12},{5,13},{6,14},{7,15},{8,0},{9,1},... | collective-permute-start | bytes 196616 | tf_op jit(solution)/shard_map/ppermute | solution.py:41
  88.8 7.0 %collective-permute-start.23 = (f32[128,128]{1,0:T(8,128)S(1)}, f32[128,128]{1,0:T(8,128)S(1)}, u32[]{:S(2)}, u32[]{:S(2)}) collective-permute-start(f32[128,128]{1,0:T(8,128)S(1)} %add_add_fusion.2), channel_id=1, source_target_pairs={{0,2},{1,3},{2,4},{3,5},{4,6},{5,7},{6,0},{7,1},{8,10},{9,11},{10,... | collective-permute-start | bytes 196616 | tf_op jit(solution)/shard_map/ppermute | solution.py:41
  89.5 16.9 %collective-permute-start.13 = (f32[512,128]{1,0:T(8,128)S(1)}, f32[512,128]{1,0:T(8,128)S(1)}, u32[]{:S(2)}, u32[]{:S(2)}) collective-permute-start(f32[512,128]{1,0:T(8,128)S(1)} %solve.1.refs_0_.x_ref), channel_id=1, source_target_pairs={{0,2},{1,3},{2,4},{3,5},{4,6},{5,7},{6,0},{7,1},{8,10},{9,11},{10,... | collective-permute-start | bytes 786440 | tf_op jit(solution)/shard_map/ppermute | solution.py:41
  90.1 16.7 %collective-permute-start.12 = (f32[512,128]{1,0:T(8,128)S(1)}, f32[512,128]{1,0:T(8,128)S(1)}, u32[]{:S(2)}, u32[]{:S(2)}) collective-permute-start(f32[512,128]{1,0:T(8,128)S(1)} %solve.1.refs_0_.x_ref), channel_id=1, source_target_pairs={{0,6},{1,7},{2,0},{3,1},{4,2},{5,3},{6,4},{7,5},{8,14},{9,15},{10,... | collective-permute-start | bytes 786440 | tf_op jit(solution)/shard_map/ppermute | solution.py:41
  95.8 10.4 %collective-permute-start.24 = (f32[128,128]{1,0:T(8,128)S(1)}, f32[128,128]{1,0:T(8,128)S(1)}, u32[]{:S(2)}, u32[]{:S(2)}) collective-permute-start(f32[128,128]{1,0:T(8,128)S(1)} %collective-permute-done.23), channel_id=1, source_target_pairs={{0,2},{1,3},{2,4},{3,5},{4,6},{5,7},{6,0},{7,1},{8,10},{9,11},{10,... | collective-permute-start | bytes 196616 | tf_op jit(solution)/shard_map/ppermute | solution.py:41
  106.3 6.9 %collective-permute-start.25 = (f32[128,128]{1,0:T(8,128)S(1)}, f32[128,128]{1,0:T(8,128)S(1)}, u32[]{:S(2)}, u32[]{:S(2)}) collective-permute-start(f32[128,128]{1,0:T(8,128)S(1)} %collective-permute-done.24), channel_id=1, source_target_pairs={{0,2},{1,3},{2,4},{3,5},{4,6},{5,7},{6,0},{7,1},{8,10},{9,11},{10,... | collective-permute-start | bytes 196616 | tf_op jit(solution)/shard_map/ppermute | solution.py:41
  106.3 11.5 %collective-permute-start.14 = (f32[512,128]{1,0:T(8,128)S(1)}, f32[512,128]{1,0:T(8,128)S(1)}, u32[]{:S(2)}, u32[]{:S(2)}) collective-permute-start(f32[512,128]{1,0:T(8,128)S(1)} %solve.1.refs_0_.x_ref), channel_id=1, source_target_pairs={{0,1},{1,0},{2,3},{3,2},{4,5},{5,4},{6,7},{7,6},{8,9},{9,8},{10,11... | collective-permute-start | bytes 786440 | tf_op jit(solution)/shard_map/ppermute | solution.py:41
  106.4 9.5 %collective-permute-start.17 = (f32[256,128]{1,0:T(8,128)S(1)}, f32[256,128]{1,0:T(8,128)S(1)}, u32[]{:S(2)}, u32[]{:S(2)}) collective-permute-start(f32[256,128]{1,0:T(8,128)S(1)} %slice.44), channel_id=1, source_target_pairs={{0,2},{1,3},{2,4},{3,5},{4,6},{5,7},{6,0},{7,1},{8,10},{9,11},{10,... | collective-permute-start | bytes 393224 | tf_op jit(solution)/shard_map/ppermute | solution.py:41
  106.8 9.9 %collective-permute-start.18 = (f32[256,128]{1,0:T(8,128)S(1)}, f32[256,128]{1,0:T(8,128)S(1)}, u32[]{:S(2)}, u32[]{:S(2)}) collective-permute-start(f32[256,128]{1,0:T(8,128)S(1)} %slice.45), channel_id=1, source_target_pairs={{0,6},{1,7},{2,0},{3,1},{4,2},{5,3},{6,4},{7,5},{8,14},{9,15},{10,... | collective-permute-start | bytes 393224 | tf_op jit(solution)/shard_map/ppermute | solution.py:41
  110.4 7.4 %collective-permute-start.16 = (f32[512,128]{1,0:T(8,128)S(1)}, f32[512,128]{1,0:T(8,128)S(1)}, u32[]{:S(2)}, u32[]{:S(2)}) collective-permute-start(f32[512,128]{1,0:T(8,128)S(1)} %collective-permute-done.13.refs_2_), channel_id=1, source_target_pairs={{0,1},{1,0},{2,3},{3,2},{4,5},{5,4},{6,7},{7,6},{8,9},{9,8},{10,11... | collective-permute-start | bytes 786440 | tf_op jit(solution)/shard_map/ppermute | solution.py:41
  113.2 4.6 %collective-permute-start.15 = (f32[512,128]{1,0:T(8,128)S(1)}, f32[512,128]{1,0:T(8,128)S(1)}, u32[]{:S(2)}, u32[]{:S(2)}) collective-permute-start(f32[512,128]{1,0:T(8,128)S(1)} %collective-permute-done.12.refs_1_), channel_id=1, source_target_pairs={{0,1},{1,0},{2,3},{3,2},{4,5},{5,4},{6,7},{7,6},{8,9},{9,8},{10,11... | collective-permute-start | bytes 786440 | tf_op jit(solution)/shard_map/ppermute | solution.py:41
  115.9 1.3 %collective-permute-start.26 = (f32[128,128]{1,0:T(8,128)S(1)}, f32[128,128]{1,0:T(8,128)S(1)}, u32[]{:S(2)}, u32[]{:S(2)}) collective-permute-start(f32[128,128]{1,0:T(8,128)S(1)} %add_add_fusion.1), channel_id=1, source_target_pairs={{0,1},{1,0},{2,3},{3,2},{4,5},{5,4},{6,7},{7,6},{8,9},{9,8},{10,11... | collective-permute-start | bytes 196616 | tf_op jit(solution)/shard_map/ppermute | solution.py:41
  116.7 3.0 %collective-permute-start.19 = (f32[512,128]{1,0:T(8,128)S(1)}, f32[512,128]{1,0:T(8,128)S(1)}, u32[]{:S(2)}, u32[]{:S(2)}) collective-permute-start(f32[512,128]{1,0:T(8,128)S(1)} %constant_dynamic-update-slice_fusion.refs_1_), channel_id=1, source_target_pairs={{0,1},{1,0},{2,3},{3,2},{4,5},{5,4},{6,7},{7,6},{8,9},{9,8},{10,11... | collective-permute-start | bytes 786440 | tf_op jit(solution)/shard_map/ppermute | solution.py:41

commit v2 on v1

--- a/solution.py
+++ b/solution.py
@@ -17,6 +17,7 @@
 DIRECT_VMEM = 12 * 2**20
 CHUNK_VMEM = 24 * 2**20
 SMALL_VMEM = 8 * 2**20
+CHOOSE_VMEM = 60 * 2**20
 
 
 def split(x):
@@ -44,30 +45,33 @@
 def choose(grouped, which):
     blocks, _, width, _ = grouped.shape
 
-    def body(which_ref, source, target):
-        target[...] = source[...]
+    def body(which_ref, source, target, sem):
+        copy = pltpu.make_async_copy(source.at[:, which_ref[0]], target, sem)
+        copy.start()
+        copy.wait()
 
     return pl.pallas_call(
         body,
         grid_spec=pltpu.PrefetchScalarGridSpec(
             num_scalar_prefetch=1,
             grid=(1,),
-            in_specs=[pl.BlockSpec((blocks, None, width, width), lambda i, which: (0, which[0], 0, 0))],
-            out_specs=pl.BlockSpec((blocks, width, width), lambda i, which: (0, 0, 0)),
+            in_specs=[pl.BlockSpec(memory_space=pl.ANY)],
+            out_specs=pl.BlockSpec(memory_space=pltpu.VMEM),
+            scratch_shapes=[pltpu.SemaphoreType.DMA],
         ),
         out_shape=jax.ShapeDtypeStruct((blocks, width, width), F32),
-        compiler_params=pltpu.CompilerParams(vmem_limit_bytes=SMALL_VMEM),
+        compiler_params=pltpu.CompilerParams(vmem_limit_bytes=CHOOSE_VMEM),
         name="choose",
     )(which, grouped)
 
 
-def flip_body(plan, n_parts, me_ref, ids_ref, s_ref, l_ref, d_ref, *refs):
-    outs, (inv_ref, high_ref, low_ref, acc, turned, buf, sems) = refs[:n_parts], refs[n_parts:]
+def flip_body(plan, n_parts, me_ref, ids_ref, s_ref, l_ref, *refs):
+    outs, (high_ref, low_ref, acc, turned, buf, sems) = refs[:n_parts], refs[n_parts:]
     step, n_steps, slot = pl.program_id(0), plan.n_chunks, pl.program_id(0) % 2
     n_blocks, rows, width = plan.n_blocks, plan.chunk_rows, plan.width
 
     def fetch(i, slot):
-        qb, h, qs = plan.chunk_at(ids_ref[plan.flip_place(i)])
+        qb, h, qs = plan.chunk_at(ids_ref[plan.n_chunks + i])
         target = buf.at[slot]
         if plan.pitch > n_blocks:
             target = target.at[:, :, pl.ds(0, n_blocks), :]
@@ -77,16 +81,10 @@
     def _():
         fetch(0, 0).start()
         acc[...] = jnp.zeros_like(acc)
-        inv_ref[...] = inverse_start(d_ref[...])
 
     @pl.when(step + 1 < n_steps)
     def _():
         fetch(step + 1, 1 - slot).start()
-
-    inv = inv_ref[...]
-    for level in range(plan.levels_per_step):
-        inv = inverse_level(d_ref[...], inv, step * plan.levels_per_step + level)
-    inv_ref[...] = inv
 
     l_high, l_low = split(l_ref[...].reshape(rows, width))
     left = jnp.concatenate([l_high, l_low], 1).T
@@ -115,7 +113,7 @@
             out[...] = turned[pl.ds(start, size), :]
 
 
-def flip_parts(plan, trail, panel, diag_block, ids, me, n_row):
+def flip_parts(plan, trail, panel, ids, me, n_row):
     width, n_blocks = plan.width, plan.n_blocks
     size = n_blocks * width // n_row
     kept = plan.keep * plan.chunk_rows
@@ -128,10 +126,9 @@
         buffer = pltpu.VMEM((2, n_sub, rows * n_blocks, width), F32)
 
     def l_index(i, me, ids):
-        b, h, s = plan.chunk_at(ids[plan.flip_place(i)])
+        b, h, s = plan.chunk_at(ids[plan.n_chunks + i])
         return (b, 0, h, s, 0, 0)
 
-    square = pl.BlockSpec((width, width), lambda i, me, ids: (0, 0))
     whole = pl.BlockSpec(memory_space=pltpu.VMEM)
     resident = pltpu.VMEM((kept, n_blocks * width), BF16)
     n = plan.n_chunks * plan.chunk_rows
@@ -143,9 +140,8 @@
             in_specs=[
                 pl.BlockSpec(memory_space=pl.ANY),
                 pl.BlockSpec((None, n_sub, None, None, rows, width), l_index),
-                square,
             ],
-            out_specs=[pl.BlockSpec((size, width), lambda i, me, ids: (0, 0))] * n_row + [square, whole, whole],
+            out_specs=[pl.BlockSpec((size, width), lambda i, me, ids: (0, 0))] * n_row + [whole, whole],
             scratch_shapes=[
                 pltpu.VMEM((width, n_blocks * width), F32),
                 pltpu.VMEM((n_blocks * width, width), F32),
@@ -154,29 +150,14 @@
             ],
         ),
         out_shape=[jax.ShapeDtypeStruct((size, width), F32)] * n_row
-        + [jax.ShapeDtypeStruct((width, width), F32), resident, resident],
+        + [resident, resident],
         compiler_params=pltpu.CompilerParams(vmem_limit_bytes=FLIP_VMEM),
         cost_estimate=pl.CostEstimate(
             flops=6 * n * n_blocks * width * width, bytes_accessed=4 * n * n_blocks * width, transcendentals=0
         ),
         name="flip",
-    )(me, ids, source, panel.reshape(*plan.view, width), diag_block)
-    return out[:n_row], out[n_row], out[n_row + 1], out[n_row + 2]
-
-
-def inverse_start(d):
-    i = lax.broadcasted_iota(jnp.int32, d.shape, 0)
-    j = lax.broadcasted_iota(jnp.int32, d.shape, 1)
-    return jnp.where(i == j, 1.0 / d, 0.0)
-
-
-def inverse_level(d, inv, level):
-    i = lax.broadcasted_iota(jnp.int32, d.shape, 0)
-    j = lax.broadcasted_iota(jnp.int32, d.shape, 1)
-    same = (i >> (level + 1)) == (j >> (level + 1))
-    below = (i >> level) > (j >> level)
-    part = jnp.where(jnp.logical_and(same, below), d, 0.0)
-    return inv - full_dot(inv, full_dot(part, inv))
+    )(me, ids, source, panel.reshape(*plan.view, width))
+    return out[:n_row], out[n_row], out[n_row + 1]
 
 
 def direct_body(n_blocks, group, half, ids_ref, s_ref, p_ref, away_ref, keep_ref, right):
@@ -243,11 +224,7 @@
         ),
         out_shape=[out, out],
         compiler_params=pltpu.CompilerParams(vmem_limit_bytes=CHUNK_VMEM),
-        cost_estimate=pl.CostEstimate(
-            flops=12 * half * chunk_rows * n_blocks * width * width,
-            bytes_accessed=8 * half * chunk_rows * n_blocks * width,
-            transcendentals=0,
-        ),
+        cost_estimate=pl.CostEstimate(flops=1, bytes_accessed=1, transcendentals=0),
         name="direct",
     )(ids, chunked, col_panel)
 
@@ -291,11 +268,94 @@
         out_shape=[out, out],
         scratch_shapes=[pltpu.VMEM((depth, 2 * width), BF16)],
         compiler_params=pltpu.CompilerParams(vmem_limit_bytes=DIRECT_VMEM),
-        cost_estimate=pl.CostEstimate(
-            flops=12 * half * rows * depth * width, bytes_accessed=8 * half * rows * width, transcendentals=0
-        ),
+        cost_estimate=pl.CostEstimate(flops=1, bytes_accessed=1, transcendentals=0),
         name="direct_kept",
     )(high, low, col_panel)
+
+
+def inverse_body(d_ref, o_ref):
+    d = d_ref[...]
+    width = d.shape[0]
+    i = lax.broadcasted_iota(jnp.int32, d.shape, 0)
+    j = lax.broadcasted_iota(jnp.int32, d.shape, 1)
+    inv = jnp.where(i == j, 1.0 / d, 0.0)
+    level = 0
+    while (1 << level) < width:
+        same = (i >> (level + 1)) == (j >> (level + 1))
+        below = (i >> level) > (j >> level)
+        part = jnp.where(jnp.logical_and(same, below), d, 0.0)
+        inv = inv - full_dot(inv, full_dot(part, inv))
+        level += 1
+    o_ref[...] = inv
+
+
+def inverse(diag_block):
+    return pl.pallas_call(
+        inverse_body,
+        out_shape=jax.ShapeDtypeStruct(diag_block.shape, F32),
+        compiler_params=pltpu.CompilerParams(vmem_limit_bytes=SMALL_VMEM),
+        name="inverse",
+    )(diag_block)
+
+
+def over_rows(a, b, **kwargs):
+    return lax.dot_general(a, b, (((0,), (0,)), ((), ())), preferred_element_type=F32, **kwargs)
+
+
+def moment_body(n_parts, ids_ref, me_ref, *refs):
+    parts, (p_ref, b_ref, l_ref, out_ref) = refs[:n_parts], refs[n_parts:]
+    size, width = parts[0].shape
+    product = jnp.zeros((width, width), F32)
+    for k, part in enumerate(parts):
+        start = pl.multiple_of((me_ref[0] ^ k) * size, size)
+        p_high, p_low = split(p_ref[pl.ds(start, size), :])
+        f_high, f_low = split(part[...])
+        product += over_rows(p_high, f_high) + over_rows(p_high, f_low) + over_rows(p_low, f_high)
+    b = b_ref[...].reshape(-1, width)
+    l = l_ref[...].reshape(-1, width)
+    out_ref[...] = over_rows(b, l, precision=HIGHEST) - product - product.T
+
+
+def moment(plan, parts, col_panel, given, panel, ids, me):
+    _, n_sub, _, _, rows = plan.view
+    width = plan.width
+
+    def at(i, ids, me):
+        b, h, s = plan.chunk_at(ids[plan.mine])
+        return (b, 0, h, s, 0, 0)
+
+    def whole(shape):
+        return pl.BlockSpec(shape, lambda i, ids, me: (0, 0))
+
+    chunk = pl.BlockSpec((None, n_sub, None, None, rows, width), at)
+    return pl.pallas_call(
+        functools.partial(moment_body, len(parts)),
+        grid_spec=pltpu.PrefetchScalarGridSpec(
+            num_scalar_prefetch=2,
+            grid=(1,),
+            in_specs=[whole(x.shape) for x in parts] + [whole(col_panel.shape), chunk, chunk],
+            out_specs=whole((width, width)),
+        ),
+        out_shape=jax.ShapeDtypeStruct((width, width), F32),
+        compiler_params=pltpu.CompilerParams(vmem_limit_bytes=DIRECT_VMEM),
+        name="moment",
+    )(ids, me, *parts, col_panel, given.reshape(*plan.view, width), panel.reshape(*plan.view, width))
+
+
+def gram_body(inv_ref, moment_ref, g_ref):
+    g = -over_rows(inv_ref[...], moment_ref[...], precision=HIGHEST)
+    i = lax.broadcasted_iota(jnp.int32, g.shape, 0)
+    j = lax.broadcasted_iota(jnp.int32, g.shape, 1)
+    g_ref[...] = jnp.where(i >= j, g, 0.0)
+
+
+def gram_of(inv, total):
+    return pl.pallas_call(
+        gram_body,
+        out_shape=jax.ShapeDtypeStruct(inv.shape, F32),
+        compiler_params=pltpu.CompilerParams(vmem_limit_bytes=SMALL_VMEM),
+        name="gram",
+    )(inv, total)
 
 
 def solve_body(n_terms, ids_ref, *refs):
@@ -307,18 +367,11 @@
     x_ref[...] = full_dot(total, inv_ref[...])
 
 
-def gram_body(ids_ref, x_ref, l_ref, g_ref):
-    x = x_ref[...]
-    g_ref[...] = -lax.dot_general(
-        x, l_ref[...].reshape(x.shape), (((0,), (0,)), ((), ())), precision=HIGHEST, preferred_element_type=F32
-    )
-
-
 def on_my_chunk(plan, body, ids, inputs, laid_out, out_shape, name):
     _, n_sub, _, _, rows = plan.view
 
     def at(i, ids):
-        b, h, s = plan.chunk_at(ids[plan.n_chunks - 1])
+        b, h, s = plan.chunk_at(ids[plan.mine])
         return (b, 0, h, s, 0, 0)
 
     def whole(shape):
@@ -344,36 +397,40 @@
     pieces = refs[1:-2] if has_base else refs[:-2]
     _, n_sub, _, _, rows = plan.view
     copies = []
-    for k, (piece, slot) in enumerate(zip(pieces, slots)):
-        b, h, s = plan.chunk_at(ids_ref[slot[0]])
+    for piece, (slot, half) in zip(pieces, slots):
+        b, h, s = plan.chunk_at(ids_ref[slot])
+        first, count = half * piece.shape[0], piece.shape[0]
         for i in range(n_sub):
-            source = piece.at[pl.ds(i * rows, rows), :]
-            copies.append(pltpu.make_async_copy(source, out_ref.at[b, i, h, s], sems.at[k, i]))
+            low, high = max(first, i * rows), min(first + count, (i + 1) * rows)
+            if low < high:
+                source = piece.at[pl.ds(low - first, high - low), :]
+                target = out_ref.at[b, i, h, s, pl.ds(low - i * rows, high - low), :]
+                copies.append(pltpu.make_async_copy(source, target, sems.at[len(copies)]))
     for copy in copies:
         copy.start()
     for copy in copies:
         copy.wait()
 
 
-def place(plan, base, pieces, slots, ids):
-    _, n_sub, _, _, _ = plan.view
+def place(plan, base, pieces, ids):
     anywhere = pl.BlockSpec(memory_space=pl.ANY)
     held = pl.BlockSpec(memory_space=pltpu.VMEM)
     bases = [] if base is None else [base]
-    return pl.pallas_call(
-        functools.partial(place_body, plan, [(slot,) for slot in slots], base is not None),
+    count = len(pieces) * (plan.view[1] + 1)
+    return pl.pallas_call(
+        functools.partial(place_body, plan, [piece[1:] for piece in pieces], base is not None),
         grid_spec=pltpu.PrefetchScalarGridSpec(
             num_scalar_prefetch=1,
             grid=(1,),
             in_specs=[anywhere] * len(bases) + [held] * len(pieces),
             out_specs=anywhere,
-            scratch_shapes=[pltpu.SemaphoreType.DMA((len(pieces), n_sub))],
+            scratch_shapes=[pltpu.SemaphoreType.DMA((count,))],
         ),
         out_shape=jax.ShapeDtypeStruct((*plan.view, plan.width), F32),
         input_output_aliases={1: 0} if bases else {},
         compiler_params=pltpu.CompilerParams(vmem_limit_bytes=SMALL_VMEM),
         name="place",
-    )(ids, *bases, *pieces)
+    )(ids, *bases, *[piece[0] for piece in pieces])
 
 
 class Plan:
@@ -395,19 +452,23 @@
             here = sorted({distance % n_z, -distance % n_z})
             self.steps.append((len(self.offsets), here))
             self.offsets += here + here
+            if distance == 0:
+                self.mine = len(self.offsets) - 1
             self.twins += [1] * len(here) + [0] * len(here)
         fits = KEEP_BYTES // (4 * self.chunk_rows * col_blocks * width)
-        ends = [begin + 2 * len(here) for begin, here in self.steps]
-        self.keep = max([end for end in ends if end <= fits], default=ends[0])
+        self.slots, held = {}, []
+        for begin, here in sorted(self.steps, key=lambda step: step[1][0] == 0):
+            places = range(begin, begin + 2 * len(here))
+            if len(held) + len(places) <= fits:
+                self.slots[begin] = len(held)
+                held += places
+        self.keep = len(held)
         self.skip = self.n_chunks - self.keep
-        self.levels_per_step = -(-(width - 1).bit_length() // self.n_chunks)
+        self.flip_order = [p for p in range(self.n_chunks) if p not in held] + held
 
     def chunk_at(self, chunk):
         h, q = chunk // self.n_row, chunk % self.n_row
         return q // self.qs, h, q % self.qs
-
-    def flip_place(self, i):
-        return (i + self.keep) % self.n_chunks
 
 
 def per_device(trail_adjoint, panel, panel_adjoint, diag_block):
@@ -426,7 +487,10 @@
     up = lambda r, c: (r, (c + 2) % n_col)
     down = lambda r, c: (r, (c - 2) % n_col)
     twin = lambda r, c: (r, c ^ 1)
-    ids = (z + jnp.array(plan.offsets, jnp.int32)) % n_z * 2 + (core ^ jnp.array(plan.twins, jnp.int32))
+    places = list(range(plan.n_chunks)) + plan.flip_order
+    offsets = jnp.array([plan.offsets[p] for p in places], jnp.int32)
+    twins = jnp.array([plan.twins[p] for p in places], jnp.int32)
+    ids = (z + offsets) % n_z * 2 + (core ^ twins)
 
     def to_panel_user(r, c):
         h, s = divmod(c, n_row)
@@ -435,63 +499,84 @@
     chosen = choose(panel.reshape(col_blocks, ratio, width, width), (col_index // n_row).reshape(1))
     col_panel = move(chosen.reshape(col_blocks * width, width), to_panel_user)
 
-    parts, inv, high, low = flip_parts(plan, trail_adjoint, panel, diag_block, ids, row_index.reshape(1), n_row)
-    flipped = parts[0]
-    for k in range(1, n_row):
-        flipped = flipped + move(parts[k], lambda r, c: (r ^ k, c))
-    flipped = move(flipped, lambda r, c: (c % n_row, c // n_row * n_row + r))
+    me = row_index.reshape(1)
+    parts, high, low = flip_parts(plan, trail_adjoint, panel, ids, me, n_row)
+    arrived = [move(parts[k], lambda r, c: (r ^ k, c)) for k in range(1, n_row)]
+    flip_sum = sum(arrived, parts[0])
+    flipped = move(flip_sum, lambda r, c: (c % n_row, c // n_row * n_row + r))
+    inv = inverse(diag_block)
+
+    moments = [moment(plan, parts, col_panel, panel_adjoint, panel, ids, me)]
+    bit = 1
+    while bit < n_row:
+        moments.append(moments[-1] + move(moments[-1], lambda r, c: (r ^ bit, c)))
+        bit *= 2
+    row_steps = len(moments) - 1
 
     rows = plan.chunk_rows
     cut = rows // 2
-    below, above, mine, after = None, None, None, None
+    below, above = None, None
     for begin, here in plan.steps:
-        right, _ = lax.optimization_barrier((col_panel, after))
-        if begin + 2 * len(here) <= plan.keep:
-            away, keep = direct_kept(plan, high, low, right, begin, len(here))
+        if here[0] == 0:
+            fence = totals
+        elif begin:
+            fence = (keep, below, above, flip_sum)
+        else:
+            fence = inv
+        right, _ = lax.optimization_barrier((col_panel, fence))
+        if begin in plan.slots:
+            away, keep = direct_kept(plan, high, low, right, plan.slots[begin], len(here))
         else:
             chunked = trail_adjoint.reshape(*plan.view[:4], plan.view[4] * col_blocks, width)
             away, keep = direct_chunks(chunked, right, ids, begin, len(here), plan.chunk_at)
-        after = total = keep + move(away, twin)
+        totals = []
+        for k in range(len(here)):
+            piece = slice(k * rows, (k + 1) * rows)
+            totals.append(keep[piece] + move(away[piece], twin))
         if here[0] == 0:
-            mine = [total, below, above, flipped]
+            own = totals[0]
         elif len(here) == 1:
-            below, above = move(total[:cut], up), move(total[cut:], down)
+            below, above = move(totals[0][:cut], up), move(totals[0][cut:], down)
         else:
-            first, second = total[:rows], total[rows:]
+            first, second = totals
             if below.shape[0] == cut:
                 first = jnp.concatenate([first[:cut] + below, first[cut:]], 0)
                 second = jnp.concatenate([second[:cut], second[cut:] + above], 0)
             else:
                 first, second = first + below, second + above
             below, above = move(first, up), move(second, down)
-
+    mine = [own, below, above, flipped]
+
+    bit = 1
+    while bit < n_z:
+        moments.append(moments[-1] + move(moments[-1], lambda r, c: (r, c ^ (2 * bit))))
+        bit *= 2
     x = on_my_chunk(
         plan, functools.partial(solve_body, len(mine)), ids, mine + [inv], panel_adjoint, (rows, width), "solve"
     )
 
-    held = {0: x}
-    below, above = x, x
+    lower, upper = {0: x[:cut]}, {0: x[cut:]}
+    below, above = (x[:cut], x[cut:]), (x[cut:], x[:cut])
     for distance in range(1, plan.far):
-        below, above = move(below, up), move(above, down)
-        held[-distance % n_z], held[distance] = below, above
-    gram = on_my_chunk(plan, gram_body, ids, [x], panel, (width, width), "gram")
-    gram = gram + sum(move(gram, lambda r, c: (r ^ k, c)) for k in range(1, n_row))
-    other = {d: move(piece, twin) for d, piece in held.items()}
-    halves = [move(below[:cut], up), move(above[cut:], down)]
-    moving, total = gram, gram
-    for _ in range(1, n_z):
-        moving = move(moving, up)
-        total = total + moving
+        below, above = [move(b, up) for b in below], [move(a, down) for a in above]
+        lower[-distance % n_z], upper[-distance % n_z] = below
+        upper[distance], lower[distance] = above
+    (go_up, go_down), _ = lax.optimization_barrier(((below[0], above[0]), moments[row_steps]))
+    lower[plan.far], upper[plan.far] = move(go_up, up), move(go_down, down)
     order = (z + jnp.arange(n_z, dtype=jnp.int32)) % n_z * 2
     place_ids = jnp.concatenate([order + core, order + (1 - core)])
-    near = sorted(held)
-    solved = place(
-        plan, None, [held[d] for d in near] + [other[d] for d in near], near + [n_z + d for d in near], place_ids
+    near = [d for d in range(n_z) if d != plan.far]
+    pieces = [(lower[d], d, 0) for d in near] + [(upper[d], d, 1) for d in near]
+    pieces += [(move(piece, twin), n_z + d, half) for piece, d, half in pieces]
+    solved = place(plan, None, pieces, place_ids)
+    gram = gram_of(inv, moments[-1] + move(moments[-1], twin))
+    (lower[plan.far], upper[plan.far]), (solved, gram) = lax.optimization_barrier(
+        ((lower[plan.far], upper[plan.far]), (solved, gram))
     )
-    last = jnp.concatenate(halves, 0)
-    solved = place(plan, solved, [last, move(last, twin)], [plan.far, n_z + plan.far], place_ids)
-    gram = total + move(total, twin)
-    return (solved.reshape(row_blocks, width, width), jnp.tril(gram))
+    last = [(lower[plan.far], plan.far, 0), (upper[plan.far], plan.far, 1)]
+    last += [(move(piece, twin), n_z + d, half) for piece, d, half in last]
+    solved = place(plan, solved, last, place_ids)
+    return solved.reshape(row_blocks, width, width), gram
 
 
 def solution(mesh):

time: 121 us -> 111 us (0.917)
  waiting for transfers between devices: 43.4 us -> 30.4 us
  Pallas kernels: 41.5 us -> 45.8 us
  local copies, waits for them, and re-layouts: 1.67 us -> 0.1 us
    ppermute x27 -> x32, waiting for transfers between devices: 43.4 us -> 30.4 us  [send(): return lax.ppermute(x, AXES, pairs)]
    pallas_call x2 -> x5, Pallas kernels: 3.28 us -> 9.08 us  [the longest x2 3.7 us: place(): pl.pallas_call(functools.partial(place_body, plan, [piece[1:] for piece i...]
    pallas_call x1, Pallas kernels: 20.7 us -> 18.9 us  [flip_parts(): pl.pallas_call(functools.partial(flip_body, plan, n_row), grid_spec=pltpu...]
    unnamed x13 -> x10, local copies, waits for them, and re-layouts: 1.62 us -> 0.03 us
    pallas_call x1, Pallas kernels: 1.04 us -> 2.36 us  [choose(): pl.pallas_call(body, grid_spec=pltpu.PrefetchScalarGridSpec(num_scalar_pr...]
    ppermute x27 -> x32, starting transfers between devices: 32.6 us -> 32.7 us  [send(): return lax.ppermute(x, AXES, pairs)]
  transfers between devices with their start and end apart: 27 -> 32, of which waited for: 14 -> 15; matrix products, arithmetic and copies ran while one was open for 1% -> 0% of each run, Pallas kernels for 24% -> 31%
where the time goes in v2:
time: 111 us; the launch traced here: 110 us
  Pallas kernels  45.8 us (41%)
  starting transfers between devices  32.7 us (29%)
  waiting for transfers between devices  30.4 us (27%)
    ppermute x32, starting transfers between devices, send(): return lax.ppermute(x, AXES, pairs)  32.7 us
    ppermute x32, waiting for transfers between devices, send(): return lax.ppermute(x, AXES, pairs)  30.4 us
    pallas_call x1, Pallas kernels, flip_parts(): pl.pallas_call(functools.partial(flip_body, plan, n_row), grid_spec=pltpu...  18.9 us
    pallas_call x2, Pallas kernels, direct_kept(): pl.pallas_call(functools.partial(kept_body, first, half), grid=(2 * half,...  8.19 us
    pallas_call x1, Pallas kernels, direct_chunks(): pl.pallas_call(functools.partial(direct_body, n_blocks, group, half), gri...  6.29 us
    pallas_call x2, Pallas kernels, place(): pl.pallas_call(functools.partial(place_body, plan, [piece[1:] for piece i...  3.7 us
    pallas_call x1, Pallas kernels, inverse(): pl.pallas_call(inverse_body, out_shape=jax.ShapeDtypeStruct(diag_block.sh...  3.09 us
    pallas_call x1, Pallas kernels, choose(): pl.pallas_call(body, grid_spec=pltpu.PrefetchScalarGridSpec(num_scalar_pr...  2.36 us
  transfers between devices with their start and end apart: 32, of which 15 were waited for; matrix products, arithmetic and copies ran while one was open for 0% of the time, Pallas kernels for 31%

profile of v2, /device:TPU:0, one launch (start us, length us, event | category | flops | bytes accessed | tf_op | source)
XLA Modules:
  0.0 110.3 jit_solution(18146244299827918575)
XLA Ops:
  0.7 2.4 %choose.1 = f32[16,128,128]{2,1,0:T(8,128)} custom-call(s32[1]{0:T(128)} %bitcast.1.which_ref, f32[16,2,128,128]{3,2,1,0:T(8,128)} %bitcast.9), custom_call_target="tpu_custom_call" | custom-call | tf_op jit(solution)/shard_map/choose/pallas_call | solution.py:53
  3.1 3.0 %collective-permute-start = (f32[2048,128]{1,0:T(8,128)}, f32[2048,128]{1,0:T(8,128)S(1)}, u32[]{:S(2)}, u32[]{:S(2)}) collective-permute-start(f32[2048,128]{1,0:T(8,128)} %bitcast.17), channel_id=1, source_target_pairs={{0,8},{1,16},{2,24},{3,0},{4,12},{5,20},{6,28},{7,4},{8,25},{9,1},... | collective-permute-start | bytes 3145736 | tf_op jit(solution)/shard_map/ppermute | solution.py:42
  6.1 3.1 %inverse.1.refs_4_.inv_ref = f32[128,128]{1,0:T(8,128)S(1)} custom-call(f32[128,128]{1,0:T(8,128)S(1)} %copy-done.2), custom_call_target="tpu_custom_call" | custom-call | tf_op jit(solution)/shard_map/inverse/pallas_call | solution.py:293
  9.2 18.9 %flip.1 = (f32[512,128]{1,0:T(8,128)S(1)}, f32[512,128]{1,0:T(8,128)S(1)}, f32[512,128]{1,0:T(8,128)S(1)}, f32[512,128]{1,0:T(8,128)S(1)}, bf16[3072,2048]{1,0:T...) custom-call(s32[1]{0:T(128)} %bitcast.4.me_ref, s32[16]{0:T(128)S(1)} %fusion.2.ids_ref, ...), custom_call_target="tpu_custom_call" | custom-call | flops 6442450944 | bytes 33554432 | tf_op jit(solution)/shard_map/flip/pallas_call | solution.py:135
  28.2 1.8 %collective-permute-done.p_ref.refs_4_ = f32[2048,128]{1,0:T(8,128)S(1)} collective-permute-done((f32[2048,128]{1,0:T(8,128)}, f32[2048,128]{1,0:T(8,128)S(1)}, u32[]{:S(2)}, u32[]{:S(2)}) %collective-permute-start) | collective-permute-done | bytes 1048608 | tf_op jit(solution)/shard_map/ppermute | solution.py:42
  29.9 2.8 %direct_kept.2 = (f32[512,128]{1,0:T(8,128)S(1)}, f32[512,128]{1,0:T(8,128)S(1)}) custom-call(bf16[3072,2048]{1,0:T(8,128)(2,1)S(1)} %get-tuple-element.23.high_ref, bf16[3072,2048]{1,0:T(8,128)(2,1)S(1)} %get-tuple-element.24.low_ref, f32[2048,128]{1,0:T(8,128)S(1)} %collective-permute-done.p_ref.refs_4_), custom_call_target="tpu_custom_call" | custom-call | flops 1 | bytes 1 | tf_op jit(solution)/shard_map/direct_kept/pallas_call | solution.py:260
  32.8 2.4 %collective-permute-start.4 = (f32[512,128]{1,0:T(8,128)S(1)}, f32[512,128]{1,0:T(8,128)S(1)}, u32[]{:S(2)}, u32[]{:S(2)}) collective-permute-start(f32[512,128]{1,0:T(8,128)S(1)} %get-tuple-element.29.refs_1_), channel_id=1, source_target_pairs={{0,8},{1,9},{2,10},{3,11},{4,12},{5,13},{6,14},{7,15},{8,0},{9,1},... | collective-permute-start | bytes 786440 | tf_op jit(solution)/shard_map/ppermute | solution.py:42
  35.2 0.7 collective-permute-start.5
  35.9 1.0 collective-permute-start.6
  37.0 4.0 %collective-permute-start.3 = (f32[256,128]{1,0:T(8,128)S(1)}, f32[256,128]{1,0:T(8,128)S(1)}, u32[]{:S(2)}, u32[]{:S(2)}) collective-permute-start(f32[256,128]{1,0:T(8,128)S(1)} %get-tuple-element.54), channel_id=1, source_target_pairs={{0,6},{1,7},{2,0},{3,1},{4,2},{5,3},{6,4},{7,5},{8,14},{9,15},{10,... | collective-permute-start | bytes 393224 | tf_op jit(solution)/shard_map/ppermute | solution.py:42
  41.0 1.4 %collective-permute-done.4 = f32[512,128]{1,0:T(8,128)S(1)} collective-permute-done((f32[512,128]{1,0:T(8,128)S(1)}, f32[512,128]{1,0:T(8,128)S(1)}, u32[]{:S(2)}, u32[]{:S(2)}) %collective-permute-start.4) | collective-permute-done | bytes 262176 | tf_op jit(solution)/shard_map/ppermute | solution.py:42
  42.4 6.8 %collective-permute-done.5 = f32[512,128]{1,0:T(8,128)S(1)} collective-permute-done((f32[512,128]{1,0:T(8,128)S(1)}, f32[512,128]{1,0:T(8,128)S(1)}, u32[]{:S(2)}, u32[]{:S(2)}) %collective-permute-start.5) | collective-permute-done | bytes 262176 | tf_op jit(solution)/shard_map/ppermute | solution.py:42
  49.3 5.4 %direct_kept.3 = (f32[1024,128]{1,0:T(8,128)S(1)}, f32[1024,128]{1,0:T(8,128)S(1)}) custom-call(bf16[3072,2048]{1,0:T(8,128)(2,1)S(1)} %get-tuple-element.23.high_ref, bf16[3072,2048]{1,0:T(8,128)(2,1)S(1)} %get-tuple-element.24.low_ref, f32[2048,128]{1,0:T(8,128)S(1)} %collective-permute-done.p_ref.refs_4_), custom_call_target="tpu_custom_call" | custom-call | flops 1 | bytes 1 | tf_op jit(solution)/shard_map/direct_kept/pallas_call | solution.py:260
  54.8 0.5 collective-permute-start.7
  55.3 0.7 collective-permute-start.12
  56.0 0.4 collective-permute-done.8
  56.4 0.4 collective-permute-done.7
  56.9 5.0 %collective-permute-start.11 = (f32[512,128]{1,0:T(8,128)S(1)}, f32[512,128]{1,0:T(8,128)S(1)}, u32[]{:S(2)}, u32[]{:S(2)}) collective-permute-start(f32[512,128]{1,0:T(8,128)S(1)} %pad_maximum_fusion.1), channel_id=1, source_target_pairs={{0,6},{1,7},{2,0},{3,1},{4,2},{5,3},{6,4},{7,5},{8,14},{9,15},{10,... | collective-permute-start | bytes 786440 | tf_op jit(solution)/shard_map/ppermute | solution.py:42
  61.9 6.3 %direct.1 = (f32[512,128]{1,0:T(8,128)S(1)}, f32[512,128]{1,0:T(8,128)S(1)}) custom-call(s32[16]{0:T(128)S(1)} %fusion.2.ids_ref, f32[4,4,2,1,2048,128]{5,4,3,2,1,0:T(8,128)} %bitcast.15, f32[2048,128]{1,0:T(8,128)S(1)} %collective-permute-done.p_ref.refs_4_), custom_call_target="tpu_custom_call" | custom-call | flops 1 | bytes 1 | tf_op jit(solution)/shard_map/direct/pallas_call | solution.py:210
  68.2 0.2 collective-permute-start.9
  68.5 1.4 %moment.1 = f32[128,128]{1,0:T(8,128)S(1)} custom-call(s32[16]{0:T(128)S(1)} %fusion.2.ids_ref, s32[1]{0:T(128)} %bitcast.4.me_ref, f32[512,128]{1,0:T(8,128)S(1)} %get-tuple-element.28.refs_0_, f32[512,128]{1,0:T(8,128)S(1)} %get-tuple-element.29.refs_1_, f32[512,128]{1,0:T(8,128)S(1)} %get-tuple-element.30.refs_2_, ...), custom_call_target="tpu_custom_call" | custom-call | tf_op jit(solution)/shard_map/moment/pallas_call | solution.py:331
  70.0 1.1 collective-permute-start.15
  71.0 3.3 %collective-permute-done.15 = f32[128,128]{1,0:T(8,128)S(1)} collective-permute-done((f32[128,128]{1,0:T(8,128)S(1)}, f32[128,128]{1,0:T(8,128)S(1)}, u32[]{:S(2)}, u32[]{:S(2)}) %collective-permute-start.15) | collective-permute-done | bytes 65568 | tf_op jit(solution)/shard_map/ppermute | solution.py:42
  74.4 1.0 collective-permute-start.16
  75.4 3.3 %collective-permute-done.16 = f32[128,128]{1,0:T(8,128)S(1)} collective-permute-done((f32[128,128]{1,0:T(8,128)S(1)}, f32[128,128]{1,0:T(8,128)S(1)}, u32[]{:S(2)}, u32[]{:S(2)}) %collective-permute-start.16) | collective-permute-done | bytes 65568 | tf_op jit(solution)/shard_map/ppermute | solution.py:42
  78.7 0.3 collective-permute-start.27
  79.1 0.7 collective-permute-done.10.refs_1_
  79.8 0.9 solve.1
  80.8 1.1 %collective-permute-start.20 = (f32[256,128]{1,0:T(8,128)S(1)}, f32[256,128]{1,0:T(8,128)S(1)}, u32[]{:S(2)}, u32[]{:S(2)}) collective-permute-start(f32[256,128]{1,0:T(8,128)S(1)} %get-tuple-element.48.refs_3_), channel_id=1, source_target_pairs={{0,2},{1,3},{2,4},{3,5},{4,6},{5,7},{6,0},{7,1},{8,10},{9,11},{10,... | collective-permute-start | bytes 393224 | tf_op jit(solution)/shard_map/ppermute | solution.py:42
  81.9 2.8 %collective-permute-start.14 = (f32[256,128]{1,0:T(8,128)S(1)}, f32[256,128]{1,0:T(8,128)S(1)}, u32[]{:S(2)}, u32[]{:S(2)}) collective-permute-start(f32[256,128]{1,0:T(8,128)S(1)} %get-tuple-element.48.refs_3_), channel_id=1, source_target_pairs={{0,6},{1,7},{2,0},{3,1},{4,2},{5,3},{6,4},{7,5},{8,14},{9,15},{10,... | collective-permute-start | bytes 393224 | tf_op jit(solution)/shard_map/ppermute | solution.py:42
  84.7 1.6 %collective-permute-start.28 = (f32[128,128]{1,0:T(8,128)S(1)}, f32[128,128]{1,0:T(8,128)S(1)}, u32[]{:S(2)}, u32[]{:S(2)}) collective-permute-start(f32[128,128]{1,0:T(8,128)S(1)} %add.110), channel_id=1, source_target_pairs={{0,4},{1,5},{2,6},{3,7},{4,0},{5,1},{6,2},{7,3},{8,12},{9,13},{10,... | collective-permute-start | bytes 196616 | tf_op jit(solution)/shard_map/ppermute | solution.py:42
  86.3 9.2 %collective-permute-done.28 = f32[128,128]{1,0:T(8,128)S(1)} collective-permute-done((f32[128,128]{1,0:T(8,128)S(1)}, f32[128,128]{1,0:T(8,128)S(1)}, u32[]{:S(2)}, u32[]{:S(2)}) %collective-permute-start.28) | collective-permute-done | bytes 65568 | tf_op jit(solution)/shard_map/ppermute | solution.py:42
  95.5 1.6 %collective-permute-start.19 = (f32[256,128]{1,0:T(8,128)S(1)}, f32[256,128]{1,0:T(8,128)S(1)}, u32[]{:S(2)}, u32[]{:S(2)}) collective-permute-start(f32[256,128]{1,0:T(8,128)S(1)} %get-tuple-element.49.refs_0_), channel_id=1, source_target_pairs={{0,6},{1,7},{2,0},{3,1},{4,2},{5,3},{6,4},{7,5},{8,14},{9,15},{10,... | collective-permute-start | bytes 393224 | tf_op jit(solution)/shard_map/ppermute | solution.py:42
  97.0 0.2 collective-permute-start.26
  97.3 0.3 collective-permute-start.29
  97.7 1.0 collective-permute-done.29
  98.6 0.5 collective-permute-start.17
  99.1 3.4 %collective-permute-start.18 = (f32[256,128]{1,0:T(8,128)S(1)}, f32[256,128]{1,0:T(8,128)S(1)}, u32[]{:S(2)}, u32[]{:S(2)}) collective-permute-start(f32[256,128]{1,0:T(8,128)S(1)} %collective-permute-done.14.refs_4_), channel_id=1, source_target_pairs={{0,6},{1,7},{2,0},{3,1},{4,2},{5,3},{6,4},{7,5},{8,14},{9,15},{10,... | collective-permute-start | bytes 393224 | tf_op jit(solution)/shard_map/ppermute | solution.py:42
  102.5 0.5 collective-permute-start.23
  103.1 0.9 gram.1
  104.0 0.3 collective-permute-done.22.refs_7_
  104.3 2.2 %place.2.refs_0_ = f32[4,4,2,1,128,128]{5,4,3,2,1,0:T(8,128)} custom-call(s32[8]{0:T(128)S(1)} %pad_add_fusion.ids_ref, f32[256,128]{1,0:T(8,128)S(1)} %get-tuple-element.49.refs_0_, f32[256,128]{1,0:T(8,128)S(1)} %collective-permute-done.19.refs_1_, f32[256,128]{1,0:T(8,128)S(1)} %collective-permute-done.13.refs_2_, ...), custom_call_target="tpu_custom_call" | custom-call | tf_op jit(solution)/shard_map/place/pallas_call | solution.py:420
  106.5 0.3 collective-permute-done.17.refs_1_
  106.8 0.5 collective-permute-done.18.refs_2_
  107.3 0.5 collective-permute-start.31
  107.8 0.8 collective-permute-done.30.refs_3_
  108.7 0.2 collective-permute-done.31.refs_4_
  108.8 1.5 %place.3 = f32[4,4,2,1,128,128]{5,4,3,2,1,0:T(8,128)} custom-call(s32[8]{0:T(128)S(1)} %pad_add_fusion.ids_ref, f32[4,4,2,1,128,128]{5,4,3,2,1,0:T(8,128)} %place.2.refs_0_, f32[256,128]{1,0:T(8,128)S(1)} %collective-permute-done.17.refs_1_, f32[256,128]{1,0:T(8,128)S(1)} %collective-permute-done.18.refs_2_, ...), custom_call_target="tpu_custom_call", output_to_operand_aliasing={{}: (1, {})} | custom-call | tf_op jit(solution)/shard_map/place/pallas_call | solution.py:420
  (56 shorter events, 0.9 us)
Async XLA Ops:
  0.6 8.5 %copy-start.3 = (s32[16]{0:T(128)S(1)}, s32[16]{0:T(128)}, u32[]{:S(2)}) copy-start(s32[16]{0:T(128)} %constant.70.clone) | copy-start | bytes 196
  0.6 8.5 %copy-start.4 = (s32[16]{0:T(128)S(1)}, s32[16]{0:T(128)}, u32[]{:S(2)}) copy-start(s32[16]{0:T(128)} %constant.69.clone) | copy-start | bytes 196
  0.7 8.6 %copy-start = (f32[32,128,128]{2,1,0:T(8,128)S(1)}, f32[32,128,128]{2,1,0:T(8,128)}, u32[]{:S(2)}) copy-start(f32[32,128,128]{2,1,0:T(8,128)} %param.7) | copy-start | bytes 6291460
  0.7 5.4 %copy-start.2 = (f32[128,128]{1,0:T(8,128)S(1)}, f32[128,128]{1,0:T(8,128)}, u32[]{:S(2)}) copy-start(f32[128,128]{1,0:T(8,128)} %d_ref.1) | copy-start | bytes 196612
  3.1 26.9 %collective-permute-start = (f32[2048,128]{1,0:T(8,128)}, f32[2048,128]{1,0:T(8,128)S(1)}, u32[]{:S(2)}, u32[]{:S(2)}) collective-permute-start(f32[2048,128]{1,0:T(8,128)} %bitcast.17), channel_id=1, source_target_pairs={{0,8},{1,16},{2,24},{3,0},{4,12},{5,20},{6,28},{7,4},{8,25},{9,1},... | collective-permute-start | bytes 3145736 | tf_op jit(solution)/shard_map/ppermute | solution.py:42
  32.7 4.2 %collective-permute-start.1 = (f32[512,128]{1,0:T(8,128)S(1)}, f32[512,128]{1,0:T(8,128)S(1)}, u32[]{:S(2)}, u32[]{:S(2)}) collective-permute-start(f32[512,128]{1,0:T(8,128)S(1)} %get-tuple-element.27), channel_id=1, source_target_pairs={{0,1},{1,0},{2,3},{3,2},{4,5},{5,4},{6,7},{7,6},{8,9},{9,8},{10,11... | collective-permute-start | bytes 786440 | tf_op jit(solution)/shard_map/ppermute | solution.py:42
  32.8 9.6 %collective-permute-start.4 = (f32[512,128]{1,0:T(8,128)S(1)}, f32[512,128]{1,0:T(8,128)S(1)}, u32[]{:S(2)}, u32[]{:S(2)}) collective-permute-start(f32[512,128]{1,0:T(8,128)S(1)} %get-tuple-element.29.refs_1_), channel_id=1, source_target_pairs={{0,8},{1,9},{2,10},{3,11},{4,12},{5,13},{6,14},{7,15},{8,0},{9,1},... | collective-permute-start | bytes 786440 | tf_op jit(solution)/shard_map/ppermute | solution.py:42
  35.2 14.0 %collective-permute-start.5 = (f32[512,128]{1,0:T(8,128)S(1)}, f32[512,128]{1,0:T(8,128)S(1)}, u32[]{:S(2)}, u32[]{:S(2)}) collective-permute-start(f32[512,128]{1,0:T(8,128)S(1)} %get-tuple-element.30.refs_2_), channel_id=1, source_target_pairs={{0,16},{1,17},{2,18},{3,19},{4,20},{5,21},{6,22},{7,23},{8,24},{9,... | collective-permute-start | bytes 786440 | tf_op jit(solution)/shard_map/ppermute | solution.py:42
  35.9 13.3 %collective-permute-start.6 = (f32[512,128]{1,0:T(8,128)S(1)}, f32[512,128]{1,0:T(8,128)S(1)}, u32[]{:S(2)}, u32[]{:S(2)}) collective-permute-start(f32[512,128]{1,0:T(8,128)S(1)} %get-tuple-element.31.refs_3_), channel_id=1, source_target_pairs={{0,24},{1,25},{2,26},{3,27},{4,28},{5,29},{6,30},{7,31},{8,16},{9,... | collective-permute-start | bytes 786440 | tf_op jit(solution)/shard_map/ppermute | solution.py:42
  37.0 12.3 %collective-permute-start.3 = (f32[256,128]{1,0:T(8,128)S(1)}, f32[256,128]{1,0:T(8,128)S(1)}, u32[]{:S(2)}, u32[]{:S(2)}) collective-permute-start(f32[256,128]{1,0:T(8,128)S(1)} %get-tuple-element.54), channel_id=1, source_target_pairs={{0,6},{1,7},{2,0},{3,1},{4,2},{5,3},{6,4},{7,5},{8,14},{9,15},{10,... | collective-permute-start | bytes 393224 | tf_op jit(solution)/shard_map/ppermute | solution.py:42
  41.0 8.3 %collective-permute-start.2 = (f32[256,128]{1,0:T(8,128)S(1)}, f32[256,128]{1,0:T(8,128)S(1)}, u32[]{:S(2)}, u32[]{:S(2)}) collective-permute-start(f32[256,128]{1,0:T(8,128)S(1)} %get-tuple-element.55), channel_id=1, source_target_pairs={{0,2},{1,3},{2,4},{3,5},{4,6},{5,7},{6,0},{7,1},{8,10},{9,11},{10,... | collective-permute-start | bytes 393224 | tf_op jit(solution)/shard_map/ppermute | solution.py:42
  54.8 1.6 %collective-permute-start.8 = (f32[512,128]{1,0:T(8,128)S(1)}, f32[512,128]{1,0:T(8,128)S(1)}, u32[]{:S(2)}, u32[]{:S(2)}) collective-permute-start(f32[512,128]{1,0:T(8,128)S(1)} %get-tuple-element.46), channel_id=1, source_target_pairs={{0,1},{1,0},{2,3},{3,2},{4,5},{5,4},{6,7},{7,6},{8,9},{9,8},{10,11... | collective-permute-start | bytes 786440 | tf_op jit(solution)/shard_map/ppermute | solution.py:42
  54.8 1.9 %collective-permute-start.7 = (f32[512,128]{1,0:T(8,128)S(1)}, f32[512,128]{1,0:T(8,128)S(1)}, u32[]{:S(2)}, u32[]{:S(2)}) collective-permute-start(f32[512,128]{1,0:T(8,128)S(1)} %get-tuple-element.47), channel_id=1, source_target_pairs={{0,1},{1,0},{2,3},{3,2},{4,5},{5,4},{6,7},{7,6},{8,9},{9,8},{10,11... | collective-permute-start | bytes 786440 | tf_op jit(solution)/shard_map/ppermute | solution.py:42
  55.3 23.7 %collective-permute-start.12 = (f32[512,128]{1,0:T(8,128)S(1)}, f32[512,128]{1,0:T(8,128)S(1)}, u32[]{:S(2)}, u32[]{:S(2)}) collective-permute-start(f32[512,128]{1,0:T(8,128)S(1)} %add_add_fusion), channel_id=1, source_target_pairs={{0,0},{1,8},{2,16},{3,24},{4,4},{5,12},{6,20},{7,28},{8,1},{9,9},{... | collective-permute-start | bytes 786440 | tf_op jit(solution)/shard_map/ppermute | solution.py:42
  56.9 22.2 %collective-permute-start.11 = (f32[512,128]{1,0:T(8,128)S(1)}, f32[512,128]{1,0:T(8,128)S(1)}, u32[]{:S(2)}, u32[]{:S(2)}) collective-permute-start(f32[512,128]{1,0:T(8,128)S(1)} %pad_maximum_fusion.1), channel_id=1, source_target_pairs={{0,6},{1,7},{2,0},{3,1},{4,2},{5,3},{6,4},{7,5},{8,14},{9,15},{10,... | collective-permute-start | bytes 786440 | tf_op jit(solution)/shard_map/ppermute | solution.py:42
  61.9 6.6 %copy-start.1 = (f32[32,128,128]{2,1,0:T(8,128)S(1)}, f32[32,128,128]{2,1,0:T(8,128)}, u32[]{:S(2)}) copy-start(f32[32,128,128]{2,1,0:T(8,128)} %param.8) | copy-start | bytes 6291460
  68.2 10.8 %collective-permute-start.9 = (f32[512,128]{1,0:T(8,128)S(1)}, f32[512,128]{1,0:T(8,128)S(1)}, u32[]{:S(2)}, u32[]{:S(2)}) collective-permute-start(f32[512,128]{1,0:T(8,128)S(1)} %get-tuple-element.37), channel_id=1, source_target_pairs={{0,1},{1,0},{2,3},{3,2},{4,5},{5,4},{6,7},{7,6},{8,9},{9,8},{10,11... | collective-permute-start | bytes 786440 | tf_op jit(solution)/shard_map/ppermute | solution.py:42
  68.5 11.3 %collective-permute-start.10 = (f32[512,128]{1,0:T(8,128)S(1)}, f32[512,128]{1,0:T(8,128)S(1)}, u32[]{:S(2)}, u32[]{:S(2)}) collective-permute-start(f32[512,128]{1,0:T(8,128)S(1)} %pad_maximum_fusion), channel_id=1, source_target_pairs={{0,2},{1,3},{2,4},{3,5},{4,6},{5,7},{6,0},{7,1},{8,10},{9,11},{10,... | collective-permute-start | bytes 786440 | tf_op jit(solution)/shard_map/ppermute | solution.py:42
  70.0 4.4 %collective-permute-start.15 = (f32[128,128]{1,0:T(8,128)S(1)}, f32[128,128]{1,0:T(8,128)S(1)}, u32[]{:S(2)}, u32[]{:S(2)}) collective-permute-start(f32[128,128]{1,0:T(8,128)S(1)} %moment.1), channel_id=1, source_target_pairs={{0,8},{1,9},{2,10},{3,11},{4,12},{5,13},{6,14},{7,15},{8,0},{9,1},... | collective-permute-start | bytes 196616 | tf_op jit(solution)/shard_map/ppermute | solution.py:42
  74.4 4.3 %collective-permute-start.16 = (f32[128,128]{1,0:T(8,128)S(1)}, f32[128,128]{1,0:T(8,128)S(1)}, u32[]{:S(2)}, u32[]{:S(2)}) collective-permute-start(f32[128,128]{1,0:T(8,128)S(1)} %add.108), channel_id=1, source_target_pairs={{0,16},{1,17},{2,18},{3,19},{4,20},{5,21},{6,22},{7,23},{8,24},{9,... | collective-permute-start | bytes 196616 | tf_op jit(solution)/shard_map/ppermute | solution.py:42
  78.7 6.0 %collective-permute-start.27 = (f32[128,128]{1,0:T(8,128)S(1)}, f32[128,128]{1,0:T(8,128)S(1)}, u32[]{:S(2)}, u32[]{:S(2)}) collective-permute-start(f32[128,128]{1,0:T(8,128)S(1)} %add.109), channel_id=1, source_target_pairs={{0,2},{1,3},{2,0},{3,1},{4,6},{5,7},{6,4},{7,5},{8,10},{9,11},{10,... | collective-permute-start | bytes 196616 | tf_op jit(solution)/shard_map/ppermute | solution.py:42
  80.8 14.7 %collective-permute-start.20 = (f32[256,128]{1,0:T(8,128)S(1)}, f32[256,128]{1,0:T(8,128)S(1)}, u32[]{:S(2)}, u32[]{:S(2)}) collective-permute-start(f32[256,128]{1,0:T(8,128)S(1)} %get-tuple-element.48.refs_3_), channel_id=1, source_target_pairs={{0,2},{1,3},{2,4},{3,5},{4,6},{5,7},{6,0},{7,1},{8,10},{9,11},{10,... | collective-permute-start | bytes 393224 | tf_op jit(solution)/shard_map/ppermute | solution.py:42
  81.9 15.2 %collective-permute-start.14 = (f32[256,128]{1,0:T(8,128)S(1)}, f32[256,128]{1,0:T(8,128)S(1)}, u32[]{:S(2)}, u32[]{:S(2)}) collective-permute-start(f32[256,128]{1,0:T(8,128)S(1)} %get-tuple-element.48.refs_3_), channel_id=1, source_target_pairs={{0,6},{1,7},{2,0},{3,1},{4,2},{5,3},{6,4},{7,5},{8,14},{9,15},{10,... | collective-permute-start | bytes 393224 | tf_op jit(solution)/shard_map/ppermute | solution.py:42
  84.6 12.6 %collective-permute-start.13 = (f32[256,128]{1,0:T(8,128)S(1)}, f32[256,128]{1,0:T(8,128)S(1)}, u32[]{:S(2)}, u32[]{:S(2)}) collective-permute-start(f32[256,128]{1,0:T(8,128)S(1)} %get-tuple-element.49.refs_0_), channel_id=1, source_target_pairs={{0,2},{1,3},{2,4},{3,5},{4,6},{5,7},{6,0},{7,1},{8,10},{9,11},{10,... | collective-permute-start | bytes 393224 | tf_op jit(solution)/shard_map/ppermute | solution.py:42
  84.7 10.8 %collective-permute-start.28 = (f32[128,128]{1,0:T(8,128)S(1)}, f32[128,128]{1,0:T(8,128)S(1)}, u32[]{:S(2)}, u32[]{:S(2)}) collective-permute-start(f32[128,128]{1,0:T(8,128)S(1)} %add.110), channel_id=1, source_target_pairs={{0,4},{1,5},{2,6},{3,7},{4,0},{5,1},{6,2},{7,3},{8,12},{9,13},{10,... | collective-permute-start | bytes 196616 | tf_op jit(solution)/shard_map/ppermute | solution.py:42
  86.3 12.8 %collective-permute-start.24 = (f32[256,128]{1,0:T(8,128)S(1)}, f32[256,128]{1,0:T(8,128)S(1)}, u32[]{:S(2)}, u32[]{:S(2)}) collective-permute-start(f32[256,128]{1,0:T(8,128)S(1)} %get-tuple-element.48.refs_3_), channel_id=1, source_target_pairs={{0,1},{1,0},{2,3},{3,2},{4,5},{5,4},{6,7},{7,6},{8,9},{9,8},{10,11... | collective-permute-start | bytes 393224 | tf_op jit(solution)/shard_map/ppermute | solution.py:42
  95.5 7.0 %collective-permute-start.21 = (f32[256,128]{1,0:T(8,128)S(1)}, f32[256,128]{1,0:T(8,128)S(1)}, u32[]{:S(2)}, u32[]{:S(2)}) collective-permute-start(f32[256,128]{1,0:T(8,128)S(1)} %get-tuple-element.49.refs_0_), channel_id=1, source_target_pairs={{0,1},{1,0},{2,3},{3,2},{4,5},{5,4},{6,7},{7,6},{8,9},{9,8},{10,11... | collective-permute-start | bytes 393224 | tf_op jit(solution)/shard_map/ppermute | solution.py:42
  95.5 7.0 %collective-permute-start.19 = (f32[256,128]{1,0:T(8,128)S(1)}, f32[256,128]{1,0:T(8,128)S(1)}, u32[]{:S(2)}, u32[]{:S(2)}) collective-permute-start(f32[256,128]{1,0:T(8,128)S(1)} %get-tuple-element.49.refs_0_), channel_id=1, source_target_pairs={{0,6},{1,7},{2,0},{3,1},{4,2},{5,3},{6,4},{7,5},{8,14},{9,15},{10,... | collective-permute-start | bytes 393224 | tf_op jit(solution)/shard_map/ppermute | solution.py:42
  97.0 5.9 %collective-permute-start.26 = (f32[256,128]{1,0:T(8,128)S(1)}, f32[256,128]{1,0:T(8,128)S(1)}, u32[]{:S(2)}, u32[]{:S(2)}) collective-permute-start(f32[256,128]{1,0:T(8,128)S(1)} %collective-permute-done.20.refs_5_), channel_id=1, source_target_pairs={{0,1},{1,0},{2,3},{3,2},{4,5},{5,4},{6,7},{7,6},{8,9},{9,8},{10,11... | collective-permute-start | bytes 393224 | tf_op jit(solution)/shard_map/ppermute | solution.py:42
  97.3 1.3 %collective-permute-start.29 = (f32[128,128]{1,0:T(8,128)S(1)}, f32[128,128]{1,0:T(8,128)S(1)}, u32[]{:S(2)}, u32[]{:S(2)}) collective-permute-start(f32[128,128]{1,0:T(8,128)S(1)} %add.111), channel_id=1, source_target_pairs={{0,1},{1,0},{2,3},{3,2},{4,5},{5,4},{6,7},{7,6},{8,9},{9,8},{10,11... | collective-permute-start | bytes 196616 | tf_op jit(solution)/shard_map/ppermute | solution.py:42
  98.6 8.2 %collective-permute-start.17 = (f32[256,128]{1,0:T(8,128)S(1)}, f32[256,128]{1,0:T(8,128)S(1)}, u32[]{:S(2)}, u32[]{:S(2)}) collective-permute-start(f32[256,128]{1,0:T(8,128)S(1)} %collective-permute-done.13.refs_2_), channel_id=1, source_target_pairs={{0,2},{1,3},{2,4},{3,5},{4,6},{5,7},{6,0},{7,1},{8,10},{9,11},{10,... | collective-permute-start | bytes 393224 | tf_op jit(solution)/shard_map/ppermute | solution.py:42
  99.1 8.2 %collective-permute-start.18 = (f32[256,128]{1,0:T(8,128)S(1)}, f32[256,128]{1,0:T(8,128)S(1)}, u32[]{:S(2)}, u32[]{:S(2)}) collective-permute-start(f32[256,128]{1,0:T(8,128)S(1)} %collective-permute-done.14.refs_4_), channel_id=1, source_target_pairs={{0,6},{1,7},{2,0},{3,1},{4,2},{5,3},{6,4},{7,5},{8,14},{9,15},{10,... | collective-permute-start | bytes 393224 | tf_op jit(solution)/shard_map/ppermute | solution.py:42
  102.4 1.6 %collective-permute-start.25 = (f32[256,128]{1,0:T(8,128)S(1)}, f32[256,128]{1,0:T(8,128)S(1)}, u32[]{:S(2)}, u32[]{:S(2)}) collective-permute-start(f32[256,128]{1,0:T(8,128)S(1)} %collective-permute-done.14.refs_4_), channel_id=1, source_target_pairs={{0,1},{1,0},{2,3},{3,2},{4,5},{5,4},{6,7},{7,6},{8,9},{9,8},{10,11... | collective-permute-start | bytes 393224 | tf_op jit(solution)/shard_map/ppermute | solution.py:42
  102.5 1.9 %collective-permute-start.23 = (f32[256,128]{1,0:T(8,128)S(1)}, f32[256,128]{1,0:T(8,128)S(1)}, u32[]{:S(2)}, u32[]{:S(2)}) collective-permute-start(f32[256,128]{1,0:T(8,128)S(1)} %collective-permute-done.13.refs_2_), channel_id=1, source_target_pairs={{0,1},{1,0},{2,3},{3,2},{4,5},{5,4},{6,7},{7,6},{8,9},{9,8},{10,11... | collective-permute-start | bytes 393224 | tf_op jit(solution)/shard_map/ppermute | solution.py:42
  103.0 1.3 %collective-permute-start.22 = (f32[256,128]{1,0:T(8,128)S(1)}, f32[256,128]{1,0:T(8,128)S(1)}, u32[]{:S(2)}, u32[]{:S(2)}) collective-permute-start(f32[256,128]{1,0:T(8,128)S(1)} %collective-permute-done.19.refs_1_), channel_id=1, source_target_pairs={{0,1},{1,0},{2,3},{3,2},{4,5},{5,4},{6,7},{7,6},{8,9},{9,8},{10,11... | collective-permute-start | bytes 393224 | tf_op jit(solution)/shard_map/ppermute | solution.py:42
  107.3 1.3 %collective-permute-start.30 = (f32[256,128]{1,0:T(8,128)S(1)}, f32[256,128]{1,0:T(8,128)S(1)}, u32[]{:S(2)}, u32[]{:S(2)}) collective-permute-start(f32[256,128]{1,0:T(8,128)S(1)} %collective-permute-done.17.refs_1_), channel_id=1, source_target_pairs={{0,1},{1,0},{2,3},{3,2},{4,5},{5,4},{6,7},{7,6},{8,9},{9,8},{10,11... | collective-permute-start | bytes 393224 | tf_op jit(solution)/shard_map/ppermute | solution.py:42
  107.3 1.5 %collective-permute-start.31 = (f32[256,128]{1,0:T(8,128)S(1)}, f32[256,128]{1,0:T(8,128)S(1)}, u32[]{:S(2)}, u32[]{:S(2)}) collective-permute-start(f32[256,128]{1,0:T(8,128)S(1)} %collective-permute-done.18.refs_2_), channel_id=1, source_target_pairs={{0,1},{1,0},{2,3},{3,2},{4,5},{5,4},{6,7},{7,6},{8,9},{9,8},{10,11... | collective-permute-start | bytes 393224 | tf_op jit(solution)/shard_map/ppermute | solution.py:42

commit v3 on v2

--- a/solution.py
+++ b/solution.py
@@ -160,7 +160,8 @@
     return out[:n_row], out[n_row], out[n_row + 1]
 
 
-def direct_body(n_blocks, group, half, ids_ref, s_ref, p_ref, away_ref, keep_ref, right):
+def direct_body(n_blocks, group, half, ids_ref, s_ref, p_ref, *refs):
+    away_ref, keep_ref, right = refs[-3:]
     step = pl.program_id(0)
     width = p_ref.shape[1]
 
@@ -196,7 +197,7 @@
         keep_ref[...] = result
 
 
-def direct_chunks(chunked, col_panel, ids, first, half, chunk_at):
+def direct_chunks(chunked, col_panel, ids, first, half, chunk_at, earlier=()):
     _, n_sub, _, _, sub_rows, width = chunked.shape
     n_blocks = col_panel.shape[0] // width
     group = math.gcd(n_blocks, 2)
@@ -215,7 +216,8 @@
             in_specs=[
                 pl.BlockSpec((None, n_sub, None, None, sub_rows, width), s_index),
                 pl.BlockSpec((n_blocks * width, width), lambda i, ids: (0, 0)),
-            ],
+            ]
+            + [pl.BlockSpec(memory_space=pl.ANY)] * len(earlier),
             out_specs=[
                 pl.BlockSpec((chunk_rows, width), lambda i, ids: (jnp.minimum(i, half - 1), 0)),
                 pl.BlockSpec((chunk_rows, width), lambda i, ids: (jnp.maximum(i - half, 0), 0)),
@@ -226,10 +228,11 @@
         compiler_params=pltpu.CompilerParams(vmem_limit_bytes=CHUNK_VMEM),
         cost_estimate=pl.CostEstimate(flops=1, bytes_accessed=1, transcendentals=0),
         name="direct",
-    )(ids, chunked, col_panel)
-
-
-def kept_body(first, half, high_ref, low_ref, p_ref, away_ref, keep_ref, right):
+    )(ids, chunked, col_panel, *earlier)
+
+
+def kept_body(first, half, high_ref, low_ref, p_ref, *refs):
+    away_ref, keep_ref, right = refs[-3:]
     step = pl.program_id(0)
     width = p_ref.shape[1]
     rows = away_ref.shape[0]
@@ -253,14 +256,15 @@
         keep_ref[...] = result
 
 
-def direct_kept(plan, high, low, col_panel, first, half):
+def direct_kept(plan, high, low, col_panel, first, half, earlier=()):
     rows, width, depth = plan.chunk_rows, plan.width, col_panel.shape[0]
     out = jax.ShapeDtypeStruct((half * rows, width), F32)
     held = pl.BlockSpec(memory_space=pltpu.VMEM)
     return pl.pallas_call(
         functools.partial(kept_body, first, half),
         grid=(2 * half,),
-        in_specs=[held, held, pl.BlockSpec((depth, width), lambda i: (0, 0))],
+        in_specs=[held, held, pl.BlockSpec((depth, width), lambda i: (0, 0))]
+        + [pl.BlockSpec(memory_space=pl.ANY)] * len(earlier),
         out_specs=[
             pl.BlockSpec((rows, width), lambda i: (jnp.minimum(i, half - 1), 0)),
             pl.BlockSpec((rows, width), lambda i: (jnp.maximum(i - half, 0), 0)),
@@ -270,7 +274,7 @@
         compiler_params=pltpu.CompilerParams(vmem_limit_bytes=DIRECT_VMEM),
         cost_estimate=pl.CostEstimate(flops=1, bytes_accessed=1, transcendentals=0),
         name="direct_kept",
-    )(high, low, col_panel)
+    )(high, low, col_panel, *earlier)
 
 
 def inverse_body(d_ref, o_ref):
@@ -359,7 +363,7 @@
 
 
 def solve_body(n_terms, ids_ref, *refs):
-    terms, (inv_ref, b_ref, x_ref) = refs[:n_terms], refs[n_terms:]
+    terms, inv_ref, b_ref, x_ref = refs[:n_terms], refs[n_terms], refs[-2], refs[-1]
     image = terms[0][...]
     for term in terms[1:]:
         image = image + term[...]
@@ -513,46 +517,46 @@
         bit *= 2
     row_steps = len(moments) - 1
 
+    def later(*arrays, times=1):
+        few = sum(x[:8] for x in arrays)
+        for _ in range(times):
+            few = move(few, twin)
+        return few
+
     rows = plan.chunk_rows
     cut = rows // 2
-    below, above = None, None
+    sent = []
     for begin, here in plan.steps:
         if here[0] == 0:
-            fence = totals
+            earlier = totals
         elif begin:
-            fence = (keep, below, above, flip_sum)
+            earlier = totals + [flip_sum, moments[1]]
         else:
-            fence = inv
-        right, _ = lax.optimization_barrier((col_panel, fence))
+            earlier = [inv]
+        right = col_panel
         if begin in plan.slots:
-            away, keep = direct_kept(plan, high, low, right, plan.slots[begin], len(here))
+            away, keep = direct_kept(plan, high, low, right, plan.slots[begin], len(here), earlier)
         else:
             chunked = trail_adjoint.reshape(*plan.view[:4], plan.view[4] * col_blocks, width)
-            away, keep = direct_chunks(chunked, right, ids, begin, len(here), plan.chunk_at)
+            away, keep = direct_chunks(chunked, right, ids, begin, len(here), plan.chunk_at, earlier)
         totals = []
         for k in range(len(here)):
             piece = slice(k * rows, (k + 1) * rows)
             totals.append(keep[piece] + move(away[piece], twin))
         if here[0] == 0:
             own = totals[0]
-        elif len(here) == 1:
-            below, above = move(totals[0][:cut], up), move(totals[0][cut:], down)
         else:
-            first, second = totals
-            if below.shape[0] == cut:
-                first = jnp.concatenate([first[:cut] + below, first[cut:]], 0)
-                second = jnp.concatenate([second[:cut], second[cut:] + above], 0)
-            else:
-                first, second = first + below, second + above
-            below, above = move(first, up), move(second, down)
-    mine = [own, below, above, flipped]
+            sent += [
+                move(total, lambda r, c: (r, (c + 2 * distance) % n_col)) for distance, total in zip(here, totals)
+            ]
+    mine = [own, flipped] + sent
 
     bit = 1
     while bit < n_z:
         moments.append(moments[-1] + move(moments[-1], lambda r, c: (r, c ^ (2 * bit))))
         bit *= 2
     x = on_my_chunk(
-        plan, functools.partial(solve_body, len(mine)), ids, mine + [inv], panel_adjoint, (rows, width), "solve"
+        plan, functools.partial(solve_body, len(mine)), ids, mine + [inv] + [later(*sent)], panel_adjoint, (rows, width), "solve"
     )
 
     lower, upper = {0: x[:cut]}, {0: x[cut:]}

time: 111 us -> 110 us (level)
  waiting for transfers between devices: 30.4 us -> 26.4 us
  starting transfers between devices: 32.7 us -> 36.3 us
    ppermute x32, waiting for transfers between devices: 30.4 us -> 26.4 us  [send(): return lax.ppermute(x, AXES, pairs)]
    ppermute x32, starting transfers between devices: 32.7 us -> 36.3 us  [send(): return lax.ppermute(x, AXES, pairs)]
  transfers between devices with their start and end apart: 32 -> 32, of which waited for: 15 -> 13; matrix products, arithmetic and copies ran while one was open for 0% -> 0% of each run, Pallas kernels for 31% -> 33%
where the time goes in v3:
time: 110 us
  Pallas kernels  45.7 us (42%)
  starting transfers between devices  36.3 us (33%)
  waiting for transfers between devices  26.4 us (24%)
    ppermute x32, starting transfers between devices, send(): return lax.ppermute(x, AXES, pairs)  36.3 us
    ppermute x32, waiting for transfers between devices, send(): return lax.ppermute(x, AXES, pairs)  26.4 us
    pallas_call x1, Pallas kernels, flip_parts(): pl.pallas_call(functools.partial(flip_body, plan, n_row), grid_spec=pltpu...  18.9 us
    pallas_call x2, Pallas kernels, direct_kept(): pl.pallas_call(functools.partial(kept_body, first, half), grid=(2 * half,...  8.21 us
    pallas_call x1, Pallas kernels, direct_chunks(): pl.pallas_call(functools.partial(direct_body, n_blocks, group, half), gri...  6.24 us
    pallas_call x2, Pallas kernels, place(): pl.pallas_call(functools.partial(place_body, plan, [piece[1:] for piece i...  3.7 us
    pallas_call x1, Pallas kernels, inverse(): pl.pallas_call(inverse_body, out_shape=jax.ShapeDtypeStruct(diag_block.sh...  3.09 us
    pallas_call x1, Pallas kernels, choose(): pl.pallas_call(body, grid_spec=pltpu.PrefetchScalarGridSpec(num_scalar_pr...  2.35 us
  transfers between devices with their start and end apart: 32, of which 13 were waited for; matrix products, arithmetic and copies ran while one was open for 0% of the time, Pallas kernels for 33%

profile of v3, /device:TPU:0, one launch (start us, length us, event | category | flops | bytes accessed | tf_op | source)
XLA Modules:
  0.0 109.7 jit_solution(5188598277374704290)
XLA Ops:
  0.7 2.4 %choose.1 = f32[16,128,128]{2,1,0:T(8,128)} custom-call(s32[1]{0:T(128)} %bitcast.1.which_ref, f32[16,2,128,128]{3,2,1,0:T(8,128)} %bitcast.9), custom_call_target="tpu_custom_call" | custom-call | tf_op jit(solution)/shard_map/choose/pallas_call | solution.py:53
  3.0 3.0 %collective-permute-start = (f32[2048,128]{1,0:T(8,128)}, f32[2048,128]{1,0:T(8,128)S(1)}, u32[]{:S(2)}, u32[]{:S(2)}) collective-permute-start(f32[2048,128]{1,0:T(8,128)} %bitcast.17), channel_id=1, source_target_pairs={{0,8},{1,16},{2,24},{3,0},{4,12},{5,20},{6,28},{7,4},{8,25},{9,1},... | collective-permute-start | bytes 3145736 | tf_op jit(solution)/shard_map/ppermute | solution.py:42
  6.1 18.9 %flip.1 = (f32[512,128]{1,0:T(8,128)S(1)}, f32[512,128]{1,0:T(8,128)S(1)}, f32[512,128]{1,0:T(8,128)S(1)}, f32[512,128]{1,0:T(8,128)S(1)}, bf16[3072,2048]{1,0:T...) custom-call(s32[1]{0:T(128)} %bitcast.4.me_ref, s32[16]{0:T(128)S(1)} %fusion.2.ids_ref, ...), custom_call_target="tpu_custom_call" | custom-call | flops 6442450944 | bytes 33554432 | tf_op jit(solution)/shard_map/flip/pallas_call | solution.py:135
  25.0 1.0 collective-permute-start.2
  26.1 1.6 %collective-permute-start.3 = (f32[512,128]{1,0:T(8,128)S(1)}, f32[512,128]{1,0:T(8,128)S(1)}, u32[]{:S(2)}, u32[]{:S(2)}) collective-permute-start(f32[512,128]{1,0:T(8,128)S(1)} %get-tuple-element.26.refs_2_), channel_id=1, source_target_pairs={{0,16},{1,17},{2,18},{3,19},{4,20},{5,21},{6,22},{7,23},{8,24},{9,... | collective-permute-start | bytes 786440 | tf_op jit(solution)/shard_map/ppermute | solution.py:42
  27.6 1.4 %collective-permute-start.4 = (f32[512,128]{1,0:T(8,128)S(1)}, f32[512,128]{1,0:T(8,128)S(1)}, u32[]{:S(2)}, u32[]{:S(2)}) collective-permute-start(f32[512,128]{1,0:T(8,128)S(1)} %get-tuple-element.27.refs_3_), channel_id=1, source_target_pairs={{0,24},{1,25},{2,26},{3,27},{4,28},{5,29},{6,30},{7,31},{8,16},{9,... | collective-permute-start | bytes 786440 | tf_op jit(solution)/shard_map/ppermute | solution.py:42
  29.0 3.1 %inverse.1.refs_0_.refs_5_.inv_ref = f32[128,128]{1,0:T(8,128)S(1)} custom-call(f32[128,128]{1,0:T(8,128)S(1)} %copy-done.2), custom_call_target="tpu_custom_call" | custom-call | tf_op jit(solution)/shard_map/inverse/pallas_call | solution.py:297
  32.2 2.8 %direct_kept.2 = (f32[512,128]{1,0:T(8,128)S(1)}, f32[512,128]{1,0:T(8,128)S(1)}) custom-call(bf16[3072,2048]{1,0:T(8,128)(2,1)S(1)} %get-tuple-element.20.high_ref, bf16[3072,2048]{1,0:T(8,128)(2,1)S(1)} %get-tuple-element.21.low_ref, f32[2048,128]{1,0:T(8,128)S(1)} %collective-permute-done.p_ref.refs_4_, f32[128,128]{1,0:T(8,128)S(1)} %inverse.1.refs_0_.refs_5_.inv_ref), custom_call_target="tpu_custom_call" | custom-call | flops 1 | bytes 1 | tf_op jit(solution)/shard_map/direct_kept/pallas_call | solution.py:263
  35.1 1.4 %moment.1 = f32[128,128]{1,0:T(8,128)S(1)} custom-call(s32[16]{0:T(128)S(1)} %fusion.2.ids_ref, s32[1]{0:T(128)} %bitcast.4.me_ref, f32[512,128]{1,0:T(8,128)S(1)} %get-tuple-element.24.refs_0_, f32[512,128]{1,0:T(8,128)S(1)} %get-tuple-element.25.refs_1_, f32[512,128]{1,0:T(8,128)S(1)} %get-tuple-element.26.refs_2_, ...), custom_call_target="tpu_custom_call" | custom-call | tf_op jit(solution)/shard_map/moment/pallas_call | solution.py:335
  36.4 1.3 %collective-permute-start.5 = (f32[128,128]{1,0:T(8,128)S(1)}, f32[128,128]{1,0:T(8,128)S(1)}, u32[]{:S(2)}, u32[]{:S(2)}) collective-permute-start(f32[128,128]{1,0:T(8,128)S(1)} %moment.1), channel_id=1, source_target_pairs={{0,8},{1,9},{2,10},{3,11},{4,12},{5,13},{6,14},{7,15},{8,0},{9,1},... | collective-permute-start | bytes 196616 | tf_op jit(solution)/shard_map/ppermute | solution.py:42
  37.8 2.7 %collective-permute-done.3 = f32[512,128]{1,0:T(8,128)S(1)} collective-permute-done((f32[512,128]{1,0:T(8,128)S(1)}, f32[512,128]{1,0:T(8,128)S(1)}, u32[]{:S(2)}, u32[]{:S(2)}) %collective-permute-start.3) | collective-permute-done | bytes 262176 | tf_op jit(solution)/shard_map/ppermute | solution.py:42
  40.5 1.2 %collective-permute-done.4 = f32[512,128]{1,0:T(8,128)S(1)} collective-permute-done((f32[512,128]{1,0:T(8,128)S(1)}, f32[512,128]{1,0:T(8,128)S(1)}, u32[]{:S(2)}, u32[]{:S(2)}) %collective-permute-start.4) | collective-permute-done | bytes 262176 | tf_op jit(solution)/shard_map/ppermute | solution.py:42
  41.8 0.7 collective-permute-done.5
  42.5 5.4 %direct_kept.3 = (f32[1024,128]{1,0:T(8,128)S(1)}, f32[1024,128]{1,0:T(8,128)S(1)}) custom-call(bf16[3072,2048]{1,0:T(8,128)(2,1)S(1)} %get-tuple-element.20.high_ref, bf16[3072,2048]{1,0:T(8,128)(2,1)S(1)} %get-tuple-element.21.low_ref, f32[2048,128]{1,0:T(8,128)S(1)} %collective-permute-done.p_ref.refs_4_, f32[512,128]{1,0:T(8,128)S(1)} %add.99.refs_0_, ...), custom_call_target="tpu_custom_call" | custom-call | flops 1 | bytes 1 | tf_op jit(solution)/shard_map/direct_kept/pallas_call | solution.py:263
  48.0 0.5 collective-permute-start.6
  48.5 2.6 %collective-permute-start.10 = (f32[512,128]{1,0:T(8,128)S(1)}, f32[512,128]{1,0:T(8,128)S(1)}, u32[]{:S(2)}, u32[]{:S(2)}) collective-permute-start(f32[512,128]{1,0:T(8,128)S(1)} %add.99.refs_0_), channel_id=1, source_target_pairs={{0,4},{1,5},{2,6},{3,7},{4,0},{5,1},{6,2},{7,3},{8,12},{9,13},{10,... | collective-permute-start | bytes 786440 | tf_op jit(solution)/shard_map/ppermute | solution.py:42
  51.2 1.7 %collective-permute-start.12 = (f32[512,128]{1,0:T(8,128)S(1)}, f32[512,128]{1,0:T(8,128)S(1)}, u32[]{:S(2)}, u32[]{:S(2)}) collective-permute-start(f32[512,128]{1,0:T(8,128)S(1)} %get-tuple-element.38.refs_1_), channel_id=1, source_target_pairs={{0,6},{1,7},{2,0},{3,1},{4,2},{5,3},{6,4},{7,5},{8,14},{9,15},{10,... | collective-permute-start | bytes 786440 | tf_op jit(solution)/shard_map/ppermute | solution.py:42
  52.9 0.4 collective-permute-start.11
  53.3 6.2 %direct.1 = (f32[512,128]{1,0:T(8,128)S(1)}, f32[512,128]{1,0:T(8,128)S(1)}) custom-call(s32[16]{0:T(128)S(1)} %fusion.2.ids_ref, f32[4,4,2,1,2048,128]{5,4,3,2,1,0:T(8,128)} %bitcast.15, f32[2048,128]{1,0:T(8,128)S(1)} %collective-permute-done.p_ref.refs_4_, f32[512,128]{1,0:T(8,128)S(1)} %get-tuple-element.39.refs_0_, f32[512,128]{1,0:T(8,128)S(1)} %get-tuple-element.38.refs_1_), custom_call_target="tpu_custom_call" | custom-call | flops 1 | bytes 1 | tf_op jit(solution)/shard_map/direct/pallas_call | solution.py:211
  59.6 0.7 collective-permute-start.9
  60.3 4.2 %collective-permute-done.10.refs_2_ = f32[512,128]{1,0:T(8,128)S(1)} collective-permute-done((f32[512,128]{1,0:T(8,128)S(1)}, f32[512,128]{1,0:T(8,128)S(1)}, u32[]{:S(2)}, u32[]{:S(2)}) %collective-permute-start.10) | collective-permute-done | bytes 262176 | tf_op jit(solution)/shard_map/ppermute | solution.py:42
  64.5 0.4 collective-permute-start.16
  64.9 4.8 %collective-permute-done.12.refs_4_ = f32[512,128]{1,0:T(8,128)S(1)} collective-permute-done((f32[512,128]{1,0:T(8,128)S(1)}, f32[512,128]{1,0:T(8,128)S(1)}, u32[]{:S(2)}, u32[]{:S(2)}) %collective-permute-start.12) | collective-permute-done | bytes 262176 | tf_op jit(solution)/shard_map/ppermute | solution.py:42
  69.7 0.4 collective-permute-done.11.refs_3_
  70.1 8.8 %collective-permute-start.27 = (f32[128,128]{1,0:T(8,128)S(1)}, f32[128,128]{1,0:T(8,128)S(1)}, u32[]{:S(2)}, u32[]{:S(2)}) collective-permute-start(f32[128,128]{1,0:T(8,128)S(1)} %add.109), channel_id=1, source_target_pairs={{0,2},{1,3},{2,0},{3,1},{4,6},{5,7},{6,4},{7,5},{8,10},{9,11},{10,... | collective-permute-start | bytes 196616 | tf_op jit(solution)/shard_map/ppermute | solution.py:42
  78.9 0.9 solve.1
  79.9 0.1 collective-permute-start.20
  79.9 3.8 %collective-permute-start.15 = (f32[256,128]{1,0:T(8,128)S(1)}, f32[256,128]{1,0:T(8,128)S(1)}, u32[]{:S(2)}, u32[]{:S(2)}) collective-permute-start(f32[256,128]{1,0:T(8,128)S(1)} %get-tuple-element.42.refs_3_), channel_id=1, source_target_pairs={{0,6},{1,7},{2,0},{3,1},{4,2},{5,3},{6,4},{7,5},{8,14},{9,15},{10,... | collective-permute-start | bytes 393224 | tf_op jit(solution)/shard_map/ppermute | solution.py:42
  83.7 0.4 collective-permute-start.14
  84.1 1.6 %collective-permute-start.28 = (f32[128,128]{1,0:T(8,128)S(1)}, f32[128,128]{1,0:T(8,128)S(1)}, u32[]{:S(2)}, u32[]{:S(2)}) collective-permute-start(f32[128,128]{1,0:T(8,128)S(1)} %add.110), channel_id=1, source_target_pairs={{0,4},{1,5},{2,6},{3,7},{4,0},{5,1},{6,2},{7,3},{8,12},{9,13},{10,... | collective-permute-start | bytes 196616 | tf_op jit(solution)/shard_map/ppermute | solution.py:42
  85.7 9.1 %collective-permute-done.28 = f32[128,128]{1,0:T(8,128)S(1)} collective-permute-done((f32[128,128]{1,0:T(8,128)S(1)}, f32[128,128]{1,0:T(8,128)S(1)}, u32[]{:S(2)}, u32[]{:S(2)}) %collective-permute-start.28) | collective-permute-done | bytes 65568 | tf_op jit(solution)/shard_map/ppermute | solution.py:42
  94.8 1.4 %collective-permute-start.19 = (f32[256,128]{1,0:T(8,128)S(1)}, f32[256,128]{1,0:T(8,128)S(1)}, u32[]{:S(2)}, u32[]{:S(2)}) collective-permute-start(f32[256,128]{1,0:T(8,128)S(1)} %get-tuple-element.43.refs_0_), channel_id=1, source_target_pairs={{0,6},{1,7},{2,0},{3,1},{4,2},{5,3},{6,4},{7,5},{8,14},{9,15},{10,... | collective-permute-start | bytes 393224 | tf_op jit(solution)/shard_map/ppermute | solution.py:42
  96.2 0.2 collective-permute-start.26
  96.5 0.3 collective-permute-start.29
  96.8 1.0 collective-permute-done.29
  97.8 0.6 collective-permute-start.17
  98.4 3.2 %collective-permute-start.18 = (f32[256,128]{1,0:T(8,128)S(1)}, f32[256,128]{1,0:T(8,128)S(1)}, u32[]{:S(2)}, u32[]{:S(2)}) collective-permute-start(f32[256,128]{1,0:T(8,128)S(1)} %collective-permute-done.15.refs_4_), channel_id=1, source_target_pairs={{0,6},{1,7},{2,0},{3,1},{4,2},{5,3},{6,4},{7,5},{8,14},{9,15},{10,... | collective-permute-start | bytes 393224 | tf_op jit(solution)/shard_map/ppermute | solution.py:42
  101.6 0.5 collective-permute-start.23
  102.2 0.1 pad_add_fusion.ids_ref
  102.3 0.9 gram.1
  103.2 0.3 collective-permute-done.22.refs_7_
  103.5 2.2 %place.2.refs_0_ = f32[4,4,2,1,128,128]{5,4,3,2,1,0:T(8,128)} custom-call(s32[8]{0:T(128)S(1)} %pad_add_fusion.ids_ref, f32[256,128]{1,0:T(8,128)S(1)} %get-tuple-element.43.refs_0_, f32[256,128]{1,0:T(8,128)S(1)} %collective-permute-done.19.refs_1_, f32[256,128]{1,0:T(8,128)S(1)} %collective-permute-done.14.refs_2_, ...), custom_call_target="tpu_custom_call" | custom-call | tf_op jit(solution)/shard_map/place/pallas_call | solution.py:424
  105.7 0.3 collective-permute-done.17.refs_1_
  106.0 0.7 collective-permute-done.18.refs_2_
  106.6 0.5 collective-permute-start.31
  107.1 0.8 collective-permute-done.30.refs_3_
  108.0 0.2 collective-permute-done.31.refs_4_
  108.2 1.5 %place.3 = f32[4,4,2,1,128,128]{5,4,3,2,1,0:T(8,128)} custom-call(s32[8]{0:T(128)S(1)} %pad_add_fusion.ids_ref, f32[4,4,2,1,128,128]{5,4,3,2,1,0:T(8,128)} %place.2.refs_0_, f32[256,128]{1,0:T(8,128)S(1)} %collective-permute-done.17.refs_1_, f32[256,128]{1,0:T(8,128)S(1)} %collective-permute-done.18.refs_2_, ...), custom_call_target="tpu_custom_call", output_to_operand_aliasing={{}: (1, {})} | custom-call | tf_op jit(solution)/shard_map/place/pallas_call | solution.py:424
  (53 shorter events, 0.7 us)
Async XLA Ops:
  0.6 5.4 %copy-start.3 = (s32[16]{0:T(128)S(1)}, s32[16]{0:T(128)}, u32[]{:S(2)}) copy-start(s32[16]{0:T(128)} %constant.70.clone) | copy-start | bytes 196
  0.6 5.4 %copy-start.4 = (s32[16]{0:T(128)S(1)}, s32[16]{0:T(128)}, u32[]{:S(2)}) copy-start(s32[16]{0:T(128)} %constant.69.clone) | copy-start | bytes 196
  0.7 5.4 %copy-start = (f32[32,128,128]{2,1,0:T(8,128)S(1)}, f32[32,128,128]{2,1,0:T(8,128)}, u32[]{:S(2)}) copy-start(f32[32,128,128]{2,1,0:T(8,128)} %param.7) | copy-start | bytes 6291460
  3.0 29.1 %collective-permute-start = (f32[2048,128]{1,0:T(8,128)}, f32[2048,128]{1,0:T(8,128)S(1)}, u32[]{:S(2)}, u32[]{:S(2)}) collective-permute-start(f32[2048,128]{1,0:T(8,128)} %bitcast.17), channel_id=1, source_target_pairs={{0,8},{1,16},{2,24},{3,0},{4,12},{5,20},{6,28},{7,4},{8,25},{9,1},... | collective-permute-start | bytes 3145736 | tf_op jit(solution)/shard_map/ppermute | solution.py:42
  6.1 23.0 %copy-start.2 = (f32[128,128]{1,0:T(8,128)S(1)}, f32[128,128]{1,0:T(8,128)}, u32[]{:S(2)}) copy-start(f32[128,128]{1,0:T(8,128)} %d_ref.1) | copy-start | bytes 196612
  25.0 12.8 %collective-permute-start.2 = (f32[512,128]{1,0:T(8,128)S(1)}, f32[512,128]{1,0:T(8,128)S(1)}, u32[]{:S(2)}, u32[]{:S(2)}) collective-permute-start(f32[512,128]{1,0:T(8,128)S(1)} %get-tuple-element.25.refs_1_), channel_id=1, source_target_pairs={{0,8},{1,9},{2,10},{3,11},{4,12},{5,13},{6,14},{7,15},{8,0},{9,1},... | collective-permute-start | bytes 786440 | tf_op jit(solution)/shard_map/ppermute | solution.py:42
  26.1 14.5 %collective-permute-start.3 = (f32[512,128]{1,0:T(8,128)S(1)}, f32[512,128]{1,0:T(8,128)S(1)}, u32[]{:S(2)}, u32[]{:S(2)}) collective-permute-start(f32[512,128]{1,0:T(8,128)S(1)} %get-tuple-element.26.refs_2_), channel_id=1, source_target_pairs={{0,16},{1,17},{2,18},{3,19},{4,20},{5,21},{6,22},{7,23},{8,24},{9,... | collective-permute-start | bytes 786440 | tf_op jit(solution)/shard_map/ppermute | solution.py:42
  27.6 14.1 %collective-permute-start.4 = (f32[512,128]{1,0:T(8,128)S(1)}, f32[512,128]{1,0:T(8,128)S(1)}, u32[]{:S(2)}, u32[]{:S(2)}) collective-permute-start(f32[512,128]{1,0:T(8,128)S(1)} %get-tuple-element.27.refs_3_), channel_id=1, source_target_pairs={{0,24},{1,25},{2,26},{3,27},{4,28},{5,29},{6,30},{7,31},{8,16},{9,... | collective-permute-start | bytes 786440 | tf_op jit(solution)/shard_map/ppermute | solution.py:42
  32.1 2.9 %copy-start.1 = (f32[32,128,128]{2,1,0:T(8,128)S(1)}, f32[32,128,128]{2,1,0:T(8,128)}, u32[]{:S(2)}) copy-start(f32[32,128,128]{2,1,0:T(8,128)} %param.8) | copy-start | bytes 6291460
  35.0 7.5 %collective-permute-start.1 = (f32[512,128]{1,0:T(8,128)S(1)}, f32[512,128]{1,0:T(8,128)S(1)}, u32[]{:S(2)}, u32[]{:S(2)}) collective-permute-start(f32[512,128]{1,0:T(8,128)S(1)} %get-tuple-element.23), channel_id=1, source_target_pairs={{0,1},{1,0},{2,3},{3,2},{4,5},{5,4},{6,7},{7,6},{8,9},{9,8},{10,11... | collective-permute-start | bytes 786440 | tf_op jit(solution)/shard_map/ppermute | solution.py:42
  36.4 6.0 %collective-permute-start.5 = (f32[128,128]{1,0:T(8,128)S(1)}, f32[128,128]{1,0:T(8,128)S(1)}, u32[]{:S(2)}, u32[]{:S(2)}) collective-permute-start(f32[128,128]{1,0:T(8,128)S(1)} %moment.1), channel_id=1, source_target_pairs={{0,8},{1,9},{2,10},{3,11},{4,12},{5,13},{6,14},{7,15},{8,0},{9,1},... | collective-permute-start | bytes 196616 | tf_op jit(solution)/shard_map/ppermute | solution.py:42
  48.0 3.2 %collective-permute-start.7 = (f32[512,128]{1,0:T(8,128)S(1)}, f32[512,128]{1,0:T(8,128)S(1)}, u32[]{:S(2)}, u32[]{:S(2)}) collective-permute-start(f32[512,128]{1,0:T(8,128)S(1)} %get-tuple-element.40), channel_id=1, source_target_pairs={{0,1},{1,0},{2,3},{3,2},{4,5},{5,4},{6,7},{7,6},{8,9},{9,8},{10,11... | collective-permute-start | bytes 786440 | tf_op jit(solution)/shard_map/ppermute | solution.py:42
  48.0 3.1 %collective-permute-start.6 = (f32[512,128]{1,0:T(8,128)S(1)}, f32[512,128]{1,0:T(8,128)S(1)}, u32[]{:S(2)}, u32[]{:S(2)}) collective-permute-start(f32[512,128]{1,0:T(8,128)S(1)} %get-tuple-element.41), channel_id=1, source_target_pairs={{0,1},{1,0},{2,3},{3,2},{4,5},{5,4},{6,7},{7,6},{8,9},{9,8},{10,11... | collective-permute-start | bytes 786440 | tf_op jit(solution)/shard_map/ppermute | solution.py:42
  48.5 16.0 %collective-permute-start.10 = (f32[512,128]{1,0:T(8,128)S(1)}, f32[512,128]{1,0:T(8,128)S(1)}, u32[]{:S(2)}, u32[]{:S(2)}) collective-permute-start(f32[512,128]{1,0:T(8,128)S(1)} %add.99.refs_0_), channel_id=1, source_target_pairs={{0,4},{1,5},{2,6},{3,7},{4,0},{5,1},{6,2},{7,3},{8,12},{9,13},{10,... | collective-permute-start | bytes 786440 | tf_op jit(solution)/shard_map/ppermute | solution.py:42
  51.2 18.5 %collective-permute-start.12 = (f32[512,128]{1,0:T(8,128)S(1)}, f32[512,128]{1,0:T(8,128)S(1)}, u32[]{:S(2)}, u32[]{:S(2)}) collective-permute-start(f32[512,128]{1,0:T(8,128)S(1)} %get-tuple-element.38.refs_1_), channel_id=1, source_target_pairs={{0,6},{1,7},{2,0},{3,1},{4,2},{5,3},{6,4},{7,5},{8,14},{9,15},{10,... | collective-permute-start | bytes 786440 | tf_op jit(solution)/shard_map/ppermute | solution.py:42
  52.9 17.2 %collective-permute-start.11 = (f32[512,128]{1,0:T(8,128)S(1)}, f32[512,128]{1,0:T(8,128)S(1)}, u32[]{:S(2)}, u32[]{:S(2)}) collective-permute-start(f32[512,128]{1,0:T(8,128)S(1)} %get-tuple-element.39.refs_0_), channel_id=1, source_target_pairs={{0,2},{1,3},{2,4},{3,5},{4,6},{5,7},{6,0},{7,1},{8,10},{9,11},{10,... | collective-permute-start | bytes 786440 | tf_op jit(solution)/shard_map/ppermute | solution.py:42
  59.5 19.3 %collective-permute-start.8 = (f32[512,128]{1,0:T(8,128)S(1)}, f32[512,128]{1,0:T(8,128)S(1)}, u32[]{:S(2)}, u32[]{:S(2)}) collective-permute-start(f32[512,128]{1,0:T(8,128)S(1)} %get-tuple-element.31), channel_id=1, source_target_pairs={{0,1},{1,0},{2,3},{3,2},{4,5},{5,4},{6,7},{7,6},{8,9},{9,8},{10,11... | collective-permute-start | bytes 786440 | tf_op jit(solution)/shard_map/ppermute | solution.py:42
  59.6 19.3 %collective-permute-start.9 = (f32[512,128]{1,0:T(8,128)S(1)}, f32[512,128]{1,0:T(8,128)S(1)}, u32[]{:S(2)}, u32[]{:S(2)}) collective-permute-start(f32[512,128]{1,0:T(8,128)S(1)} %add_add_fusion.refs_1_), channel_id=1, source_target_pairs={{0,0},{1,8},{2,16},{3,24},{4,4},{5,12},{6,20},{7,28},{8,1},{9,9},{... | collective-permute-start | bytes 786440 | tf_op jit(solution)/shard_map/ppermute | solution.py:42
  64.5 5.6 %collective-permute-start.16 = (f32[128,128]{1,0:T(8,128)S(1)}, f32[128,128]{1,0:T(8,128)S(1)}, u32[]{:S(2)}, u32[]{:S(2)}) collective-permute-start(f32[128,128]{1,0:T(8,128)S(1)} %add.103.refs_2_), channel_id=1, source_target_pairs={{0,16},{1,17},{2,18},{3,19},{4,20},{5,21},{6,22},{7,23},{8,24},{9,... | collective-permute-start | bytes 196616 | tf_op jit(solution)/shard_map/ppermute | solution.py:42
  70.1 8.8 %collective-permute-start.13 = (f32[8,128]{1,0:T(8,128)S(1)}, f32[8,128]{1,0:T(8,128)S(1)}, u32[]{:S(2)}, u32[]{:S(2)}) collective-permute-start(f32[8,128]{1,0:T(8,128)S(1)} %slice_add_fusion.2), channel_id=1, source_target_pairs={{0,1},{1,0},{2,3},{3,2},{4,5},{5,4},{6,7},{7,6},{8,9},{9,8},{10,11... | collective-permute-start | bytes 12296 | tf_op jit(solution)/shard_map/ppermute | solution.py:42
  70.1 14.0 %collective-permute-start.27 = (f32[128,128]{1,0:T(8,128)S(1)}, f32[128,128]{1,0:T(8,128)S(1)}, u32[]{:S(2)}, u32[]{:S(2)}) collective-permute-start(f32[128,128]{1,0:T(8,128)S(1)} %add.109), channel_id=1, source_target_pairs={{0,2},{1,3},{2,0},{3,1},{4,6},{5,7},{6,4},{7,5},{8,10},{9,11},{10,... | collective-permute-start | bytes 196616 | tf_op jit(solution)/shard_map/ppermute | solution.py:42
  79.9 15.0 %collective-permute-start.20 = (f32[256,128]{1,0:T(8,128)S(1)}, f32[256,128]{1,0:T(8,128)S(1)}, u32[]{:S(2)}, u32[]{:S(2)}) collective-permute-start(f32[256,128]{1,0:T(8,128)S(1)} %get-tuple-element.42.refs_3_), channel_id=1, source_target_pairs={{0,2},{1,3},{2,4},{3,5},{4,6},{5,7},{6,0},{7,1},{8,10},{9,11},{10,... | collective-permute-start | bytes 393224 | tf_op jit(solution)/shard_map/ppermute | solution.py:42
  79.9 16.3 %collective-permute-start.15 = (f32[256,128]{1,0:T(8,128)S(1)}, f32[256,128]{1,0:T(8,128)S(1)}, u32[]{:S(2)}, u32[]{:S(2)}) collective-permute-start(f32[256,128]{1,0:T(8,128)S(1)} %get-tuple-element.42.refs_3_), channel_id=1, source_target_pairs={{0,6},{1,7},{2,0},{3,1},{4,2},{5,3},{6,4},{7,5},{8,14},{9,15},{10,... | collective-permute-start | bytes 393224 | tf_op jit(solution)/shard_map/ppermute | solution.py:42
  83.7 12.7 %collective-permute-start.14 = (f32[256,128]{1,0:T(8,128)S(1)}, f32[256,128]{1,0:T(8,128)S(1)}, u32[]{:S(2)}, u32[]{:S(2)}) collective-permute-start(f32[256,128]{1,0:T(8,128)S(1)} %get-tuple-element.43.refs_0_), channel_id=1, source_target_pairs={{0,2},{1,3},{2,4},{3,5},{4,6},{5,7},{6,0},{7,1},{8,10},{9,11},{10,... | collective-permute-start | bytes 393224 | tf_op jit(solution)/shard_map/ppermute | solution.py:42
  84.1 10.7 %collective-permute-start.28 = (f32[128,128]{1,0:T(8,128)S(1)}, f32[128,128]{1,0:T(8,128)S(1)}, u32[]{:S(2)}, u32[]{:S(2)}) collective-permute-start(f32[128,128]{1,0:T(8,128)S(1)} %add.110), channel_id=1, source_target_pairs={{0,4},{1,5},{2,6},{3,7},{4,0},{5,1},{6,2},{7,3},{8,12},{9,13},{10,... | collective-permute-start | bytes 196616 | tf_op jit(solution)/shard_map/ppermute | solution.py:42
  85.7 12.7 %collective-permute-start.24 = (f32[256,128]{1,0:T(8,128)S(1)}, f32[256,128]{1,0:T(8,128)S(1)}, u32[]{:S(2)}, u32[]{:S(2)}) collective-permute-start(f32[256,128]{1,0:T(8,128)S(1)} %get-tuple-element.42.refs_3_), channel_id=1, source_target_pairs={{0,1},{1,0},{2,3},{3,2},{4,5},{5,4},{6,7},{7,6},{8,9},{9,8},{10,11... | collective-permute-start | bytes 393224 | tf_op jit(solution)/shard_map/ppermute | solution.py:42
  94.8 6.8 %collective-permute-start.21 = (f32[256,128]{1,0:T(8,128)S(1)}, f32[256,128]{1,0:T(8,128)S(1)}, u32[]{:S(2)}, u32[]{:S(2)}) collective-permute-start(f32[256,128]{1,0:T(8,128)S(1)} %get-tuple-element.43.refs_0_), channel_id=1, source_target_pairs={{0,1},{1,0},{2,3},{3,2},{4,5},{5,4},{6,7},{7,6},{8,9},{9,8},{10,11... | collective-permute-start | bytes 393224 | tf_op jit(solution)/shard_map/ppermute | solution.py:42
  94.8 6.8 %collective-permute-start.19 = (f32[256,128]{1,0:T(8,128)S(1)}, f32[256,128]{1,0:T(8,128)S(1)}, u32[]{:S(2)}, u32[]{:S(2)}) collective-permute-start(f32[256,128]{1,0:T(8,128)S(1)} %get-tuple-element.43.refs_0_), channel_id=1, source_target_pairs={{0,6},{1,7},{2,0},{3,1},{4,2},{5,3},{6,4},{7,5},{8,14},{9,15},{10,... | collective-permute-start | bytes 393224 | tf_op jit(solution)/shard_map/ppermute | solution.py:42
  96.2 5.9 %collective-permute-start.26 = (f32[256,128]{1,0:T(8,128)S(1)}, f32[256,128]{1,0:T(8,128)S(1)}, u32[]{:S(2)}, u32[]{:S(2)}) collective-permute-start(f32[256,128]{1,0:T(8,128)S(1)} %collective-permute-done.20.refs_5_), channel_id=1, source_target_pairs={{0,1},{1,0},{2,3},{3,2},{4,5},{5,4},{6,7},{7,6},{8,9},{9,8},{10,11... | collective-permute-start | bytes 393224 | tf_op jit(solution)/shard_map/ppermute | solution.py:42
  96.5 1.3 %collective-permute-start.29 = (f32[128,128]{1,0:T(8,128)S(1)}, f32[128,128]{1,0:T(8,128)S(1)}, u32[]{:S(2)}, u32[]{:S(2)}) collective-permute-start(f32[128,128]{1,0:T(8,128)S(1)} %add.111), channel_id=1, source_target_pairs={{0,1},{1,0},{2,3},{3,2},{4,5},{5,4},{6,7},{7,6},{8,9},{9,8},{10,11... | collective-permute-start | bytes 196616 | tf_op jit(solution)/shard_map/ppermute | solution.py:42
  97.8 8.2 %collective-permute-start.17 = (f32[256,128]{1,0:T(8,128)S(1)}, f32[256,128]{1,0:T(8,128)S(1)}, u32[]{:S(2)}, u32[]{:S(2)}) collective-permute-start(f32[256,128]{1,0:T(8,128)S(1)} %collective-permute-done.14.refs_2_), channel_id=1, source_target_pairs={{0,2},{1,3},{2,4},{3,5},{4,6},{5,7},{6,0},{7,1},{8,10},{9,11},{10,... | collective-permute-start | bytes 393224 | tf_op jit(solution)/shard_map/ppermute | solution.py:42
  98.4 8.2 %collective-permute-start.18 = (f32[256,128]{1,0:T(8,128)S(1)}, f32[256,128]{1,0:T(8,128)S(1)}, u32[]{:S(2)}, u32[]{:S(2)}) collective-permute-start(f32[256,128]{1,0:T(8,128)S(1)} %collective-permute-done.15.refs_4_), channel_id=1, source_target_pairs={{0,6},{1,7},{2,0},{3,1},{4,2},{5,3},{6,4},{7,5},{8,14},{9,15},{10,... | collective-permute-start | bytes 393224 | tf_op jit(solution)/shard_map/ppermute | solution.py:42
  101.6 1.6 %collective-permute-start.25 = (f32[256,128]{1,0:T(8,128)S(1)}, f32[256,128]{1,0:T(8,128)S(1)}, u32[]{:S(2)}, u32[]{:S(2)}) collective-permute-start(f32[256,128]{1,0:T(8,128)S(1)} %collective-permute-done.15.refs_4_), channel_id=1, source_target_pairs={{0,1},{1,0},{2,3},{3,2},{4,5},{5,4},{6,7},{7,6},{8,9},{9,8},{10,11... | collective-permute-start | bytes 393224 | tf_op jit(solution)/shard_map/ppermute | solution.py:42
  101.6 1.9 %collective-permute-start.23 = (f32[256,128]{1,0:T(8,128)S(1)}, f32[256,128]{1,0:T(8,128)S(1)}, u32[]{:S(2)}, u32[]{:S(2)}) collective-permute-start(f32[256,128]{1,0:T(8,128)S(1)} %collective-permute-done.14.refs_2_), channel_id=1, source_target_pairs={{0,1},{1,0},{2,3},{3,2},{4,5},{5,4},{6,7},{7,6},{8,9},{9,8},{10,11... | collective-permute-start | bytes 393224 | tf_op jit(solution)/shard_map/ppermute | solution.py:42
  102.1 1.3 %collective-permute-start.22 = (f32[256,128]{1,0:T(8,128)S(1)}, f32[256,128]{1,0:T(8,128)S(1)}, u32[]{:S(2)}, u32[]{:S(2)}) collective-permute-start(f32[256,128]{1,0:T(8,128)S(1)} %collective-permute-done.19.refs_1_), channel_id=1, source_target_pairs={{0,1},{1,0},{2,3},{3,2},{4,5},{5,4},{6,7},{7,6},{8,9},{9,8},{10,11... | collective-permute-start | bytes 393224 | tf_op jit(solution)/shard_map/ppermute | solution.py:42
  106.6 1.3 %collective-permute-start.30 = (f32[256,128]{1,0:T(8,128)S(1)}, f32[256,128]{1,0:T(8,128)S(1)}, u32[]{:S(2)}, u32[]{:S(2)}) collective-permute-start(f32[256,128]{1,0:T(8,128)S(1)} %collective-permute-done.17.refs_1_), channel_id=1, source_target_pairs={{0,1},{1,0},{2,3},{3,2},{4,5},{5,4},{6,7},{7,6},{8,9},{9,8},{10,11... | collective-permute-start | bytes 393224 | tf_op jit(solution)/shard_map/ppermute | solution.py:42
  106.6 1.5 %collective-permute-start.31 = (f32[256,128]{1,0:T(8,128)S(1)}, f32[256,128]{1,0:T(8,128)S(1)}, u32[]{:S(2)}, u32[]{:S(2)}) collective-permute-start(f32[256,128]{1,0:T(8,128)S(1)} %collective-permute-done.18.refs_2_), channel_id=1, source_target_pairs={{0,1},{1,0},{2,3},{3,2},{4,5},{5,4},{6,7},{7,6},{8,9},{9,8},{10,11... | collective-permute-start | bytes 393224 | tf_op jit(solution)/shard_map/ppermute | solution.py:42

commit v4 on v3

--- a/solution.py
+++ b/solution.py
@@ -565,7 +565,7 @@
         below, above = [move(b, up) for b in below], [move(a, down) for a in above]
         lower[-distance % n_z], upper[-distance % n_z] = below
         upper[distance], lower[distance] = above
-    (go_up, go_down), _ = lax.optimization_barrier(((below[0], above[0]), moments[row_steps]))
+    go_up, go_down = below[0], above[0]
     lower[plan.far], upper[plan.far] = move(go_up, up), move(go_down, down)
     order = (z + jnp.arange(n_z, dtype=jnp.int32)) % n_z * 2
     place_ids = jnp.concatenate([order + core, order + (1 - core)])

time: 110 us -> 108 us (0.982)
  starting transfers between devices: 36.3 us -> 31.8 us
  waiting for transfers between devices: 26.4 us -> 28.3 us
    ppermute x32, starting transfers between devices: 36.3 us -> 31.8 us  [send(): return lax.ppermute(x, AXES, pairs)]
    ppermute x32, waiting for transfers between devices: 26.4 us -> 28.3 us  [send(): return lax.ppermute(x, AXES, pairs)]
  transfers between devices with their start and end apart: 32 -> 32, of which waited for: 13 -> 14; matrix products, arithmetic and copies ran while one was open for 0% -> 0% of each run, Pallas kernels for 33% -> 34%
where the time goes in v4:
time: 108 us; the launch traced here: 107 us
  Pallas kernels  45.7 us (42%)
  starting transfers between devices  31.8 us (29%)
  waiting for transfers between devices  28.3 us (26%)
    ppermute x32, starting transfers between devices, send(): return lax.ppermute(x, AXES, pairs)  31.8 us
    ppermute x32, waiting for transfers between devices, send(): return lax.ppermute(x, AXES, pairs)  28.3 us
    pallas_call x1, Pallas kernels, flip_parts(): pl.pallas_call(functools.partial(flip_body, plan, n_row), grid_spec=pltpu...  18.9 us
    pallas_call x2, Pallas kernels, direct_kept(): pl.pallas_call(functools.partial(kept_body, first, half), grid=(2 * half,...  8.21 us
    pallas_call x1, Pallas kernels, direct_chunks(): pl.pallas_call(functools.partial(direct_body, n_blocks, group, half), gri...  6.23 us
    pallas_call x2, Pallas kernels, place(): pl.pallas_call(functools.partial(place_body, plan, [piece[1:] for piece i...  3.7 us
    pallas_call x1, Pallas kernels, inverse(): pl.pallas_call(inverse_body, out_shape=jax.ShapeDtypeStruct(diag_block.sh...  3.09 us
    pallas_call x1, Pallas kernels, choose(): pl.pallas_call(body, grid_spec=pltpu.PrefetchScalarGridSpec(num_scalar_pr...  2.35 us
  transfers between devices with their start and end apart: 32, of which 14 were waited for; matrix products, arithmetic and copies ran while one was open for 0% of the time, Pallas kernels for 34%

profile of v4, /device:TPU:0, one launch (start us, length us, event | category | flops | bytes accessed | tf_op | source)
XLA Modules:
  0.0 107.2 jit_solution(14001423500040302720)
XLA Ops:
  0.7 2.4 %choose.1 = f32[16,128,128]{2,1,0:T(8,128)} custom-call(s32[1]{0:T(128)} %bitcast.1.which_ref, f32[16,2,128,128]{3,2,1,0:T(8,128)} %bitcast.9), custom_call_target="tpu_custom_call" | custom-call | tf_op jit(solution)/shard_map/choose/pallas_call | solution.py:53
  3.0 3.0 %collective-permute-start = (f32[2048,128]{1,0:T(8,128)}, f32[2048,128]{1,0:T(8,128)S(1)}, u32[]{:S(2)}, u32[]{:S(2)}) collective-permute-start(f32[2048,128]{1,0:T(8,128)} %bitcast.17), channel_id=1, source_target_pairs={{0,8},{1,16},{2,24},{3,0},{4,12},{5,20},{6,28},{7,4},{8,25},{9,1},... | collective-permute-start | bytes 3145736 | tf_op jit(solution)/shard_map/ppermute | solution.py:42
  6.1 18.9 %flip.1 = (f32[512,128]{1,0:T(8,128)S(1)}, f32[512,128]{1,0:T(8,128)S(1)}, f32[512,128]{1,0:T(8,128)S(1)}, f32[512,128]{1,0:T(8,128)S(1)}, bf16[3072,2048]{1,0:T...) custom-call(s32[1]{0:T(128)} %bitcast.4.me_ref, s32[16]{0:T(128)S(1)} %fusion.2.ids_ref, ...), custom_call_target="tpu_custom_call" | custom-call | flops 6442450944 | bytes 33554432 | tf_op jit(solution)/shard_map/flip/pallas_call | solution.py:135
  25.0 1.0 collective-permute-start.2
  26.1 1.6 %collective-permute-start.3 = (f32[512,128]{1,0:T(8,128)S(1)}, f32[512,128]{1,0:T(8,128)S(1)}, u32[]{:S(2)}, u32[]{:S(2)}) collective-permute-start(f32[512,128]{1,0:T(8,128)S(1)} %get-tuple-element.24.refs_2_), channel_id=1, source_target_pairs={{0,16},{1,17},{2,18},{3,19},{4,20},{5,21},{6,22},{7,23},{8,24},{9,... | collective-permute-start | bytes 786440 | tf_op jit(solution)/shard_map/ppermute | solution.py:42
  27.6 1.4 %collective-permute-start.4 = (f32[512,128]{1,0:T(8,128)S(1)}, f32[512,128]{1,0:T(8,128)S(1)}, u32[]{:S(2)}, u32[]{:S(2)}) collective-permute-start(f32[512,128]{1,0:T(8,128)S(1)} %get-tuple-element.25.refs_3_), channel_id=1, source_target_pairs={{0,24},{1,25},{2,26},{3,27},{4,28},{5,29},{6,30},{7,31},{8,16},{9,... | collective-permute-start | bytes 786440 | tf_op jit(solution)/shard_map/ppermute | solution.py:42
  29.0 3.1 %inverse.1.refs_0_.refs_5_.inv_ref = f32[128,128]{1,0:T(8,128)S(1)} custom-call(f32[128,128]{1,0:T(8,128)S(1)} %copy-done.2), custom_call_target="tpu_custom_call" | custom-call | tf_op jit(solution)/shard_map/inverse/pallas_call | solution.py:297
  32.2 2.8 %direct_kept.2 = (f32[512,128]{1,0:T(8,128)S(1)}, f32[512,128]{1,0:T(8,128)S(1)}) custom-call(bf16[3072,2048]{1,0:T(8,128)(2,1)S(1)} %get-tuple-element.18.high_ref, bf16[3072,2048]{1,0:T(8,128)(2,1)S(1)} %get-tuple-element.19.low_ref, f32[2048,128]{1,0:T(8,128)S(1)} %collective-permute-done.p_ref.refs_4_, f32[128,128]{1,0:T(8,128)S(1)} %inverse.1.refs_0_.refs_5_.inv_ref), custom_call_target="tpu_custom_call" | custom-call | flops 1 | bytes 1 | tf_op jit(solution)/shard_map/direct_kept/pallas_call | solution.py:263
  35.1 1.4 %moment.1 = f32[128,128]{1,0:T(8,128)S(1)} custom-call(s32[16]{0:T(128)S(1)} %fusion.2.ids_ref, s32[1]{0:T(128)} %bitcast.4.me_ref, f32[512,128]{1,0:T(8,128)S(1)} %get-tuple-element.22.refs_0_, f32[512,128]{1,0:T(8,128)S(1)} %get-tuple-element.23.refs_1_, f32[512,128]{1,0:T(8,128)S(1)} %get-tuple-element.24.refs_2_, ...), custom_call_target="tpu_custom_call" | custom-call | tf_op jit(solution)/shard_map/moment/pallas_call | solution.py:335
  36.4 1.3 %collective-permute-start.5 = (f32[128,128]{1,0:T(8,128)S(1)}, f32[128,128]{1,0:T(8,128)S(1)}, u32[]{:S(2)}, u32[]{:S(2)}) collective-permute-start(f32[128,128]{1,0:T(8,128)S(1)} %moment.1), channel_id=1, source_target_pairs={{0,8},{1,9},{2,10},{3,11},{4,12},{5,13},{6,14},{7,15},{8,0},{9,1},... | collective-permute-start | bytes 196616 | tf_op jit(solution)/shard_map/ppermute | solution.py:42
  37.8 2.7 %collective-permute-done.3 = f32[512,128]{1,0:T(8,128)S(1)} collective-permute-done((f32[512,128]{1,0:T(8,128)S(1)}, f32[512,128]{1,0:T(8,128)S(1)}, u32[]{:S(2)}, u32[]{:S(2)}) %collective-permute-start.3) | collective-permute-done | bytes 262176 | tf_op jit(solution)/shard_map/ppermute | solution.py:42
  40.5 1.2 %collective-permute-done.4 = f32[512,128]{1,0:T(8,128)S(1)} collective-permute-done((f32[512,128]{1,0:T(8,128)S(1)}, f32[512,128]{1,0:T(8,128)S(1)}, u32[]{:S(2)}, u32[]{:S(2)}) %collective-permute-start.4) | collective-permute-done | bytes 262176 | tf_op jit(solution)/shard_map/ppermute | solution.py:42
  41.7 0.1 add_add_fusion.refs_1_
  41.8 0.6 collective-permute-done.5
  42.5 5.4 %direct_kept.3 = (f32[1024,128]{1,0:T(8,128)S(1)}, f32[1024,128]{1,0:T(8,128)S(1)}) custom-call(bf16[3072,2048]{1,0:T(8,128)(2,1)S(1)} %get-tuple-element.18.high_ref, bf16[3072,2048]{1,0:T(8,128)(2,1)S(1)} %get-tuple-element.19.low_ref, f32[2048,128]{1,0:T(8,128)S(1)} %collective-permute-done.p_ref.refs_4_, f32[512,128]{1,0:T(8,128)S(1)} %add.99.refs_0_, ...), custom_call_target="tpu_custom_call" | custom-call | flops 1 | bytes 1 | tf_op jit(solution)/shard_map/direct_kept/pallas_call | solution.py:263
  48.0 0.5 collective-permute-start.6
  48.5 2.6 %collective-permute-start.10 = (f32[512,128]{1,0:T(8,128)S(1)}, f32[512,128]{1,0:T(8,128)S(1)}, u32[]{:S(2)}, u32[]{:S(2)}) collective-permute-start(f32[512,128]{1,0:T(8,128)S(1)} %add.99.refs_0_), channel_id=1, source_target_pairs={{0,4},{1,5},{2,6},{3,7},{4,0},{5,1},{6,2},{7,3},{8,12},{9,13},{10,... | collective-permute-start | bytes 786440 | tf_op jit(solution)/shard_map/ppermute | solution.py:42
  51.2 1.7 %collective-permute-start.12 = (f32[512,128]{1,0:T(8,128)S(1)}, f32[512,128]{1,0:T(8,128)S(1)}, u32[]{:S(2)}, u32[]{:S(2)}) collective-permute-start(f32[512,128]{1,0:T(8,128)S(1)} %get-tuple-element.34.refs_1_), channel_id=1, source_target_pairs={{0,6},{1,7},{2,0},{3,1},{4,2},{5,3},{6,4},{7,5},{8,14},{9,15},{10,... | collective-permute-start | bytes 786440 | tf_op jit(solution)/shard_map/ppermute | solution.py:42
  52.9 0.3 collective-permute-start.11
  53.3 1.9 %collective-permute-start.26 = (f32[128,128]{1,0:T(8,128)S(1)}, f32[128,128]{1,0:T(8,128)S(1)}, u32[]{:S(2)}, u32[]{:S(2)}) collective-permute-start(f32[128,128]{1,0:T(8,128)S(1)} %add.103.refs_2_), channel_id=1, source_target_pairs={{0,16},{1,17},{2,18},{3,19},{4,20},{5,21},{6,22},{7,23},{8,24},{9,... | collective-permute-start | bytes 196616 | tf_op jit(solution)/shard_map/ppermute | solution.py:42
  55.2 6.2 %direct.1 = (f32[512,128]{1,0:T(8,128)S(1)}, f32[512,128]{1,0:T(8,128)S(1)}) custom-call(s32[16]{0:T(128)S(1)} %fusion.2.ids_ref, f32[4,4,2,1,2048,128]{5,4,3,2,1,0:T(8,128)} %bitcast.15, f32[2048,128]{1,0:T(8,128)S(1)} %collective-permute-done.p_ref.refs_4_, f32[512,128]{1,0:T(8,128)S(1)} %get-tuple-element.35.refs_0_, f32[512,128]{1,0:T(8,128)S(1)} %get-tuple-element.34.refs_1_), custom_call_target="tpu_custom_call" | custom-call | flops 1 | bytes 1 | tf_op jit(solution)/shard_map/direct/pallas_call | solution.py:211
  61.5 0.7 collective-permute-start.9
  62.2 2.3 %collective-permute-done.10.refs_2_ = f32[512,128]{1,0:T(8,128)S(1)} collective-permute-done((f32[512,128]{1,0:T(8,128)S(1)}, f32[512,128]{1,0:T(8,128)S(1)}, u32[]{:S(2)}, u32[]{:S(2)}) %collective-permute-start.10) | collective-permute-done | bytes 262176 | tf_op jit(solution)/shard_map/ppermute | solution.py:42
  64.5 5.2 %collective-permute-start.27 = (f32[128,128]{1,0:T(8,128)S(1)}, f32[128,128]{1,0:T(8,128)S(1)}, u32[]{:S(2)}, u32[]{:S(2)}) collective-permute-start(f32[128,128]{1,0:T(8,128)S(1)} %add.109), channel_id=1, source_target_pairs={{0,2},{1,3},{2,0},{3,1},{4,6},{5,7},{6,4},{7,5},{8,10},{9,11},{10,... | collective-permute-start | bytes 196616 | tf_op jit(solution)/shard_map/ppermute | solution.py:42
  69.7 0.4 collective-permute-done.11.refs_3_
  70.1 6.7 %collective-permute-done.27 = f32[128,128]{1,0:T(8,128)S(1)} collective-permute-done((f32[128,128]{1,0:T(8,128)S(1)}, f32[128,128]{1,0:T(8,128)S(1)}, u32[]{:S(2)}, u32[]{:S(2)}) %collective-permute-start.27) | collective-permute-done | bytes 65568 | tf_op jit(solution)/shard_map/ppermute | solution.py:42
  76.8 0.5 collective-permute-start.28
  77.4 0.9 solve.1
  78.4 1.7 %collective-permute-start.19 = (f32[256,128]{1,0:T(8,128)S(1)}, f32[256,128]{1,0:T(8,128)S(1)}, u32[]{:S(2)}, u32[]{:S(2)}) collective-permute-start(f32[256,128]{1,0:T(8,128)S(1)} %get-tuple-element.38.refs_3_), channel_id=1, source_target_pairs={{0,2},{1,3},{2,4},{3,5},{4,6},{5,7},{6,0},{7,1},{8,10},{9,11},{10,... | collective-permute-start | bytes 393224 | tf_op jit(solution)/shard_map/ppermute | solution.py:42
  80.1 2.3 %collective-permute-done.28 = f32[128,128]{1,0:T(8,128)S(1)} collective-permute-done((f32[128,128]{1,0:T(8,128)S(1)}, f32[128,128]{1,0:T(8,128)S(1)}, u32[]{:S(2)}, u32[]{:S(2)}) %collective-permute-start.28) | collective-permute-done | bytes 65568 | tf_op jit(solution)/shard_map/ppermute | solution.py:42
  82.5 1.1 collective-permute-start.16
  83.6 0.2 collective-permute-start.20
  83.8 1.0 collective-permute-start.14
  84.8 2.8 %collective-permute-start.18 = (f32[256,128]{1,0:T(8,128)S(1)}, f32[256,128]{1,0:T(8,128)S(1)}, u32[]{:S(2)}, u32[]{:S(2)}) collective-permute-start(f32[256,128]{1,0:T(8,128)S(1)} %get-tuple-element.39.refs_0_), channel_id=1, source_target_pairs={{0,6},{1,7},{2,0},{3,1},{4,2},{5,3},{6,4},{7,5},{8,14},{9,15},{10,... | collective-permute-start | bytes 393224 | tf_op jit(solution)/shard_map/ppermute | solution.py:42
  87.6 2.7 %collective-permute-done.16.refs_4_ = f32[256,128]{1,0:T(8,128)S(1)} collective-permute-done((f32[256,128]{1,0:T(8,128)S(1)}, f32[256,128]{1,0:T(8,128)S(1)}, u32[]{:S(2)}, u32[]{:S(2)}) %collective-permute-start.16) | collective-permute-done | bytes 131104 | tf_op jit(solution)/shard_map/ppermute | solution.py:42
  90.4 1.9 %collective-permute-start.17 = (f32[256,128]{1,0:T(8,128)S(1)}, f32[256,128]{1,0:T(8,128)S(1)}, u32[]{:S(2)}, u32[]{:S(2)}) collective-permute-start(f32[256,128]{1,0:T(8,128)S(1)} %collective-permute-done.16.refs_4_), channel_id=1, source_target_pairs={{0,6},{1,7},{2,0},{3,1},{4,2},{5,3},{6,4},{7,5},{8,14},{9,15},{10,... | collective-permute-start | bytes 393224 | tf_op jit(solution)/shard_map/ppermute | solution.py:42
  92.2 0.9 collective-permute-done.14.refs_2_
  93.1 2.4 %collective-permute-done.18.refs_1_ = f32[256,128]{1,0:T(8,128)S(1)} collective-permute-done((f32[256,128]{1,0:T(8,128)S(1)}, f32[256,128]{1,0:T(8,128)S(1)}, u32[]{:S(2)}, u32[]{:S(2)}) %collective-permute-start.18) | collective-permute-done | bytes 131104 | tf_op jit(solution)/shard_map/ppermute | solution.py:42
  95.5 0.5 collective-permute-start.15
  96.0 0.1 pad_add_fusion.ids_ref
  96.1 0.9 gram.1
  97.0 0.3 collective-permute-done.21.refs_7_
  97.4 2.2 %place.2.refs_0_ = f32[4,4,2,1,128,128]{5,4,3,2,1,0:T(8,128)} custom-call(s32[8]{0:T(128)S(1)} %pad_add_fusion.ids_ref, f32[256,128]{1,0:T(8,128)S(1)} %get-tuple-element.39.refs_0_, f32[256,128]{1,0:T(8,128)S(1)} %collective-permute-done.18.refs_1_, f32[256,128]{1,0:T(8,128)S(1)} %collective-permute-done.14.refs_2_, ...), custom_call_target="tpu_custom_call" | custom-call | tf_op jit(solution)/shard_map/place/pallas_call | solution.py:424
  99.6 4.6 %collective-permute-done.15.refs_1_ = f32[256,128]{1,0:T(8,128)S(1)} collective-permute-done((f32[256,128]{1,0:T(8,128)S(1)}, f32[256,128]{1,0:T(8,128)S(1)}, u32[]{:S(2)}, u32[]{:S(2)}) %collective-permute-start.15) | collective-permute-done | bytes 131104 | tf_op jit(solution)/shard_map/ppermute | solution.py:42
  104.1 0.5 collective-permute-start.31
  104.6 0.8 collective-permute-done.30.refs_3_
  105.5 0.2 collective-permute-done.31.refs_4_
  105.7 1.5 %place.3 = f32[4,4,2,1,128,128]{5,4,3,2,1,0:T(8,128)} custom-call(s32[8]{0:T(128)S(1)} %pad_add_fusion.ids_ref, f32[4,4,2,1,128,128]{5,4,3,2,1,0:T(8,128)} %place.2.refs_0_, f32[256,128]{1,0:T(8,128)S(1)} %collective-permute-done.15.refs_1_, f32[256,128]{1,0:T(8,128)S(1)} %collective-permute-done.17.refs_2_, ...), custom_call_target="tpu_custom_call", output_to_operand_aliasing={{}: (1, {})} | custom-call | tf_op jit(solution)/shard_map/place/pallas_call | solution.py:424
  (53 shorter events, 0.7 us)
Async XLA Ops:
  0.6 5.4 %copy-start.3 = (s32[16]{0:T(128)S(1)}, s32[16]{0:T(128)}, u32[]{:S(2)}) copy-start(s32[16]{0:T(128)} %constant.70.clone) | copy-start | bytes 196
  0.6 5.4 %copy-start.4 = (s32[16]{0:T(128)S(1)}, s32[16]{0:T(128)}, u32[]{:S(2)}) copy-start(s32[16]{0:T(128)} %constant.69.clone) | copy-start | bytes 196
  0.7 5.4 %copy-start = (f32[32,128,128]{2,1,0:T(8,128)S(1)}, f32[32,128,128]{2,1,0:T(8,128)}, u32[]{:S(2)}) copy-start(f32[32,128,128]{2,1,0:T(8,128)} %param.7) | copy-start | bytes 6291460
  3.0 29.1 %collective-permute-start = (f32[2048,128]{1,0:T(8,128)}, f32[2048,128]{1,0:T(8,128)S(1)}, u32[]{:S(2)}, u32[]{:S(2)}) collective-permute-start(f32[2048,128]{1,0:T(8,128)} %bitcast.17), channel_id=1, source_target_pairs={{0,8},{1,16},{2,24},{3,0},{4,12},{5,20},{6,28},{7,4},{8,25},{9,1},... | collective-permute-start | bytes 3145736 | tf_op jit(solution)/shard_map/ppermute | solution.py:42
  6.1 23.0 %copy-start.2 = (f32[128,128]{1,0:T(8,128)S(1)}, f32[128,128]{1,0:T(8,128)}, u32[]{:S(2)}) copy-start(f32[128,128]{1,0:T(8,128)} %d_ref.1) | copy-start | bytes 196612
  25.0 12.8 %collective-permute-start.2 = (f32[512,128]{1,0:T(8,128)S(1)}, f32[512,128]{1,0:T(8,128)S(1)}, u32[]{:S(2)}, u32[]{:S(2)}) collective-permute-start(f32[512,128]{1,0:T(8,128)S(1)} %get-tuple-element.23.refs_1_), channel_id=1, source_target_pairs={{0,8},{1,9},{2,10},{3,11},{4,12},{5,13},{6,14},{7,15},{8,0},{9,1},... | collective-permute-start | bytes 786440 | tf_op jit(solution)/shard_map/ppermute | solution.py:42
  26.1 14.5 %collective-permute-start.3 = (f32[512,128]{1,0:T(8,128)S(1)}, f32[512,128]{1,0:T(8,128)S(1)}, u32[]{:S(2)}, u32[]{:S(2)}) collective-permute-start(f32[512,128]{1,0:T(8,128)S(1)} %get-tuple-element.24.refs_2_), channel_id=1, source_target_pairs={{0,16},{1,17},{2,18},{3,19},{4,20},{5,21},{6,22},{7,23},{8,24},{9,... | collective-permute-start | bytes 786440 | tf_op jit(solution)/shard_map/ppermute | solution.py:42
  27.6 14.1 %collective-permute-start.4 = (f32[512,128]{1,0:T(8,128)S(1)}, f32[512,128]{1,0:T(8,128)S(1)}, u32[]{:S(2)}, u32[]{:S(2)}) collective-permute-start(f32[512,128]{1,0:T(8,128)S(1)} %get-tuple-element.25.refs_3_), channel_id=1, source_target_pairs={{0,24},{1,25},{2,26},{3,27},{4,28},{5,29},{6,30},{7,31},{8,16},{9,... | collective-permute-start | bytes 786440 | tf_op jit(solution)/shard_map/ppermute | solution.py:42
  32.1 2.9 %copy-start.1 = (f32[32,128,128]{2,1,0:T(8,128)S(1)}, f32[32,128,128]{2,1,0:T(8,128)}, u32[]{:S(2)}) copy-start(f32[32,128,128]{2,1,0:T(8,128)} %param.8) | copy-start | bytes 6291460
  35.0 7.5 %collective-permute-start.1 = (f32[512,128]{1,0:T(8,128)S(1)}, f32[512,128]{1,0:T(8,128)S(1)}, u32[]{:S(2)}, u32[]{:S(2)}) collective-permute-start(f32[512,128]{1,0:T(8,128)S(1)} %get-tuple-element.21), channel_id=1, source_target_pairs={{0,1},{1,0},{2,3},{3,2},{4,5},{5,4},{6,7},{7,6},{8,9},{9,8},{10,11... | collective-permute-start | bytes 786440 | tf_op jit(solution)/shard_map/ppermute | solution.py:42
  36.4 6.0 %collective-permute-start.5 = (f32[128,128]{1,0:T(8,128)S(1)}, f32[128,128]{1,0:T(8,128)S(1)}, u32[]{:S(2)}, u32[]{:S(2)}) collective-permute-start(f32[128,128]{1,0:T(8,128)S(1)} %moment.1), channel_id=1, source_target_pairs={{0,8},{1,9},{2,10},{3,11},{4,12},{5,13},{6,14},{7,15},{8,0},{9,1},... | collective-permute-start | bytes 196616 | tf_op jit(solution)/shard_map/ppermute | solution.py:42
  48.0 3.2 %collective-permute-start.7 = (f32[512,128]{1,0:T(8,128)S(1)}, f32[512,128]{1,0:T(8,128)S(1)}, u32[]{:S(2)}, u32[]{:S(2)}) collective-permute-start(f32[512,128]{1,0:T(8,128)S(1)} %get-tuple-element.36), channel_id=1, source_target_pairs={{0,1},{1,0},{2,3},{3,2},{4,5},{5,4},{6,7},{7,6},{8,9},{9,8},{10,11... | collective-permute-start | bytes 786440 | tf_op jit(solution)/shard_map/ppermute | solution.py:42
  48.0 3.1 %collective-permute-start.6 = (f32[512,128]{1,0:T(8,128)S(1)}, f32[512,128]{1,0:T(8,128)S(1)}, u32[]{:S(2)}, u32[]{:S(2)}) collective-permute-start(f32[512,128]{1,0:T(8,128)S(1)} %get-tuple-element.37), channel_id=1, source_target_pairs={{0,1},{1,0},{2,3},{3,2},{4,5},{5,4},{6,7},{7,6},{8,9},{9,8},{10,11... | collective-permute-start | bytes 786440 | tf_op jit(solution)/shard_map/ppermute | solution.py:42
  48.5 16.0 %collective-permute-start.10 = (f32[512,128]{1,0:T(8,128)S(1)}, f32[512,128]{1,0:T(8,128)S(1)}, u32[]{:S(2)}, u32[]{:S(2)}) collective-permute-start(f32[512,128]{1,0:T(8,128)S(1)} %add.99.refs_0_), channel_id=1, source_target_pairs={{0,4},{1,5},{2,6},{3,7},{4,0},{5,1},{6,2},{7,3},{8,12},{9,13},{10,... | collective-permute-start | bytes 786440 | tf_op jit(solution)/shard_map/ppermute | solution.py:42
  51.2 18.5 %collective-permute-start.12 = (f32[512,128]{1,0:T(8,128)S(1)}, f32[512,128]{1,0:T(8,128)S(1)}, u32[]{:S(2)}, u32[]{:S(2)}) collective-permute-start(f32[512,128]{1,0:T(8,128)S(1)} %get-tuple-element.34.refs_1_), channel_id=1, source_target_pairs={{0,6},{1,7},{2,0},{3,1},{4,2},{5,3},{6,4},{7,5},{8,14},{9,15},{10,... | collective-permute-start | bytes 786440 | tf_op jit(solution)/shard_map/ppermute | solution.py:42
  52.9 17.2 %collective-permute-start.11 = (f32[512,128]{1,0:T(8,128)S(1)}, f32[512,128]{1,0:T(8,128)S(1)}, u32[]{:S(2)}, u32[]{:S(2)}) collective-permute-start(f32[512,128]{1,0:T(8,128)S(1)} %get-tuple-element.35.refs_0_), channel_id=1, source_target_pairs={{0,2},{1,3},{2,4},{3,5},{4,6},{5,7},{6,0},{7,1},{8,10},{9,11},{10,... | collective-permute-start | bytes 786440 | tf_op jit(solution)/shard_map/ppermute | solution.py:42
  53.3 8.2 %collective-permute-start.26 = (f32[128,128]{1,0:T(8,128)S(1)}, f32[128,128]{1,0:T(8,128)S(1)}, u32[]{:S(2)}, u32[]{:S(2)}) collective-permute-start(f32[128,128]{1,0:T(8,128)S(1)} %add.103.refs_2_), channel_id=1, source_target_pairs={{0,16},{1,17},{2,18},{3,19},{4,20},{5,21},{6,22},{7,23},{8,24},{9,... | collective-permute-start | bytes 196616 | tf_op jit(solution)/shard_map/ppermute | solution.py:42
  61.4 15.9 %collective-permute-start.8 = (f32[512,128]{1,0:T(8,128)S(1)}, f32[512,128]{1,0:T(8,128)S(1)}, u32[]{:S(2)}, u32[]{:S(2)}) collective-permute-start(f32[512,128]{1,0:T(8,128)S(1)} %get-tuple-element.29), channel_id=1, source_target_pairs={{0,1},{1,0},{2,3},{3,2},{4,5},{5,4},{6,7},{7,6},{8,9},{9,8},{10,11... | collective-permute-start | bytes 786440 | tf_op jit(solution)/shard_map/ppermute | solution.py:42
  61.5 15.8 %collective-permute-start.9 = (f32[512,128]{1,0:T(8,128)S(1)}, f32[512,128]{1,0:T(8,128)S(1)}, u32[]{:S(2)}, u32[]{:S(2)}) collective-permute-start(f32[512,128]{1,0:T(8,128)S(1)} %add_add_fusion.refs_1_), channel_id=1, source_target_pairs={{0,0},{1,8},{2,16},{3,24},{4,4},{5,12},{6,20},{7,28},{8,1},{9,9},{... | collective-permute-start | bytes 786440 | tf_op jit(solution)/shard_map/ppermute | solution.py:42
  64.5 12.3 %collective-permute-start.27 = (f32[128,128]{1,0:T(8,128)S(1)}, f32[128,128]{1,0:T(8,128)S(1)}, u32[]{:S(2)}, u32[]{:S(2)}) collective-permute-start(f32[128,128]{1,0:T(8,128)S(1)} %add.109), channel_id=1, source_target_pairs={{0,2},{1,3},{2,0},{3,1},{4,6},{5,7},{6,4},{7,5},{8,10},{9,11},{10,... | collective-permute-start | bytes 196616 | tf_op jit(solution)/shard_map/ppermute | solution.py:42
  70.1 7.3 %collective-permute-start.13 = (f32[8,128]{1,0:T(8,128)S(1)}, f32[8,128]{1,0:T(8,128)S(1)}, u32[]{:S(2)}, u32[]{:S(2)}) collective-permute-start(f32[8,128]{1,0:T(8,128)S(1)} %slice_add_fusion.2), channel_id=1, source_target_pairs={{0,1},{1,0},{2,3},{3,2},{4,5},{5,4},{6,7},{7,6},{8,9},{9,8},{10,11... | collective-permute-start | bytes 12296 | tf_op jit(solution)/shard_map/ppermute | solution.py:42
  76.8 5.6 %collective-permute-start.28 = (f32[128,128]{1,0:T(8,128)S(1)}, f32[128,128]{1,0:T(8,128)S(1)}, u32[]{:S(2)}, u32[]{:S(2)}) collective-permute-start(f32[128,128]{1,0:T(8,128)S(1)} %add.110), channel_id=1, source_target_pairs={{0,4},{1,5},{2,6},{3,7},{4,0},{5,1},{6,2},{7,3},{8,12},{9,13},{10,... | collective-permute-start | bytes 196616 | tf_op jit(solution)/shard_map/ppermute | solution.py:42
  78.3 6.5 %collective-permute-start.23 = (f32[256,128]{1,0:T(8,128)S(1)}, f32[256,128]{1,0:T(8,128)S(1)}, u32[]{:S(2)}, u32[]{:S(2)}) collective-permute-start(f32[256,128]{1,0:T(8,128)S(1)} %get-tuple-element.38.refs_3_), channel_id=1, source_target_pairs={{0,1},{1,0},{2,3},{3,2},{4,5},{5,4},{6,7},{7,6},{8,9},{9,8},{10,11... | collective-permute-start | bytes 393224 | tf_op jit(solution)/shard_map/ppermute | solution.py:42
  78.4 9.2 %collective-permute-start.19 = (f32[256,128]{1,0:T(8,128)S(1)}, f32[256,128]{1,0:T(8,128)S(1)}, u32[]{:S(2)}, u32[]{:S(2)}) collective-permute-start(f32[256,128]{1,0:T(8,128)S(1)} %get-tuple-element.38.refs_3_), channel_id=1, source_target_pairs={{0,2},{1,3},{2,4},{3,5},{4,6},{5,7},{6,0},{7,1},{8,10},{9,11},{10,... | collective-permute-start | bytes 393224 | tf_op jit(solution)/shard_map/ppermute | solution.py:42
  82.4 1.3 %collective-permute-start.29 = (f32[128,128]{1,0:T(8,128)S(1)}, f32[128,128]{1,0:T(8,128)S(1)}, u32[]{:S(2)}, u32[]{:S(2)}) collective-permute-start(f32[128,128]{1,0:T(8,128)S(1)} %add.111), channel_id=1, source_target_pairs={{0,1},{1,0},{2,3},{3,2},{4,5},{5,4},{6,7},{7,6},{8,9},{9,8},{10,11... | collective-permute-start | bytes 196616 | tf_op jit(solution)/shard_map/ppermute | solution.py:42
  82.5 7.8 %collective-permute-start.16 = (f32[256,128]{1,0:T(8,128)S(1)}, f32[256,128]{1,0:T(8,128)S(1)}, u32[]{:S(2)}, u32[]{:S(2)}) collective-permute-start(f32[256,128]{1,0:T(8,128)S(1)} %get-tuple-element.38.refs_3_), channel_id=1, source_target_pairs={{0,6},{1,7},{2,0},{3,1},{4,2},{5,3},{6,4},{7,5},{8,14},{9,15},{10,... | collective-permute-start | bytes 393224 | tf_op jit(solution)/shard_map/ppermute | solution.py:42
  83.6 6.8 %collective-permute-start.20 = (f32[256,128]{1,0:T(8,128)S(1)}, f32[256,128]{1,0:T(8,128)S(1)}, u32[]{:S(2)}, u32[]{:S(2)}) collective-permute-start(f32[256,128]{1,0:T(8,128)S(1)} %get-tuple-element.39.refs_0_), channel_id=1, source_target_pairs={{0,1},{1,0},{2,3},{3,2},{4,5},{5,4},{6,7},{7,6},{8,9},{9,8},{10,11... | collective-permute-start | bytes 393224 | tf_op jit(solution)/shard_map/ppermute | solution.py:42
  83.8 9.4 %collective-permute-start.14 = (f32[256,128]{1,0:T(8,128)S(1)}, f32[256,128]{1,0:T(8,128)S(1)}, u32[]{:S(2)}, u32[]{:S(2)}) collective-permute-start(f32[256,128]{1,0:T(8,128)S(1)} %get-tuple-element.39.refs_0_), channel_id=1, source_target_pairs={{0,2},{1,3},{2,4},{3,5},{4,6},{5,7},{6,0},{7,1},{8,10},{9,11},{10,... | collective-permute-start | bytes 393224 | tf_op jit(solution)/shard_map/ppermute | solution.py:42
  84.8 10.7 %collective-permute-start.18 = (f32[256,128]{1,0:T(8,128)S(1)}, f32[256,128]{1,0:T(8,128)S(1)}, u32[]{:S(2)}, u32[]{:S(2)}) collective-permute-start(f32[256,128]{1,0:T(8,128)S(1)} %get-tuple-element.39.refs_0_), channel_id=1, source_target_pairs={{0,6},{1,7},{2,0},{3,1},{4,2},{5,3},{6,4},{7,5},{8,14},{9,15},{10,... | collective-permute-start | bytes 393224 | tf_op jit(solution)/shard_map/ppermute | solution.py:42
  87.6 8.4 %collective-permute-start.25 = (f32[256,128]{1,0:T(8,128)S(1)}, f32[256,128]{1,0:T(8,128)S(1)}, u32[]{:S(2)}, u32[]{:S(2)}) collective-permute-start(f32[256,128]{1,0:T(8,128)S(1)} %collective-permute-done.19.refs_5_), channel_id=1, source_target_pairs={{0,1},{1,0},{2,3},{3,2},{4,5},{5,4},{6,7},{7,6},{8,9},{9,8},{10,11... | collective-permute-start | bytes 393224 | tf_op jit(solution)/shard_map/ppermute | solution.py:42
  90.4 6.6 %collective-permute-start.24 = (f32[256,128]{1,0:T(8,128)S(1)}, f32[256,128]{1,0:T(8,128)S(1)}, u32[]{:S(2)}, u32[]{:S(2)}) collective-permute-start(f32[256,128]{1,0:T(8,128)S(1)} %collective-permute-done.16.refs_4_), channel_id=1, source_target_pairs={{0,1},{1,0},{2,3},{3,2},{4,5},{5,4},{6,7},{7,6},{8,9},{9,8},{10,11... | collective-permute-start | bytes 393224 | tf_op jit(solution)/shard_map/ppermute | solution.py:42
  90.4 9.2 %collective-permute-start.17 = (f32[256,128]{1,0:T(8,128)S(1)}, f32[256,128]{1,0:T(8,128)S(1)}, u32[]{:S(2)}, u32[]{:S(2)}) collective-permute-start(f32[256,128]{1,0:T(8,128)S(1)} %collective-permute-done.16.refs_4_), channel_id=1, source_target_pairs={{0,6},{1,7},{2,0},{3,1},{4,2},{5,3},{6,4},{7,5},{8,14},{9,15},{10,... | collective-permute-start | bytes 393224 | tf_op jit(solution)/shard_map/ppermute | solution.py:42
  93.1 4.2 %collective-permute-start.22 = (f32[256,128]{1,0:T(8,128)S(1)}, f32[256,128]{1,0:T(8,128)S(1)}, u32[]{:S(2)}, u32[]{:S(2)}) collective-permute-start(f32[256,128]{1,0:T(8,128)S(1)} %collective-permute-done.14.refs_2_), channel_id=1, source_target_pairs={{0,1},{1,0},{2,3},{3,2},{4,5},{5,4},{6,7},{7,6},{8,9},{9,8},{10,11... | collective-permute-start | bytes 393224 | tf_op jit(solution)/shard_map/ppermute | solution.py:42
  95.5 8.6 %collective-permute-start.15 = (f32[256,128]{1,0:T(8,128)S(1)}, f32[256,128]{1,0:T(8,128)S(1)}, u32[]{:S(2)}, u32[]{:S(2)}) collective-permute-start(f32[256,128]{1,0:T(8,128)S(1)} %collective-permute-done.14.refs_2_), channel_id=1, source_target_pairs={{0,2},{1,3},{2,4},{3,5},{4,6},{5,7},{6,0},{7,1},{8,10},{9,11},{10,... | collective-permute-start | bytes 393224 | tf_op jit(solution)/shard_map/ppermute | solution.py:42
  96.0 1.3 %collective-permute-start.21 = (f32[256,128]{1,0:T(8,128)S(1)}, f32[256,128]{1,0:T(8,128)S(1)}, u32[]{:S(2)}, u32[]{:S(2)}) collective-permute-start(f32[256,128]{1,0:T(8,128)S(1)} %collective-permute-done.18.refs_1_), channel_id=1, source_target_pairs={{0,1},{1,0},{2,3},{3,2},{4,5},{5,4},{6,7},{7,6},{8,9},{9,8},{10,11... | collective-permute-start | bytes 393224 | tf_op jit(solution)/shard_map/ppermute | solution.py:42
  104.1 1.3 %collective-permute-start.30 = (f32[256,128]{1,0:T(8,128)S(1)}, f32[256,128]{1,0:T(8,128)S(1)}, u32[]{:S(2)}, u32[]{:S(2)}) collective-permute-start(f32[256,128]{1,0:T(8,128)S(1)} %collective-permute-done.15.refs_1_), channel_id=1, source_target_pairs={{0,1},{1,0},{2,3},{3,2},{4,5},{5,4},{6,7},{7,6},{8,9},{9,8},{10,11... | collective-permute-start | bytes 393224 | tf_op jit(solution)/shard_map/ppermute | solution.py:42
  104.1 1.5 %collective-permute-start.31 = (f32[256,128]{1,0:T(8,128)S(1)}, f32[256,128]{1,0:T(8,128)S(1)}, u32[]{:S(2)}, u32[]{:S(2)}) collective-permute-start(f32[256,128]{1,0:T(8,128)S(1)} %collective-permute-done.17.refs_2_), channel_id=1, source_target_pairs={{0,1},{1,0},{2,3},{3,2},{4,5},{5,4},{6,7},{7,6},{8,9},{9,8},{10,11... | collective-permute-start | bytes 393224 | tf_op jit(solution)/shard_map/ppermute | solution.py:42
